TPU v7x, 128 devices: a whole 4x4x4 slice. The times are simulated.
128 devices in a mesh: sector: 4 (over y_hi, core), grid: 32 (over x, z, y_lo).
Axes of the slice: x: 4, y: 4 (y_hi: 2, y_lo: 2; y = y_hi * 2 + y_lo), z: 4, core: 2. Of those that a mesh axis runs over, the one named last changes fastest.
Arguments:
- coeffs: bfloat16 [8, 3072, 1024], P('sector'), may hold values from -0.109375 to 0.109375
- basis_values: bfloat16 [32768, 3072], P('grid'), may hold values from -6 to 6
- weights: float32 [32768], P('grid'), may hold values from 0.0016572815 to 0.016572814
- next_coeffs: bfloat16 [3072, 1024], replicated, may hold values from -0.109375 to 0.109375
Outputs:
- intersection: float32 [8, 1024, 1024], P('sector', 'grid')
All inputs are finite; a program needn't handle non-finite values.
Results may differ from a plain program's by a relative error of at most 0.0018.
Values may be sent and summed in bfloat16 or wider, within the bound.
No kernel may reach another device: no remote copies, remote signals or barrier semaphores. Data moves between devices by JAX's collectives and lax.ppermute only.
A program may use at most 128 MiB of HBM per device.

v0:
```python
import jax
import jax.numpy as jnp
from jax import lax
from jax.sharding import PartitionSpec as P


def shifted(value, axis, by):
    peers = lax.axis_size(axis)
    pairs = [(i, i + by) for i in range(peers) if 0 <= i + by < peers]
    return lax.ppermute(value, axis, pairs)


def per_device(coeffs, basis_values, weights, next_coeffs):
    held = coeffs.shape[0]
    width = coeffs.shape[2]

    def transform(coefficient):
        return jnp.dot(basis_values, coefficient, preferred_element_type=jnp.float32).astype(
            jnp.bfloat16
        )

    def weighted_of(field):
        return (weights[:, None] * field.astype(jnp.float32)).astype(jnp.bfloat16)

    is_last = lax.axis_index("sector") == lax.axis_size("sector") - 1
    values = [transform(coeffs[k]) for k in range(held)]
    arrived = shifted(values[0], "sector", -1)
    following = lax.cond(is_last, lambda: transform(next_coeffs), lambda: arrived)
    seconds = [weighted_of(values[1])] + [weighted_of(following)]
    share_rows = width // lax.axis_size("grid")
    partials = jnp.concatenate(
        [
            jnp.einsum("gi,gj->ij", values[k], seconds[k], preferred_element_type=jnp.float32)
            for k in range(held)
        ],
        axis=1,
    )
    summed = lax.psum(partials, "grid")
    own_rows = lax.dynamic_slice_in_dim(summed, lax.axis_index("grid") * share_rows, share_rows, 0)
    return own_rows.reshape(share_rows, held, width).transpose(1, 0, 2)


def solution(mesh):
    return jax.shard_map(
        per_device,
        mesh=mesh,
        in_specs=(P("sector", None, None), P("grid", None), P("grid"), P()),
        out_specs=P("sector", "grid", None),
        check_vma=False,
    )
```

profile of v0, /device:TPU:30, one launch (start us, length us, event | category | flops | bytes accessed | tf_op | source)
XLA Modules:
  0.0 443.7 jit_solution(6361993748574973045)
XLA Ops:
  6.5 0.0 all-reduce.2.cloned.1.call-start
  6.5 11.6 %fusion.10 = bf16[1024,1024]{1,0:T(8,128)(2,1)} fusion(bf16[1024,3072]{1,0:T(8,128)(2,1)} %param.7, bf16[2,3072,1024]{2,1,0:T(8,128)(2,1)} %param.6), kind=kOutput, calls=%fused_computation.14 | convolution fusion | flops 6443499520 | bytes 14680064 | tf_op jit(solution)/shard_map/dot_general | solution.py:18
  18.2 2.6 collective-permute-start
  20.7 0.0 copy-start.1
  20.8 10.6 %fusion.13 = bf16[1024,1024]{1,0:T(8,128)(2,1)S(1)} fusion(bf16[1024,3072]{1,0:T(8,128)(2,1)} %param.7, bf16[2,3072,1024]{2,1,0:T(8,128)(2,1)} %param.6), kind=kOutput, calls=%fused_computation.15 | convolution fusion | flops 6443499520 | bytes 14680064 | tf_op jit(solution)/shard_map/dot_general | solution.py:18
  31.4 0.0 copy-done.1
  31.4 0.0 copy-start.2
  31.4 6.8 %fusion.6 = f32[1024,1024]{0,1:T(8,128)} fusion(bf16[1024,1024]{1,0:T(8,128)(2,1)} %fusion.10, bf16[1024,1024]{1,0:T(8,128)(2,1)S(1)} %fusion.13, f32[1024]{0:T(1024)S(1)} %copy-done.1), kind=kOutput, calls=%fused_computation.10 | convolution fusion | flops 2150629376 | bytes 8392704 | tf_op jit(solution)/shard_map/gi,gj->ij/dot_general | solution.py:33
  38.2 0.0 copy-done.2
  38.2 6.4 %collective-permute-done = bf16[1024,1024]{1,0:T(8,128)(2,1)S(1)} collective-permute-done((bf16[1024,1024]{1,0:T(8,128)(2,1)}, bf16[1024,1024]{1,0:T(8,128)(2,1)S(1)}, u32[]{:S(2)}, u32[]{:S(2)}) %collective-permute-start) | collective-permute-done | bytes 2097184 | tf_op jit(solution)/shard_map/ppermute | solution.py:10
  44.6 0.0 copy-start
  44.6 4.2 fusion.7
  48.8 0.0 copy-done
  48.8 4.1 pad_maximum_fusion
  52.9 0.0 all-reduce.2.cloned.1.call-update
  52.9 381.3 %all-reduce.2.cloned.1.call-done = f32[1024,2048]{0,1:T(8,128)} async-done(((f32[1024,2048]{0,1:T(8,128)}), f32[1024,2048]{0,1:T(8,128)}) %all-reduce.2.cloned.1.call-update) | async-done | bytes 8388624 | tf_op jit(solution)/shard_map/psum | solution.py:38
  434.2 1.6 constant_dynamic-slice_fusion
  435.7 0.3 copy.8
  436.1 0.8 copy.7
  (1 shorter events, 0.0 us)
Async XLA Ops:
  6.5 427.6 %all-reduce.2.cloned.1.call-start = ((), (), s32[]{:S(2)}) async-start(), calls=%async_computation | async-start | bytes 16777216 | tf_op jit(solution)/shard_map/psum | solution.py:38
  18.2 26.4 %collective-permute-start = (bf16[1024,1024]{1,0:T(8,128)(2,1)}, bf16[1024,1024]{1,0:T(8,128)(2,1)S(1)}, u32[]{:S(2)}, u32[]{:S(2)}) collective-permute-start(bf16[1024,1024]{1,0:T(8,128)(2,1)} %fusion.10), channel_id=1, source_target_pairs={{32,0},{64,32},{96,64},{33,1},{65,33},{97,65},{34,2},{66,34},{98,6... | collective-permute-start | bytes 6291464 | tf_op jit(solution)/shard_map/ppermute | solution.py:10
  20.7 10.6 %copy-start.1 = (f32[1024]{0:T(1024)S(1)}, f32[1024]{0:T(1024)}, u32[]{:S(2)}) copy-start(f32[1024]{0:T(1024)} %param.8) | copy-start | bytes 12292
  31.4 6.8 %copy-start.2 = (bf16[1024,1024]{1,0:T(8,128)(2,1)}, bf16[1024,1024]{1,0:T(8,128)(2,1)S(1)}, u32[]{:S(2)}) copy-start(bf16[1024,1024]{1,0:T(8,128)(2,1)S(1)} %fusion.13) | copy-start | bytes 6291460
  44.6 4.2 copy-start
Sparse Core Ops, SparseCore 0:
  53.0 381.1 all-reduce.1
where the time goes:
time: 447 us; the launch traced here: 444 us
  waiting for transfers between devices  388 us (87%)
  matrix products  33.2 us (7%)
  between operations  13.5 us (3%)
    psum x1, waiting for transfers between devices, per_device(): summed = lax.psum(partials, 'grid')  381 us
    dot_general x2, matrix products, transform(): jnp.dot(basis_values, coefficient, preferred_element_type=jnp.float32)  22.2 us
    dot_general x2, matrix products, per_device(): jnp.einsum('gi,gj->ij', values[k], seconds[k], preferred_element_type=jnp...  11 us
  transfers between devices with their start and end apart: 2, of which 2 were waited for; matrix products, arithmetic and copies ran while one was open for 4% of the time, Pallas kernels for 0%

commit v1 on v0

v1 whole, which is shorter than its diff:
```python
import functools

import jax
import jax.numpy as jnp
from jax import lax
from jax.experimental import pallas as pl
from jax.experimental.pallas import tpu as pltpu
from jax.sharding import PartitionSpec as P

BF16, F32 = jnp.bfloat16, jnp.float32
ROWS = 256
SUB = 64
VMEM = pl.BlockSpec(memory_space=pltpu.VMEM)
ANY = pl.BlockSpec(memory_space=pl.ANY)
SMEM = pl.BlockSpec(memory_space=pltpu.SMEM)
PARAMS = pltpu.CompilerParams(vmem_limit_bytes=56 * 1024 * 1024)


def copies(b_hbm, c_hbm, b, c, sems):
    rows, cols = b.shape[0] // ROWS, c.shape[1] // ROWS
    of_b = [
        pltpu.make_async_copy(b_hbm.at[pl.ds(m * ROWS, ROWS)], b.at[pl.ds(m * ROWS, ROWS)], sems.at[m])
        for m in range(rows)
    ]
    of_c = [
        pltpu.make_async_copy(
            c_hbm.at[:, pl.ds(n * ROWS, ROWS)], c.at[:, pl.ds(n * ROWS, ROWS)], sems.at[rows + n]
        )
        for n in range(cols)
    ]
    return of_b, of_c


def start(of_b, of_c):
    for copy in of_b[:1] + of_c + of_b[1:]:
        copy.start()


def transform(of_b, of_c, b, c, put):
    of_b[0].wait()
    for n, copy in enumerate(of_c):
        copy.wait()
        at = slice(n * ROWS, (n + 1) * ROWS)
        put(slice(0, ROWS), at, jnp.dot(b[:ROWS, :], c[:, at], preferred_element_type=F32).astype(BF16))
    for m in range(1, len(of_b)):
        of_b[m].wait()
        at = slice(m * ROWS, (m + 1) * ROWS)
        put(at, slice(0, c.shape[1]), jnp.dot(b[at, :], c[...], preferred_element_type=F32).astype(BF16))


def spread(w, wide):
    for k in range(w.shape[0]):
        wide[k * 128 : (k + 1) * 128, :] = jnp.broadcast_to(w[k : k + 1, :], (128, 128)).T


def weighted(wide, rows, field):
    factor = jnp.concatenate([wide[rows, :]] * (field.shape[1] // 128), axis=1)
    return (factor * field.astype(F32)).astype(BF16)


def intersect(place, v, w, product, outs):
    own, odd = place[0], place[1]
    width = v.shape[1]
    for n in range(width // 512):
        at = slice(n * 512, (n + 1) * 512)
        for i in range(width // 512):
            rows = slice(i * 512, (i + 1) * 512)
            product[rows, at] = lax.dot_general(
                v[:, rows], w[:, at], (((0,), (0,)), ((), ())), preferred_element_type=F32
            )
    for k, out in enumerate(outs):
        first = lax.rem(own + k, 4)
        for second in range(4):
            block = jnp.where(odd == 1, second * 4 + first, first * 4 + second)
            rows = pl.ds(pl.multiple_of(block * SUB, SUB), SUB)
            out[second * SUB : (second + 1) * SUB, :] = product[rows, :].astype(BF16)


def first_kernel(b_hbm, c_hbm, v_out, b, c, sems):
    of_b, of_c = copies(b_hbm, c_hbm.at[0], b, c, sems)
    start(of_b, of_c)

    def put(rows, cols, values):
        v_out[rows, cols] = values

    transform(of_b, of_c, b, c, put)


def second_kernel(place, b_hbm, c_hbm, v0, weights, v_out, *rest):
    outs, (b, c, wide, w, product, sems) = rest[:4], rest[4:]
    of_b, of_c = copies(b_hbm, c_hbm.at[1], b, c, sems)
    start(of_b, of_c)
    spread(weights, wide)

    def put(rows, cols, values):
        v_out[rows, cols] = values
        w[rows, cols] = weighted(wide, rows, values)

    transform(of_b, of_c, b, c, put)
    intersect(place, v0, w, product, outs)


def third_kernel(place, b_hbm, next_hbm, v1, arrived, weights, *rest):
    outs, (b, c, wide, w, product, sems) = rest[:4], rest[4:]
    last = place[2] == 1
    of_b, of_c = copies(b_hbm, next_hbm, b, c, sems)

    @pl.when(last)
    def _():
        start(of_b, of_c)

    spread(weights, wide)

    @pl.when(last)
    def _():
        def put(rows, cols, values):
            w[rows, cols] = weighted(wide, rows, values)

        transform(of_b, of_c, b, c, put)

    @pl.when(jnp.logical_not(last))
    def _():
        for m in range(arrived.shape[0] // ROWS):
            rows = slice(m * ROWS, (m + 1) * ROWS)
            w[rows, :] = weighted(wide, rows, arrived[rows, :])

    intersect(place, v1, w, product, outs)


def add_kernel(place, *refs):
    parts, own, outs = refs[:4], refs[4], refs[5:]
    for k in range(4):
        rows = pl.ds(pl.multiple_of(lax.rem(place[3] + k, 4) * SUB, SUB), SUB)
        total = sum(part[rows, :].astype(F32) for part in parts)
        if k == 0:
            own[...] = total
        else:
            outs[k - 1][...] = total.astype(BF16)


def last_kernel(place, own, a, b, c, kept, out):
    half = SUB // 2
    for k, to in enumerate((kept, out)):
        rows = pl.ds(pl.multiple_of(lax.rem(place[4] + k, 2) * half, half), half)
        to[...] = own[rows, :] + a[rows, :].astype(F32) + b[rows, :].astype(F32) + c[rows, :].astype(F32)


def transform_scratch(grid_points, basis, width):
    return [pltpu.VMEM((grid_points, basis), BF16), pltpu.VMEM((basis, width), BF16)]


def product_scratch(grid_points, width):
    return [
        pltpu.VMEM((grid_points, 128), F32),
        pltpu.VMEM((grid_points, width), BF16),
        pltpu.VMEM((width, width), F32),
    ]


def pairs_of(move):
    found = []
    for q in range(4):
        for r in range(32):
            t = move(q, r // 8, (r // 2) % 4, r % 2)
            if t is not None:
                found.append((q * 32 + r, t[0] * 32 + (t[1] % 4) * 8 + (t[2] % 4) * 2 + t[3] % 2))
    return found


def along(first, k):
    def move(q, x, z, y):
        return (q, x + k, z, y) if (q % 2 == 0) == first else (q, x, z + k, y)

    return move


def send(value, move):
    return lax.ppermute(value, ("sector", "grid"), pairs_of(move))


def per_device(coeffs, basis_values, weights, next_coeffs):
    grid_points, basis = basis_values.shape
    width = coeffs.shape[2]
    q, r = lax.axis_index("sector"), lax.axis_index("grid")
    x, z, y = r // 8, (r // 2) % 4, r % 2
    odd = q % 2
    place = jnp.stack(
        [jnp.where(odd == 1, z, x), odd, (q == 3).astype(jnp.int32), jnp.where(odd == 1, x, z), y]
    ).astype(jnp.int32)
    rows_of = weights.reshape(grid_points // 128, 128)
    sems = pltpu.SemaphoreType.DMA((grid_points // ROWS + width // ROWS,))
    field = jax.ShapeDtypeStruct((grid_points, width), BF16)
    part = jax.ShapeDtypeStruct((width // 4, width), BF16)

    def cost(transforms, products):
        return pl.CostEstimate(
            flops=2 * grid_points * width * (transforms * basis + products * width),
            bytes_accessed=2 * (transforms * basis * (grid_points + width) + 3 * width * width),
            transcendentals=0,
        )

    v0 = pl.pallas_call(
        first_kernel,
        out_shape=field,
        in_specs=[ANY, ANY],
        out_specs=VMEM,
        scratch_shapes=transform_scratch(grid_points, basis, width) + [sems],
        compiler_params=PARAMS,
        cost_estimate=cost(1, 0),
        name="first_transform",
    )(basis_values, coeffs)
    arrived = send(v0, lambda q, x, z, y: (q - 1, x, z, y) if q else None)
    v1, *parts0 = pl.pallas_call(
        second_kernel,
        out_shape=[field] + [part] * 4,
        in_specs=[SMEM, ANY, ANY, VMEM, VMEM],
        out_specs=[VMEM] * 5,
        scratch_shapes=transform_scratch(grid_points, basis, width) + product_scratch(grid_points, width) + [sems],
        compiler_params=PARAMS,
        cost_estimate=cost(1, 1),
        name="second_transform",
    )(place, basis_values, coeffs, v0, rows_of)
    parts1 = pl.pallas_call(
        third_kernel,
        out_shape=[part] * 4,
        in_specs=[SMEM, ANY, ANY, VMEM, VMEM, VMEM],
        out_specs=[VMEM] * 4,
        scratch_shapes=transform_scratch(grid_points, basis, width) + product_scratch(grid_points, width) + [sems],
        compiler_params=PARAMS,
        cost_estimate=cost(0, 1),
        name="second_intersection",
    )(place, basis_values, next_coeffs, v1, arrived, rows_of)

    def reduced(parts):
        got = [send(parts[k], along(True, k)) for k in (1, 2, 3)]
        own, *outs = pl.pallas_call(
            add_kernel,
            out_shape=[jax.ShapeDtypeStruct((SUB, width), F32)] + [jax.ShapeDtypeStruct((SUB, width), BF16)] * 3,
            in_specs=[SMEM] + [VMEM] * 4,
            out_specs=[VMEM] * 4,
            name="first_sum",
        )(place, parts[0], *got)
        got = [send(outs[k - 1], along(False, k)) for k in (1, 2, 3)]
        kept, out = pl.pallas_call(
            last_kernel,
            out_shape=[jax.ShapeDtypeStruct((SUB // 2, width), F32)] * 2,
            in_specs=[SMEM] + [VMEM] * 4,
            out_specs=[VMEM] * 2,
            name="second_sum",
        )(place, own, *got)
        return kept + send(out, lambda q, x, z, y: (q, x, z, y + 1))

    return jnp.stack([reduced(parts0), reduced(parts1)])


def solution(mesh):
    return jax.shard_map(
        per_device,
        mesh=mesh,
        in_specs=(P("sector", None, None), P("grid", None), P("grid"), P()),
        out_specs=P("sector", "grid", None),
        check_vma=False,
    )
```

time: 447 us -> 96.6 us (0.22)
  the two profiles are of different devices: /device:TPU:30 before, /device:TPU:17 now
where the time goes in v1:
time: 96.6 us; the launch traced here: 96.3 us
  Pallas kernels  55.5 us (57%)
  starting transfers between devices  23.9 us (25%)
  waiting for transfers between devices  9.14 us (9%)
  local copies, waits for them, and re-layouts  5.07 us (5%)
  other arithmetic  2.56 us (3%)
    ppermute x15, starting transfers between devices, send(): return lax.ppermute(value, ('sector', 'grid'), pairs_of(move))  23.9 us
    pallas_call x1, Pallas kernels, per_device(): pl.pallas_call(third_kernel, out_shape=[part] * 4, in_specs=[SMEM, ANY, A...  17.2 us
    pallas_call x1, Pallas kernels, per_device(): pl.pallas_call(second_kernel, out_shape=[field] + [part] * 4, in_specs=[S...  17.1 us
    pallas_call x1, Pallas kernels, per_device(): pl.pallas_call(first_kernel, out_shape=field, in_specs=[ANY, ANY], out_sp...  12.5 us
    ppermute x15, waiting for transfers between devices, send(): return lax.ppermute(value, ('sector', 'grid'), pairs_of(move))  9.14 us
    pallas_call x2, Pallas kernels, reduced(): pl.pallas_call(add_kernel, out_shape=[jax.ShapeDtypeStruct((SUB, width),...  5 us
    unnamed x24, local copies, waits for them, and re-layouts  4.4 us
    pallas_call x2, Pallas kernels, reduced(): pl.pallas_call(last_kernel, out_shape=[jax.ShapeDtypeStruct((SUB // 2, wi...  3.76 us
  transfers between devices with their start and end apart: 15, of which 3 were waited for; matrix products, arithmetic and copies ran while one was open for 2% of the time, Pallas kernels for 45%

profile of v1, /device:TPU:17, one launch (start us, length us, event | category | flops | bytes accessed | tf_op | source)
XLA Modules:
  0.0 96.3 jit_solution(12394689663112291531)
XLA Ops:
  0.0 12.5 %first_transform.1.v0 = bf16[1024,1024]{1,0:T(8,128)(2,1)} custom-call(bf16[1024,3072]{1,0:T(8,128)(2,1)} %b_hbm.5, bf16[2,3072,1024]{2,1,0:T(8,128)(2,1)} %c_hbm.3), custom_call_target="tpu_custom_call" | custom-call | flops 6442450944 | bytes 18874368 | tf_op jit(solution)/shard_map/first_transform/pallas_call | solution.py:202
  12.5 2.9 %collective-permute-start.7 = (bf16[1024,1024]{1,0:T(8,128)(2,1)}, bf16[1024,1024]{1,0:T(8,128)(2,1)S(1)}, u32[]{:S(2)}, u32[]{:S(2)}) collective-permute-start(bf16[1024,1024]{1,0:T(8,128)(2,1)} %first_transform.1.v0), channel_id=1, source_target_pairs={{32,0},{33,1},{34,2},{35,3},{36,4},{37,5},{38,6},{39,7},{40,8},{41... | collective-permute-start | bytes 6291464 | tf_op jit(solution)/shard_map/ppermute | solution.py:178
  15.5 0.7 stack.36.place
  16.2 17.1 %second_transform.1 = (bf16[1024,1024]{1,0:T(8,128)(2,1)}, bf16[256,1024]{1,0:T(8,128)(2,1)}, bf16[256,1024]{1,0:T(8,128)(2,1)}, bf16[256,1024]{1,0:T(8,128)(2,1)}, bf16[256,1024]{1,0:T(8,128)(2,1)}) custom-call(s32[5]{0:T(128)} %stack.36.place, bf16[1024,3072]{1,0:T(8,128)(2,1)} %b_hbm.5, bf16[2,3072,1024]{2,1,0:T(8,128)(2,1)} %c_hbm.3, ...), custom_call_target="tpu_custom_call" | custom-call | flops 8589934592 | bytes 18874368 | tf_op jit(solution)/shard_map/second_transform/pallas_call | solution.py:213
  33.2 1.7 %collective-permute-start = (bf16[256,1024]{1,0:T(8,128)(2,1)}, bf16[256,1024]{1,0:T(8,128)(2,1)S(1)}, u32[]{:S(2)}, u32[]{:S(2)}) collective-permute-start(bf16[256,1024]{1,0:T(8,128)(2,1)} %get-tuple-element.27), channel_id=1, source_target_pairs={{0,8},{1,9},{2,10},{3,11},{4,12},{5,13},{6,14},{7,15},{8,16},{9,17... | collective-permute-start | bytes 1572872 | tf_op jit(solution)/shard_map/ppermute | solution.py:178
  34.9 3.3 %collective-permute-start.1 = (bf16[256,1024]{1,0:T(8,128)(2,1)}, bf16[256,1024]{1,0:T(8,128)(2,1)S(1)}, u32[]{:S(2)}, u32[]{:S(2)}) collective-permute-start(bf16[256,1024]{1,0:T(8,128)(2,1)} %get-tuple-element.28), channel_id=1, source_target_pairs={{0,16},{1,17},{2,18},{3,19},{4,20},{5,21},{6,22},{7,23},{8,24},{9,... | collective-permute-start | bytes 1572872 | tf_op jit(solution)/shard_map/ppermute | solution.py:178
  38.3 0.7 collective-permute-start.2
  39.0 0.0 collective-permute-done.7.arrived
  39.0 1.4 %copy-done = bf16[1024,1024]{1,0:T(8,128)(2,1)} copy-done((bf16[1024,1024]{1,0:T(8,128)(2,1)}, bf16[1024,1024]{1,0:T(8,128)(2,1)S(1)}, u32[]{:S(2)}) %copy-start) | copy-done | bytes 2097176
  40.3 17.2 %second_intersection.1 = (bf16[256,1024]{1,0:T(8,128)(2,1)}, bf16[256,1024]{1,0:T(8,128)(2,1)}, bf16[256,1024]{1,0:T(8,128)(2,1)}, bf16[256,1024]{1,0:T(8,128)(2,1)}) custom-call(s32[5]{0:T(128)} %stack.36.place, bf16[1024,3072]{1,0:T(8,128)(2,1)} %b_hbm.5, bf16[3072,1024]{1,0:T(8,128)(2,1)} %next_hbm.1, bf16[1024,1024]{1,0:T(8,128)(2,1)} %get-tuple-element.36.v1, ...), custom_call_target="tpu_custom_call" | custom-call | flops 2147483648 | bytes 6291456 | tf_op jit(solution)/shard_map/second_intersection/pallas_call | solution.py:223
  57.5 0.1 collective-permute-start.10
  57.6 1.5 %collective-permute-start.8 = (bf16[256,1024]{1,0:T(8,128)(2,1)}, bf16[256,1024]{1,0:T(8,128)(2,1)S(1)}, u32[]{:S(2)}, u32[]{:S(2)}) collective-permute-start(bf16[256,1024]{1,0:T(8,128)(2,1)} %get-tuple-element.38), channel_id=1, source_target_pairs={{0,8},{1,9},{2,10},{3,11},{4,12},{5,13},{6,14},{7,15},{8,16},{9,17... | collective-permute-start | bytes 1572872 | tf_op jit(solution)/shard_map/ppermute | solution.py:178
  59.1 0.0 collective-permute-done.refs_1_
  59.1 1.1 %collective-permute-start.9 = (bf16[256,1024]{1,0:T(8,128)(2,1)}, bf16[256,1024]{1,0:T(8,128)(2,1)S(1)}, u32[]{:S(2)}, u32[]{:S(2)}) collective-permute-start(bf16[256,1024]{1,0:T(8,128)(2,1)} %get-tuple-element.39), channel_id=1, source_target_pairs={{0,16},{1,17},{2,18},{3,19},{4,20},{5,21},{6,22},{7,23},{8,24},{9,... | collective-permute-start | bytes 1572872 | tf_op jit(solution)/shard_map/ppermute | solution.py:178
  60.2 0.0 collective-permute-done.1.refs_2_
  60.2 0.0 collective-permute-done.2.refs_3_
  60.2 0.8 copy-done.5
  61.0 2.5 %first_sum.2 = (f32[64,1024]{1,0:T(8,128)}, bf16[64,1024]{1,0:T(8,128)(2,1)}, bf16[64,1024]{1,0:T(8,128)(2,1)}, bf16[64,1024]{1,0:T(8,128)(2,1)}) custom-call(s32[5]{0:T(128)} %stack.36.place, bf16[256,1024]{1,0:T(8,128)(2,1)} %get-tuple-element.26.refs_0_, bf16[256,1024]{1,0:T(8,128)(2,1)} %copy-done.4, bf16[256,1024]{1,0:T(8,128)(2,1)} %copy-done.5, ...), custom_call_target="tpu_custom_call" | custom-call | tf_op jit(solution)/shard_map/first_sum/pallas_call | solution.py:236
  63.6 1.2 %collective-permute-start.3 = (bf16[64,1024]{1,0:T(8,128)(2,1)}, bf16[64,1024]{1,0:T(8,128)(2,1)S(1)}, u32[]{:S(2)}, u32[]{:S(2)}) collective-permute-start(bf16[64,1024]{1,0:T(8,128)(2,1)} %get-tuple-element.31), channel_id=1, source_target_pairs={{0,2},{1,3},{2,4},{3,5},{4,6},{5,7},{6,0},{7,1},{8,10},{9,11},{10,... | collective-permute-start | bytes 393224 | tf_op jit(solution)/shard_map/ppermute | solution.py:178
  64.8 2.5 %collective-permute-start.4 = (bf16[64,1024]{1,0:T(8,128)(2,1)}, bf16[64,1024]{1,0:T(8,128)(2,1)S(1)}, u32[]{:S(2)}, u32[]{:S(2)}) collective-permute-start(bf16[64,1024]{1,0:T(8,128)(2,1)} %get-tuple-element.32), channel_id=1, source_target_pairs={{0,4},{1,5},{2,6},{3,7},{4,0},{5,1},{6,2},{7,3},{8,12},{9,13},{10,... | collective-permute-start | bytes 393224 | tf_op jit(solution)/shard_map/ppermute | solution.py:178
  67.2 1.7 %collective-permute-done.10.refs_3_ = bf16[256,1024]{1,0:T(8,128)(2,1)S(1)} collective-permute-done((bf16[256,1024]{1,0:T(8,128)(2,1)}, bf16[256,1024]{1,0:T(8,128)(2,1)S(1)}, u32[]{:S(2)}, u32[]{:S(2)}) %collective-permute-start.10) | collective-permute-done | bytes 524320 | tf_op jit(solution)/shard_map/ppermute | solution.py:178
  68.9 1.3 %collective-permute-start.5 = (bf16[64,1024]{1,0:T(8,128)(2,1)}, bf16[64,1024]{1,0:T(8,128)(2,1)S(1)}, u32[]{:S(2)}, u32[]{:S(2)}) collective-permute-start(bf16[64,1024]{1,0:T(8,128)(2,1)} %get-tuple-element.33), channel_id=1, source_target_pairs={{0,6},{1,7},{2,0},{3,1},{4,2},{5,3},{6,4},{7,5},{8,14},{9,15},{10,... | collective-permute-start | bytes 393224 | tf_op jit(solution)/shard_map/ppermute | solution.py:178
  70.2 0.0 collective-permute-done.8.refs_1_
  70.2 5.2 %collective-permute-done.9.refs_2_ = bf16[256,1024]{1,0:T(8,128)(2,1)S(1)} collective-permute-done((bf16[256,1024]{1,0:T(8,128)(2,1)}, bf16[256,1024]{1,0:T(8,128)(2,1)S(1)}, u32[]{:S(2)}, u32[]{:S(2)}) %collective-permute-start.9) | collective-permute-done | bytes 524320 | tf_op jit(solution)/shard_map/ppermute | solution.py:178
  75.4 0.8 copy-done.3
  76.2 2.5 %first_sum.3 = (f32[64,1024]{1,0:T(8,128)}, bf16[64,1024]{1,0:T(8,128)(2,1)}, bf16[64,1024]{1,0:T(8,128)(2,1)}, bf16[64,1024]{1,0:T(8,128)(2,1)}) custom-call(s32[5]{0:T(128)} %stack.36.place, bf16[256,1024]{1,0:T(8,128)(2,1)} %get-tuple-element.37.refs_0_, bf16[256,1024]{1,0:T(8,128)(2,1)} %copy-done.2, bf16[256,1024]{1,0:T(8,128)(2,1)} %copy-done.3, ...), custom_call_target="tpu_custom_call" | custom-call | tf_op jit(solution)/shard_map/first_sum/pallas_call | solution.py:236
  78.7 3.7 %collective-permute-start.11 = (bf16[64,1024]{1,0:T(8,128)(2,1)}, bf16[64,1024]{1,0:T(8,128)(2,1)S(1)}, u32[]{:S(2)}, u32[]{:S(2)}) collective-permute-start(bf16[64,1024]{1,0:T(8,128)(2,1)} %get-tuple-element.42), channel_id=1, source_target_pairs={{0,2},{1,3},{2,4},{3,5},{4,6},{5,7},{6,0},{7,1},{8,10},{9,11},{10,... | collective-permute-start | bytes 393224 | tf_op jit(solution)/shard_map/ppermute | solution.py:178
  82.4 0.0 collective-permute-start.12
  82.4 0.0 collective-permute-done.3.a
  82.4 2.4 %collective-permute-start.13 = (bf16[64,1024]{1,0:T(8,128)(2,1)}, bf16[64,1024]{1,0:T(8,128)(2,1)S(1)}, u32[]{:S(2)}, u32[]{:S(2)}) collective-permute-start(bf16[64,1024]{1,0:T(8,128)(2,1)} %get-tuple-element.44), channel_id=1, source_target_pairs={{0,6},{1,7},{2,0},{3,1},{4,2},{5,3},{6,4},{7,5},{8,14},{9,15},{10,... | collective-permute-start | bytes 393224 | tf_op jit(solution)/shard_map/ppermute | solution.py:178
  84.8 0.0 collective-permute-done.4.b
  84.8 0.0 collective-permute-done.5.c
  84.8 0.6 copy-done.7
  85.5 0.1 copy-done.9
  85.5 1.9 %second_sum.2 = (f32[32,1024]{1,0:T(8,128)}, f32[32,1024]{1,0:T(8,128)}) custom-call(s32[5]{0:T(128)} %stack.36.place, f32[64,1024]{1,0:T(8,128)} %get-tuple-element.30.own, bf16[64,1024]{1,0:T(8,128)(2,1)} %copy-done.6, bf16[64,1024]{1,0:T(8,128)(2,1)} %copy-done.7, bf16[64,1024]{1,0:T(8,128)(2,1)} %copy-done.9), custom_call_target="tpu_custom_call" | custom-call | tf_op jit(solution)/shard_map/second_sum/pallas_call | solution.py:244
  87.4 0.6 collective-permute-start.6
  88.0 0.0 collective-permute-done.11.a
  88.0 0.0 collective-permute-done.13.c
  88.1 0.6 copy-done.8
  88.7 0.1 copy-done.10
  88.7 0.0 copy-done.11
  88.8 1.9 %second_sum.3 = (f32[32,1024]{1,0:T(8,128)}, f32[32,1024]{1,0:T(8,128)}) custom-call(s32[5]{0:T(128)} %stack.36.place, f32[64,1024]{1,0:T(8,128)} %get-tuple-element.41.own, bf16[64,1024]{1,0:T(8,128)(2,1)} %copy-done.8, bf16[64,1024]{1,0:T(8,128)(2,1)} %copy-done.10, bf16[64,1024]{1,0:T(8,128)(2,1)} %copy-done.11), custom_call_target="tpu_custom_call" | custom-call | tf_op jit(solution)/shard_map/second_sum/pallas_call | solution.py:244
  90.7 0.9 collective-permute-start.14
  91.5 0.0 collective-permute-done.6
  91.5 0.9 add_bitcast_fusion.1
  92.5 2.2 %collective-permute-done.14 = f32[32,1024]{1,0:T(8,128)S(1)} collective-permute-done((f32[32,1024]{1,0:T(8,128)}, f32[32,1024]{1,0:T(8,128)S(1)}, u32[]{:S(2)}, u32[]{:S(2)}) %collective-permute-start.14) | collective-permute-done | bytes 131104 | tf_op jit(solution)/shard_map/ppermute | solution.py:178
  94.7 0.9 add_bitcast_fusion
  95.6 0.7 pad_maximum_fusion
  (17 shorter events, 0.0 us)
Async XLA Ops:
  12.5 26.5 %collective-permute-start.7 = (bf16[1024,1024]{1,0:T(8,128)(2,1)}, bf16[1024,1024]{1,0:T(8,128)(2,1)S(1)}, u32[]{:S(2)}, u32[]{:S(2)}) collective-permute-start(bf16[1024,1024]{1,0:T(8,128)(2,1)} %first_transform.1.v0), channel_id=1, source_target_pairs={{32,0},{33,1},{34,2},{35,3},{36,4},{37,5},{38,6},{39,7},{40,8},{41... | collective-permute-start | bytes 6291464 | tf_op jit(solution)/shard_map/ppermute | solution.py:178
  33.2 25.8 %collective-permute-start = (bf16[256,1024]{1,0:T(8,128)(2,1)}, bf16[256,1024]{1,0:T(8,128)(2,1)S(1)}, u32[]{:S(2)}, u32[]{:S(2)}) collective-permute-start(bf16[256,1024]{1,0:T(8,128)(2,1)} %get-tuple-element.27), channel_id=1, source_target_pairs={{0,8},{1,9},{2,10},{3,11},{4,12},{5,13},{6,14},{7,15},{8,16},{9,17... | collective-permute-start | bytes 1572872 | tf_op jit(solution)/shard_map/ppermute | solution.py:178
  34.9 25.3 %collective-permute-start.1 = (bf16[256,1024]{1,0:T(8,128)(2,1)}, bf16[256,1024]{1,0:T(8,128)(2,1)S(1)}, u32[]{:S(2)}, u32[]{:S(2)}) collective-permute-start(bf16[256,1024]{1,0:T(8,128)(2,1)} %get-tuple-element.28), channel_id=1, source_target_pairs={{0,16},{1,17},{2,18},{3,19},{4,20},{5,21},{6,22},{7,23},{8,24},{9,... | collective-permute-start | bytes 1572872 | tf_op jit(solution)/shard_map/ppermute | solution.py:178
  38.3 22.0 %collective-permute-start.2 = (bf16[256,1024]{1,0:T(8,128)(2,1)}, bf16[256,1024]{1,0:T(8,128)(2,1)}, u32[]{:S(2)}, u32[]{:S(2)}) collective-permute-start(bf16[256,1024]{1,0:T(8,128)(2,1)} %get-tuple-element.29), channel_id=1, source_target_pairs={{0,24},{1,25},{2,26},{3,27},{4,28},{5,29},{6,30},{7,31},{8,0},{9,1... | collective-permute-start | bytes 1572872 | tf_op jit(solution)/shard_map/ppermute | solution.py:178
  39.0 1.4 %copy-start = (bf16[1024,1024]{1,0:T(8,128)(2,1)}, bf16[1024,1024]{1,0:T(8,128)(2,1)S(1)}, u32[]{:S(2)}) copy-start(bf16[1024,1024]{1,0:T(8,128)(2,1)S(1)} %collective-permute-done.7.arrived) | copy-start | bytes 6291460
  57.5 11.4 %collective-permute-start.10 = (bf16[256,1024]{1,0:T(8,128)(2,1)}, bf16[256,1024]{1,0:T(8,128)(2,1)S(1)}, u32[]{:S(2)}, u32[]{:S(2)}) collective-permute-start(bf16[256,1024]{1,0:T(8,128)(2,1)} %get-tuple-element.40), channel_id=1, source_target_pairs={{0,24},{1,25},{2,26},{3,27},{4,28},{5,29},{6,30},{7,31},{8,0},{9,1... | collective-permute-start | bytes 1572872 | tf_op jit(solution)/shard_map/ppermute | solution.py:178
  57.6 12.6 %collective-permute-start.8 = (bf16[256,1024]{1,0:T(8,128)(2,1)}, bf16[256,1024]{1,0:T(8,128)(2,1)S(1)}, u32[]{:S(2)}, u32[]{:S(2)}) collective-permute-start(bf16[256,1024]{1,0:T(8,128)(2,1)} %get-tuple-element.38), channel_id=1, source_target_pairs={{0,8},{1,9},{2,10},{3,11},{4,12},{5,13},{6,14},{7,15},{8,16},{9,17... | collective-permute-start | bytes 1572872 | tf_op jit(solution)/shard_map/ppermute | solution.py:178
  59.1 1.2 %copy-start.4 = (bf16[256,1024]{1,0:T(8,128)(2,1)}, bf16[256,1024]{1,0:T(8,128)(2,1)S(1)}, u32[]{:S(2)}) copy-start(bf16[256,1024]{1,0:T(8,128)(2,1)S(1)} %collective-permute-done.refs_1_) | copy-start | bytes 1572868
  59.1 16.3 %collective-permute-start.9 = (bf16[256,1024]{1,0:T(8,128)(2,1)}, bf16[256,1024]{1,0:T(8,128)(2,1)S(1)}, u32[]{:S(2)}, u32[]{:S(2)}) collective-permute-start(bf16[256,1024]{1,0:T(8,128)(2,1)} %get-tuple-element.39), channel_id=1, source_target_pairs={{0,16},{1,17},{2,18},{3,19},{4,20},{5,21},{6,22},{7,23},{8,24},{9,... | collective-permute-start | bytes 1572872 | tf_op jit(solution)/shard_map/ppermute | solution.py:178
  60.2 0.8 copy-start.5
  63.6 18.8 %collective-permute-start.3 = (bf16[64,1024]{1,0:T(8,128)(2,1)}, bf16[64,1024]{1,0:T(8,128)(2,1)S(1)}, u32[]{:S(2)}, u32[]{:S(2)}) collective-permute-start(bf16[64,1024]{1,0:T(8,128)(2,1)} %get-tuple-element.31), channel_id=1, source_target_pairs={{0,2},{1,3},{2,4},{3,5},{4,6},{5,7},{6,0},{7,1},{8,10},{9,11},{10,... | collective-permute-start | bytes 393224 | tf_op jit(solution)/shard_map/ppermute | solution.py:178
  64.8 20.1 %collective-permute-start.4 = (bf16[64,1024]{1,0:T(8,128)(2,1)}, bf16[64,1024]{1,0:T(8,128)(2,1)S(1)}, u32[]{:S(2)}, u32[]{:S(2)}) collective-permute-start(bf16[64,1024]{1,0:T(8,128)(2,1)} %get-tuple-element.32), channel_id=1, source_target_pairs={{0,4},{1,5},{2,6},{3,7},{4,0},{5,1},{6,2},{7,3},{8,12},{9,13},{10,... | collective-permute-start | bytes 393224 | tf_op jit(solution)/shard_map/ppermute | solution.py:178
  68.9 6.5 %copy-start.1 = (bf16[256,1024]{1,0:T(8,128)(2,1)}, bf16[256,1024]{1,0:T(8,128)(2,1)S(1)}, u32[]{:S(2)}) copy-start(bf16[256,1024]{1,0:T(8,128)(2,1)S(1)} %collective-permute-done.10.refs_3_) | copy-start | bytes 1572868
  68.9 15.9 %collective-permute-start.5 = (bf16[64,1024]{1,0:T(8,128)(2,1)}, bf16[64,1024]{1,0:T(8,128)(2,1)S(1)}, u32[]{:S(2)}, u32[]{:S(2)}) collective-permute-start(bf16[64,1024]{1,0:T(8,128)(2,1)} %get-tuple-element.33), channel_id=1, source_target_pairs={{0,6},{1,7},{2,0},{3,1},{4,2},{5,3},{6,4},{7,5},{8,14},{9,15},{10,... | collective-permute-start | bytes 393224 | tf_op jit(solution)/shard_map/ppermute | solution.py:178
  70.2 5.2 %copy-start.2 = (bf16[256,1024]{1,0:T(8,128)(2,1)}, bf16[256,1024]{1,0:T(8,128)(2,1)S(1)}, u32[]{:S(2)}) copy-start(bf16[256,1024]{1,0:T(8,128)(2,1)S(1)} %collective-permute-done.8.refs_1_) | copy-start | bytes 1572868
  75.4 0.8 copy-start.3
  78.7 9.3 %collective-permute-start.11 = (bf16[64,1024]{1,0:T(8,128)(2,1)}, bf16[64,1024]{1,0:T(8,128)(2,1)S(1)}, u32[]{:S(2)}, u32[]{:S(2)}) collective-permute-start(bf16[64,1024]{1,0:T(8,128)(2,1)} %get-tuple-element.42), channel_id=1, source_target_pairs={{0,2},{1,3},{2,4},{3,5},{4,6},{5,7},{6,0},{7,1},{8,10},{9,11},{10,... | collective-permute-start | bytes 393224 | tf_op jit(solution)/shard_map/ppermute | solution.py:178
  82.4 5.7 %collective-permute-start.12 = (bf16[64,1024]{1,0:T(8,128)(2,1)}, bf16[64,1024]{1,0:T(8,128)(2,1)S(1)}, u32[]{:S(2)}, u32[]{:S(2)}) collective-permute-start(bf16[64,1024]{1,0:T(8,128)(2,1)} %get-tuple-element.43), channel_id=1, source_target_pairs={{0,4},{1,5},{2,6},{3,7},{4,0},{5,1},{6,2},{7,3},{8,12},{9,13},{10,... | collective-permute-start | bytes 393224 | tf_op jit(solution)/shard_map/ppermute | solution.py:178
  82.4 2.5 %copy-start.6 = (bf16[64,1024]{1,0:T(8,128)(2,1)}, bf16[64,1024]{1,0:T(8,128)(2,1)S(1)}, u32[]{:S(2)}) copy-start(bf16[64,1024]{1,0:T(8,128)(2,1)S(1)} %collective-permute-done.3.a) | copy-start | bytes 393220
  82.4 5.7 %collective-permute-start.13 = (bf16[64,1024]{1,0:T(8,128)(2,1)}, bf16[64,1024]{1,0:T(8,128)(2,1)S(1)}, u32[]{:S(2)}, u32[]{:S(2)}) collective-permute-start(bf16[64,1024]{1,0:T(8,128)(2,1)} %get-tuple-element.44), channel_id=1, source_target_pairs={{0,6},{1,7},{2,0},{3,1},{4,2},{5,3},{6,4},{7,5},{8,14},{9,15},{10,... | collective-permute-start | bytes 393224 | tf_op jit(solution)/shard_map/ppermute | solution.py:178
  84.8 0.7 copy-start.7
  84.8 0.7 copy-start.9
  87.4 4.1 %collective-permute-start.6 = (f32[32,1024]{1,0:T(8,128)}, f32[32,1024]{1,0:T(8,128)S(1)}, u32[]{:S(2)}, u32[]{:S(2)}) collective-permute-start(f32[32,1024]{1,0:T(8,128)} %get-tuple-element.35), channel_id=1, source_target_pairs={{0,1},{1,0},{2,3},{3,2},{4,5},{5,4},{6,7},{7,6},{8,9},{9,8},{10,11... | collective-permute-start | bytes 393224 | tf_op jit(solution)/shard_map/ppermute | solution.py:178
  88.0 0.7 copy-start.8
  88.0 0.7 copy-start.10
  88.1 0.7 copy-start.11
  90.7 4.0 %collective-permute-start.14 = (f32[32,1024]{1,0:T(8,128)}, f32[32,1024]{1,0:T(8,128)S(1)}, u32[]{:S(2)}, u32[]{:S(2)}) collective-permute-start(f32[32,1024]{1,0:T(8,128)} %get-tuple-element.46), channel_id=1, source_target_pairs={{0,1},{1,0},{2,3},{3,2},{4,5},{5,4},{6,7},{7,6},{8,9},{9,8},{10,11... | collective-permute-start | bytes 393224 | tf_op jit(solution)/shard_map/ppermute | solution.py:178

commit v2 on v0

v2 whole, which is shorter than its diff:
```python
import jax
import jax.numpy as jnp
from jax import lax
from jax.experimental import pallas as pl
from jax.experimental.pallas import tpu as pltpu
from jax.sharding import PartitionSpec as P

BF16, F32 = jnp.bfloat16, jnp.float32
TILE = 512
SUB = 64
VMEM = pl.BlockSpec(memory_space=pltpu.VMEM)
HBM = pl.BlockSpec(memory_space=pltpu.HBM)


def params(mib):
    return pltpu.CompilerParams(vmem_limit_bytes=mib * 1024 * 1024)


def position():
    q, r = lax.axis_index("sector"), lax.axis_index("grid")
    x, z, y = r // 8, lax.rem(r // 2, 4), lax.rem(r, 2)
    odd = lax.rem(q, 2) == 1
    return jnp.where(odd, z, x), jnp.where(odd, x, z), y, odd, q == 3


def tiles(rows, cols, step):
    high = rows // TILE

    @pl.loop(0, high * (cols // TILE))
    def _(t):
        at = pl.ds(pl.multiple_of(lax.rem(t, high) * TILE, TILE), TILE)
        step(t, at, pl.ds(pl.multiple_of((t // high) * TILE, TILE), TILE))


def transform(b, c, put, wait=None):
    def step(t, rows, cols):
        if wait is not None:
            wait(t)
        put(rows, cols, jnp.dot(b[rows, :], c[:, cols], preferred_element_type=F32).astype(BF16))

    tiles(b.shape[0], c.shape[1], step)


def spread(w, wide):
    for k in range(w.shape[0]):
        wide[k * 128 : (k + 1) * 128, :] = jnp.broadcast_to(w[k : k + 1, :], (128, 128)).T


def weighted(wide, rows, field):
    factor = jnp.concatenate([wide[rows, :]] * (field.shape[1] // 128), axis=1)
    return (factor * field.astype(F32)).astype(BF16)


def intersect(v, w, product, outs):
    def step(t, rows, cols):
        product[rows, cols] = lax.dot_general(
            v[:, rows], w[:, cols], (((0,), (0,)), ((), ())), preferred_element_type=F32
        ).astype(BF16)

    tiles(v.shape[1], w.shape[1], step)
    own, _, _, odd, _ = position()
    for k, out in enumerate(outs):
        first = lax.rem(own + k, 4)
        for second in range(4):
            block = jnp.where(odd, second * 4 + first, first * 4 + second)
            rows = pl.ds(pl.multiple_of(block * SUB, SUB), SUB)
            out[second * SUB : (second + 1) * SUB, :] = product[rows, :]


def first_kernel(b_hbm, c_hbm, v_out, b, c1, c0, sems):
    halves = [pl.ds(n * TILE, TILE) for n in range(2)]
    copies = [
        pltpu.make_async_copy(b_hbm.at[halves[0]], b.at[halves[0]], sems.at[0]),
        pltpu.make_async_copy(c_hbm.at[0, :, halves[0]], c0.at[:, halves[0]], sems.at[1]),
        pltpu.make_async_copy(b_hbm.at[halves[1]], b.at[halves[1]], sems.at[2]),
        pltpu.make_async_copy(c_hbm.at[0, :, halves[1]], c0.at[:, halves[1]], sems.at[3]),
        pltpu.make_async_copy(c_hbm.at[1], c1, sems.at[4]),
    ]
    for copy in copies:
        copy.start()
    copies[0].wait()

    def wait(t):
        for n in range(3):

            @pl.when(t == n)
            def _():
                copies[n + 1].wait()

    def put(rows, cols, values):
        v_out[rows, cols] = values

    transform(b, c0, put, wait)
    copies[4].wait()


def second_kernel(b, c1, v0, weights, next_hbm, v_out, out0, out1, out2, out3, after, wide, w, product, sem):
    last = position()[4]
    copy = pltpu.make_async_copy(next_hbm, after, sem)

    @pl.when(last)
    def _():
        copy.start()

    spread(weights, wide)

    def put(rows, cols, values):
        v_out[rows, cols] = values
        w[rows, cols] = weighted(wide, rows, values)

    transform(b, c1, put)
    intersect(v0, w, product, (out0, out1, out2, out3))

    @pl.when(last)
    def _():
        copy.wait()


def third_kernel(b, after, v1, arrived, weights, out0, out1, out2, out3, wide, w, product):
    last = position()[4]
    spread(weights, wide)

    @pl.when(last)
    def _():
        def put(rows, cols, values):
            w[rows, cols] = weighted(wide, rows, values)

        transform(b, after, put)

    @pl.when(jnp.logical_not(last))
    def _():
        @pl.loop(0, arrived.shape[0] // 128)
        def _(m):
            rows = pl.ds(pl.multiple_of(m * 128, 128), 128)
            w[rows, :] = weighted(wide, rows, arrived[rows, :])

    intersect(v1, w, product, (out0, out1, out2, out3))


def first_sum(part0, part1, part2, part3, own, out1, out2, out3):
    place = position()[1]
    for k, out in enumerate((own, out1, out2, out3)):
        rows = pl.ds(pl.multiple_of(lax.rem(place + k, 4) * SUB, SUB), SUB)
        total = sum(part[rows, :].astype(F32) for part in (part0, part1, part2, part3))
        out[...] = total.astype(out.dtype)


def second_sum(own, a, b, c, kept, out):
    place, half = position()[2], SUB // 2
    for k, to in enumerate((kept, out)):
        rows = pl.ds(pl.multiple_of(lax.rem(place + k, 2) * half, half), half)
        to[...] = own[rows, :] + a[rows, :].astype(F32) + b[rows, :].astype(F32) + c[rows, :].astype(F32)


def last_sum(kept0, got0, kept1, got1, out):
    out[0] = kept0[...] + got0[...]
    out[1] = kept1[...] + got1[...]


def pairs_of(move):
    found = []
    for q in range(4):
        for r in range(32):
            t = move(q, r // 8, (r // 2) % 4, r % 2)
            if t is not None:
                found.append((q * 32 + r, t[0] * 32 + (t[1] % 4) * 8 + (t[2] % 4) * 2 + t[3] % 2))
    return found


def along(first, k):
    def move(q, x, z, y):
        return (q, x + k, z, y) if (q % 2 == 0) == first else (q, x, z + k, y)

    return move


def send(value, move):
    return lax.ppermute(value, ("sector", "grid"), pairs_of(move))


def per_device(coeffs, basis_values, weights, next_coeffs):
    grid_points, basis = basis_values.shape
    width = coeffs.shape[2]
    coeffs, basis_values, next_coeffs = (
        pltpu.with_memory_space_constraint(a, pltpu.HBM) for a in (coeffs, basis_values, next_coeffs)
    )
    rows_of = weights.reshape(grid_points // 128, 128)
    field = pltpu.VMEM((grid_points, width), BF16)
    part = pltpu.VMEM((width // 4, width), BF16)
    spectrum = pltpu.VMEM((basis, width), BF16)
    scratch = [
        pltpu.VMEM((grid_points, 128), F32),
        pltpu.VMEM((grid_points, width), BF16),
        pltpu.VMEM((width, width), BF16),
    ]

    def cost(transforms, products):
        return pl.CostEstimate(
            flops=2 * grid_points * width * (transforms * basis + products * width),
            bytes_accessed=2 * (transforms * basis * (grid_points + width) + 3 * width * width),
            transcendentals=0,
        )

    v0, b, c1 = pl.pallas_call(
        first_kernel,
        out_shape=[field, pltpu.VMEM((grid_points, basis), BF16), spectrum],
        in_specs=[HBM, HBM],
        out_specs=[VMEM] * 3,
        scratch_shapes=[spectrum, pltpu.SemaphoreType.DMA((5,))],
        compiler_params=params(16),
        cost_estimate=cost(1, 0),
        name="first_transform",
    )(basis_values, coeffs)
    arrived = send(v0, lambda q, x, z, y: (q - 1, x, z, y) if q else None)
    v1, *parts0, after = pl.pallas_call(
        second_kernel,
        out_shape=[field] + [part] * 4 + [spectrum],
        in_specs=[VMEM] * 4 + [HBM],
        out_specs=[VMEM] * 6,
        scratch_shapes=scratch + [pltpu.SemaphoreType.DMA],
        compiler_params=params(16),
        cost_estimate=cost(1, 1),
        name="second_transform",
    )(b, c1, v0, rows_of, next_coeffs)
    parts1 = pl.pallas_call(
        third_kernel,
        out_shape=[part] * 4,
        in_specs=[VMEM] * 5,
        out_specs=[VMEM] * 4,
        scratch_shapes=scratch,
        compiler_params=params(16),
        cost_estimate=cost(0, 1),
        name="second_intersection",
    )(b, after, v1, arrived, rows_of)

    def across(parts):
        got = [send(parts[k], along(True, k)) for k in (1, 2, 3)]
        return pl.pallas_call(
            first_sum,
            out_shape=[pltpu.VMEM((SUB, width), F32)] + [pltpu.VMEM((SUB, width), BF16)] * 3,
            in_specs=[VMEM] * 4,
            out_specs=[VMEM] * 4,
            compiler_params=params(8),
            name="first_sum",
        )(parts[0], *got)

    def along_second(own, outs):
        got = [send(outs[k - 1], along(False, k)) for k in (1, 2, 3)]
        return pl.pallas_call(
            second_sum,
            out_shape=[pltpu.VMEM((SUB // 2, width), F32)] * 2,
            in_specs=[VMEM] * 4,
            out_specs=[VMEM] * 2,
            compiler_params=params(8),
            name="second_sum",
        )(own, *got)

    def swapped(out):
        return send(out, lambda q, x, z, y: (q, x, z, y + 1))

    own0, *outs0 = across(parts0)
    kept0, out0 = along_second(own0, outs0)
    got0 = swapped(out0)
    own1, *outs1 = across(parts1)
    kept1, out1 = along_second(own1, outs1)
    got1 = swapped(out1)
    return pl.pallas_call(
        last_sum,
        out_shape=jax.ShapeDtypeStruct((2, SUB // 2, width), F32),
        in_specs=[VMEM] * 4,
        out_specs=VMEM,
        compiler_params=params(8),
        name="last_sum",
    )(kept0, got0, kept1, got1)


def solution(mesh):
    return jax.shard_map(
        per_device,
        mesh=mesh,
        in_specs=(P("sector", None, None), P("grid", None), P("grid"), P()),
        out_specs=P("sector", "grid", None),
        check_vma=False,
    )
```

time: 447 us -> 79.1 us (0.18)
  waiting for transfers between devices: 388 us -> 28.6 us
  matrix products: 33.2 us -> 0 us
  Pallas kernels: 0 us -> 25.9 us
  starting transfers between devices: 2.57 us -> 24.4 us
  between operations: 13.5 us -> 0.1 us
    psum x1 -> x0, waiting for transfers between devices: 381 us -> none  [per_device(): summed = lax.psum(partials, 'grid')]
    dot_general x4 -> x0, matrix products: 33.2 us -> none  [the longest x2 22.2 us: transform(): jnp.dot(basis_values, coefficient, preferred_element_type=jnp.float32)]
    pallas_call x0 -> x8, Pallas kernels: none -> 25.9 us  [the longest x1 10.7 us: per_device(): pl.pallas_call(second_kernel, out_shape=[field] + [part] * 4 + [spectrum]...]
    ppermute x1 -> x15, waiting for transfers between devices: 6.41 us -> 28.6 us  [send(): return lax.ppermute(value, ('sector', 'grid'), pairs_of(move))]
    ppermute x1 -> x15, starting transfers between devices: 2.57 us -> 24.4 us  [send(): return lax.ppermute(value, ('sector', 'grid'), pairs_of(move))]
  transfers between devices with their start and end apart: 2 -> 15, of which waited for: 2 -> 5; matrix products, arithmetic and copies ran while one was open for 4% -> 0% of each run, Pallas kernels for 0% -> 19%
where the time goes in v2:
time: 79.1 us; the launch traced here: 79 us
  waiting for transfers between devices  28.6 us (36%)
  Pallas kernels  25.9 us (33%)
  starting transfers between devices  24.4 us (31%)
    ppermute x15, waiting for transfers between devices, send(): return lax.ppermute(value, ('sector', 'grid'), pairs_of(move))  28.6 us
    ppermute x15, starting transfers between devices, send(): return lax.ppermute(value, ('sector', 'grid'), pairs_of(move))  24.4 us
    pallas_call x1, Pallas kernels, per_device(): pl.pallas_call(second_kernel, out_shape=[field] + [part] * 4 + [spectrum]...  10.7 us
    pallas_call x1, Pallas kernels, per_device(): pl.pallas_call(first_kernel, out_shape=[field, pltpu.VMEM((grid_points, b...  10.2 us
    pallas_call x1, Pallas kernels, per_device(): pl.pallas_call(third_kernel, out_shape=[part] * 4, in_specs=[VMEM] * 5, o...  3.7 us
  transfers between devices with their start and end apart: 15, of which 5 were waited for; matrix products, arithmetic and copies ran while one was open for 0% of the time, Pallas kernels for 19%

profile of v2, /device:TPU:30, one launch (start us, length us, event | category | flops | bytes accessed | tf_op | source)
XLA Modules:
  0.0 79.0 jit_solution(8734373476655854546)
XLA Ops:
  0.0 0.0 copy-start
  0.0 10.2 %first_transform.1 = (bf16[1024,1024]{1,0:T(8,128)(2,1)S(1)}, bf16[1024,3072]{1,0:T(8,128)(2,1)S(1)}, bf16[3072,1024]{1,0:T(8,128)(2,1)S(1)}) custom-call(bf16[1024,3072]{1,0:T(8,128)(2,1)} %b_hbm.1, bf16[2,3072,1024]{2,1,0:T(8,128)(2,1)} %c_hbm.1), custom_call_target="tpu_custom_call" | custom-call | flops 6442450944 | bytes 18874368 | tf_op jit(solution)/shard_map/first_transform/pallas_call | solution.py:204
  10.2 2.6 %collective-permute-start.7 = (bf16[1024,1024]{1,0:T(8,128)(2,1)S(1)}, bf16[1024,1024]{1,0:T(8,128)(2,1)S(1)}, u32[]{:S(2)}, u32[]{:S(2)}) collective-permute-start(bf16[1024,1024]{1,0:T(8,128)(2,1)S(1)} %get-tuple-element.32.v0), channel_id=1, source_target_pairs={{32,0},{33,1},{34,2},{35,3},{36,4},{37,5},{38,6},{39,7},{40,8},{41... | collective-permute-start | bytes 6291464 | tf_op jit(solution)/shard_map/ppermute | solution.py:178
  12.8 0.0 copy-done
  12.8 10.7 %second_transform.1 = (bf16[1024,1024]{1,0:T(8,128)(2,1)S(1)}, bf16[256,1024]{1,0:T(8,128)(2,1)S(1)}, bf16[256,1024]{1,0:T(8,128)(2,1)S(1)}, bf16[256,1024]{1,0:...) custom-call(bf16[1024,3072]{1,0:T(8,128)(2,1)S(1)} %get-tuple-element.30.b, ...), custom_call_target="tpu_custom_call" | custom-call | flops 8589934592 | bytes 18874368 | tf_op jit(solution)/shard_map/second_transform/pallas_call | solution.py:215
  23.5 0.5 collective-permute-start
  24.0 2.4 %collective-permute-start.1 = (bf16[256,1024]{1,0:T(8,128)(2,1)S(1)}, bf16[256,1024]{1,0:T(8,128)(2,1)S(1)}, u32[]{:S(2)}, u32[]{:S(2)}) collective-permute-start(bf16[256,1024]{1,0:T(8,128)(2,1)S(1)} %get-tuple-element.35), channel_id=1, source_target_pairs={{0,16},{1,17},{2,18},{3,19},{4,20},{5,21},{6,22},{7,23},{8,24},{9,... | collective-permute-start | bytes 1572872 | tf_op jit(solution)/shard_map/ppermute | solution.py:178
  26.5 0.0 collective-permute-start.2
  26.5 9.9 %collective-permute-done.7.arrived = bf16[1024,1024]{1,0:T(8,128)(2,1)S(1)} collective-permute-done((bf16[1024,1024]{1,0:T(8,128)(2,1)S(1)}, bf16[1024,1024]{1,0:T(8,128)(2,1)S(1)}, u32[]{:S(2)}, u32[]{:S(2)}) %collective-permute-start.7) | collective-permute-done | bytes 2097184 | tf_op jit(solution)/shard_map/ppermute | solution.py:178
  36.3 3.7 %second_intersection.1 = (bf16[256,1024]{1,0:T(8,128)(2,1)S(1)}, bf16[256,1024]{1,0:T(8,128)(2,1)S(1)}, bf16[256,1024]{1,0:T(8,128)(2,1)S(1)}, bf16[256,1024]{1,0:T(8,128)(2,1)S(1)}) custom-call(bf16[1024,3072]{1,0:T(8,128)(2,1)S(1)} %get-tuple-element.30.b, bf16[3072,1024]{1,0:T(8,128)(2,1)S(1)} %get-tuple-element.43.after, ...), custom_call_target="tpu_custom_call" | custom-call | flops 2147483648 | bytes 6291456 | tf_op jit(solution)/shard_map/second_intersection/pallas_call | solution.py:225
  40.0 0.9 %collective-permute-start.10 = (bf16[256,1024]{1,0:T(8,128)(2,1)S(1)}, bf16[256,1024]{1,0:T(8,128)(2,1)S(1)}, u32[]{:S(2)}, u32[]{:S(2)}) collective-permute-start(bf16[256,1024]{1,0:T(8,128)(2,1)S(1)} %get-tuple-element.48), channel_id=1, source_target_pairs={{0,24},{1,25},{2,26},{3,27},{4,28},{5,29},{6,30},{7,31},{8,0},{9,1... | collective-permute-start | bytes 1572872 | tf_op jit(solution)/shard_map/ppermute | solution.py:178
  40.9 2.4 %collective-permute-start.8 = (bf16[256,1024]{1,0:T(8,128)(2,1)S(1)}, bf16[256,1024]{1,0:T(8,128)(2,1)S(1)}, u32[]{:S(2)}, u32[]{:S(2)}) collective-permute-start(bf16[256,1024]{1,0:T(8,128)(2,1)S(1)} %get-tuple-element.46), channel_id=1, source_target_pairs={{0,8},{1,9},{2,10},{3,11},{4,12},{5,13},{6,14},{7,15},{8,16},{9,17... | collective-permute-start | bytes 1572872 | tf_op jit(solution)/shard_map/ppermute | solution.py:178
  43.3 0.0 collective-permute-done.part1
  43.3 0.2 collective-permute-start.9
  43.5 0.0 collective-permute-done.1.part2
  43.5 0.0 collective-permute-done.2.part3
  43.5 0.3 first_sum.2
  43.8 2.0 %collective-permute-start.3 = (bf16[64,1024]{1,0:T(8,128)(2,1)S(1)}, bf16[64,1024]{1,0:T(8,128)(2,1)S(1)}, u32[]{:S(2)}, u32[]{:S(2)}) collective-permute-start(bf16[64,1024]{1,0:T(8,128)(2,1)S(1)} %get-tuple-element.38), channel_id=1, source_target_pairs={{0,2},{1,3},{2,4},{3,5},{4,6},{5,7},{6,0},{7,1},{8,10},{9,11},{10,... | collective-permute-start | bytes 393224 | tf_op jit(solution)/shard_map/ppermute | solution.py:178
  45.8 3.6 %collective-permute-start.4 = (bf16[64,1024]{1,0:T(8,128)(2,1)S(1)}, bf16[64,1024]{1,0:T(8,128)(2,1)S(1)}, u32[]{:S(2)}, u32[]{:S(2)}) collective-permute-start(bf16[64,1024]{1,0:T(8,128)(2,1)S(1)} %get-tuple-element.39), channel_id=1, source_target_pairs={{0,4},{1,5},{2,6},{3,7},{4,0},{5,1},{6,2},{7,3},{8,12},{9,13},{10,... | collective-permute-start | bytes 393224 | tf_op jit(solution)/shard_map/ppermute | solution.py:178
  49.4 8.7 %collective-permute-done.10.part3 = bf16[256,1024]{1,0:T(8,128)(2,1)S(1)} collective-permute-done((bf16[256,1024]{1,0:T(8,128)(2,1)S(1)}, bf16[256,1024]{1,0:T(8,128)(2,1)S(1)}, u32[]{:S(2)}, u32[]{:S(2)}) %collective-permute-start.10) | collective-permute-done | bytes 524320 | tf_op jit(solution)/shard_map/ppermute | solution.py:178
  58.1 6.2 %collective-permute-start.5 = (bf16[64,1024]{1,0:T(8,128)(2,1)S(1)}, bf16[64,1024]{1,0:T(8,128)(2,1)S(1)}, u32[]{:S(2)}, u32[]{:S(2)}) collective-permute-start(bf16[64,1024]{1,0:T(8,128)(2,1)S(1)} %get-tuple-element.40), channel_id=1, source_target_pairs={{0,6},{1,7},{2,0},{3,1},{4,2},{5,3},{6,4},{7,5},{8,14},{9,15},{10,... | collective-permute-start | bytes 393224 | tf_op jit(solution)/shard_map/ppermute | solution.py:178
  64.4 0.0 collective-permute-done.8.part1
  64.4 0.0 collective-permute-done.9.part2
  64.4 0.3 first_sum.3
  64.6 0.1 collective-permute-start.11
  64.7 1.5 %collective-permute-start.12 = (bf16[64,1024]{1,0:T(8,128)(2,1)S(1)}, bf16[64,1024]{1,0:T(8,128)(2,1)S(1)}, u32[]{:S(2)}, u32[]{:S(2)}) collective-permute-start(bf16[64,1024]{1,0:T(8,128)(2,1)S(1)} %get-tuple-element.51), channel_id=1, source_target_pairs={{0,4},{1,5},{2,6},{3,7},{4,0},{5,1},{6,2},{7,3},{8,12},{9,13},{10,... | collective-permute-start | bytes 393224 | tf_op jit(solution)/shard_map/ppermute | solution.py:178
  66.2 0.0 collective-permute-done.3.a
  66.2 1.7 %collective-permute-start.13 = (bf16[64,1024]{1,0:T(8,128)(2,1)S(1)}, bf16[64,1024]{1,0:T(8,128)(2,1)S(1)}, u32[]{:S(2)}, u32[]{:S(2)}) collective-permute-start(bf16[64,1024]{1,0:T(8,128)(2,1)S(1)} %get-tuple-element.52), channel_id=1, source_target_pairs={{0,6},{1,7},{2,0},{3,1},{4,2},{5,3},{6,4},{7,5},{8,14},{9,15},{10,... | collective-permute-start | bytes 393224 | tf_op jit(solution)/shard_map/ppermute | solution.py:178
  67.9 0.0 collective-permute-done.4.b
  67.9 0.0 collective-permute-done.5.c
  68.0 0.1 second_sum.2
  68.0 0.1 collective-permute-start.6
  68.1 4.2 %collective-permute-done.11.a = bf16[64,1024]{1,0:T(8,128)(2,1)S(1)} collective-permute-done((bf16[64,1024]{1,0:T(8,128)(2,1)S(1)}, bf16[64,1024]{1,0:T(8,128)(2,1)S(1)}, u32[]{:S(2)}, u32[]{:S(2)}) %collective-permute-start.11) | collective-permute-done | bytes 131104 | tf_op jit(solution)/shard_map/ppermute | solution.py:178
  72.3 0.0 collective-permute-done.12.b
  72.3 0.9 %collective-permute-done.13.c = bf16[64,1024]{1,0:T(8,128)(2,1)S(1)} collective-permute-done((bf16[64,1024]{1,0:T(8,128)(2,1)S(1)}, bf16[64,1024]{1,0:T(8,128)(2,1)S(1)}, u32[]{:S(2)}, u32[]{:S(2)}) %collective-permute-start.13) | collective-permute-done | bytes 131104 | tf_op jit(solution)/shard_map/ppermute | solution.py:178
  73.2 0.1 second_sum.3
  73.2 0.1 collective-permute-start.14
  73.3 0.0 collective-permute-done.6.got0
  73.4 4.9 %collective-permute-done.14.got1 = f32[32,1024]{1,0:T(8,128)S(1)} collective-permute-done((f32[32,1024]{1,0:T(8,128)S(1)}, f32[32,1024]{1,0:T(8,128)S(1)}, u32[]{:S(2)}, u32[]{:S(2)}) %collective-permute-start.14) | collective-permute-done | bytes 131104 | tf_op jit(solution)/shard_map/ppermute | solution.py:178
  78.3 0.7 last_sum.1
Async XLA Ops:
  0.0 12.8 %copy-start = (f32[1024]{0:T(1024)S(1)}, f32[1024]{0:T(1024)}, u32[]{:S(2)}) copy-start(f32[1024]{0:T(1024)} %param.6) | copy-start | bytes 12292
  10.2 26.1 %collective-permute-start.7 = (bf16[1024,1024]{1,0:T(8,128)(2,1)S(1)}, bf16[1024,1024]{1,0:T(8,128)(2,1)S(1)}, u32[]{:S(2)}, u32[]{:S(2)}) collective-permute-start(bf16[1024,1024]{1,0:T(8,128)(2,1)S(1)} %get-tuple-element.32.v0), channel_id=1, source_target_pairs={{32,0},{33,1},{34,2},{35,3},{36,4},{37,5},{38,6},{39,7},{40,8},{41... | collective-permute-start | bytes 6291464 | tf_op jit(solution)/shard_map/ppermute | solution.py:178
  23.5 19.9 %collective-permute-start = (bf16[256,1024]{1,0:T(8,128)(2,1)S(1)}, bf16[256,1024]{1,0:T(8,128)(2,1)S(1)}, u32[]{:S(2)}, u32[]{:S(2)}) collective-permute-start(bf16[256,1024]{1,0:T(8,128)(2,1)S(1)} %get-tuple-element.34), channel_id=1, source_target_pairs={{0,8},{1,9},{2,10},{3,11},{4,12},{5,13},{6,14},{7,15},{8,16},{9,17... | collective-permute-start | bytes 1572872 | tf_op jit(solution)/shard_map/ppermute | solution.py:178
  24.0 19.5 %collective-permute-start.1 = (bf16[256,1024]{1,0:T(8,128)(2,1)S(1)}, bf16[256,1024]{1,0:T(8,128)(2,1)S(1)}, u32[]{:S(2)}, u32[]{:S(2)}) collective-permute-start(bf16[256,1024]{1,0:T(8,128)(2,1)S(1)} %get-tuple-element.35), channel_id=1, source_target_pairs={{0,16},{1,17},{2,18},{3,19},{4,20},{5,21},{6,22},{7,23},{8,24},{9,... | collective-permute-start | bytes 1572872 | tf_op jit(solution)/shard_map/ppermute | solution.py:178
  26.5 17.1 %collective-permute-start.2 = (bf16[256,1024]{1,0:T(8,128)(2,1)S(1)}, bf16[256,1024]{1,0:T(8,128)(2,1)S(1)}, u32[]{:S(2)}, u32[]{:S(2)}) collective-permute-start(bf16[256,1024]{1,0:T(8,128)(2,1)S(1)} %get-tuple-element.36), channel_id=1, source_target_pairs={{0,24},{1,25},{2,26},{3,27},{4,28},{5,29},{6,30},{7,31},{8,0},{9,1... | collective-permute-start | bytes 1572872 | tf_op jit(solution)/shard_map/ppermute | solution.py:178
  40.0 18.1 %collective-permute-start.10 = (bf16[256,1024]{1,0:T(8,128)(2,1)S(1)}, bf16[256,1024]{1,0:T(8,128)(2,1)S(1)}, u32[]{:S(2)}, u32[]{:S(2)}) collective-permute-start(bf16[256,1024]{1,0:T(8,128)(2,1)S(1)} %get-tuple-element.48), channel_id=1, source_target_pairs={{0,24},{1,25},{2,26},{3,27},{4,28},{5,29},{6,30},{7,31},{8,0},{9,1... | collective-permute-start | bytes 1572872 | tf_op jit(solution)/shard_map/ppermute | solution.py:178
  40.9 23.4 %collective-permute-start.8 = (bf16[256,1024]{1,0:T(8,128)(2,1)S(1)}, bf16[256,1024]{1,0:T(8,128)(2,1)S(1)}, u32[]{:S(2)}, u32[]{:S(2)}) collective-permute-start(bf16[256,1024]{1,0:T(8,128)(2,1)S(1)} %get-tuple-element.46), channel_id=1, source_target_pairs={{0,8},{1,9},{2,10},{3,11},{4,12},{5,13},{6,14},{7,15},{8,16},{9,17... | collective-permute-start | bytes 1572872 | tf_op jit(solution)/shard_map/ppermute | solution.py:178
  43.3 21.0 %collective-permute-start.9 = (bf16[256,1024]{1,0:T(8,128)(2,1)S(1)}, bf16[256,1024]{1,0:T(8,128)(2,1)S(1)}, u32[]{:S(2)}, u32[]{:S(2)}) collective-permute-start(bf16[256,1024]{1,0:T(8,128)(2,1)S(1)} %get-tuple-element.47), channel_id=1, source_target_pairs={{0,16},{1,17},{2,18},{3,19},{4,20},{5,21},{6,22},{7,23},{8,24},{9,... | collective-permute-start | bytes 1572872 | tf_op jit(solution)/shard_map/ppermute | solution.py:178
  43.8 22.4 %collective-permute-start.3 = (bf16[64,1024]{1,0:T(8,128)(2,1)S(1)}, bf16[64,1024]{1,0:T(8,128)(2,1)S(1)}, u32[]{:S(2)}, u32[]{:S(2)}) collective-permute-start(bf16[64,1024]{1,0:T(8,128)(2,1)S(1)} %get-tuple-element.38), channel_id=1, source_target_pairs={{0,2},{1,3},{2,4},{3,5},{4,6},{5,7},{6,0},{7,1},{8,10},{9,11},{10,... | collective-permute-start | bytes 393224 | tf_op jit(solution)/shard_map/ppermute | solution.py:178
  45.8 22.2 %collective-permute-start.4 = (bf16[64,1024]{1,0:T(8,128)(2,1)S(1)}, bf16[64,1024]{1,0:T(8,128)(2,1)S(1)}, u32[]{:S(2)}, u32[]{:S(2)}) collective-permute-start(bf16[64,1024]{1,0:T(8,128)(2,1)S(1)} %get-tuple-element.39), channel_id=1, source_target_pairs={{0,4},{1,5},{2,6},{3,7},{4,0},{5,1},{6,2},{7,3},{8,12},{9,13},{10,... | collective-permute-start | bytes 393224 | tf_op jit(solution)/shard_map/ppermute | solution.py:178
  58.1 9.8 %collective-permute-start.5 = (bf16[64,1024]{1,0:T(8,128)(2,1)S(1)}, bf16[64,1024]{1,0:T(8,128)(2,1)S(1)}, u32[]{:S(2)}, u32[]{:S(2)}) collective-permute-start(bf16[64,1024]{1,0:T(8,128)(2,1)S(1)} %get-tuple-element.40), channel_id=1, source_target_pairs={{0,6},{1,7},{2,0},{3,1},{4,2},{5,3},{6,4},{7,5},{8,14},{9,15},{10,... | collective-permute-start | bytes 393224 | tf_op jit(solution)/shard_map/ppermute | solution.py:178
  64.6 7.7 %collective-permute-start.11 = (bf16[64,1024]{1,0:T(8,128)(2,1)S(1)}, bf16[64,1024]{1,0:T(8,128)(2,1)S(1)}, u32[]{:S(2)}, u32[]{:S(2)}) collective-permute-start(bf16[64,1024]{1,0:T(8,128)(2,1)S(1)} %get-tuple-element.50), channel_id=1, source_target_pairs={{0,2},{1,3},{2,4},{3,5},{4,6},{5,7},{6,0},{7,1},{8,10},{9,11},{10,... | collective-permute-start | bytes 393224 | tf_op jit(solution)/shard_map/ppermute | solution.py:178
  64.7 7.6 %collective-permute-start.12 = (bf16[64,1024]{1,0:T(8,128)(2,1)S(1)}, bf16[64,1024]{1,0:T(8,128)(2,1)S(1)}, u32[]{:S(2)}, u32[]{:S(2)}) collective-permute-start(bf16[64,1024]{1,0:T(8,128)(2,1)S(1)} %get-tuple-element.51), channel_id=1, source_target_pairs={{0,4},{1,5},{2,6},{3,7},{4,0},{5,1},{6,2},{7,3},{8,12},{9,13},{10,... | collective-permute-start | bytes 393224 | tf_op jit(solution)/shard_map/ppermute | solution.py:178
  66.2 7.0 %collective-permute-start.13 = (bf16[64,1024]{1,0:T(8,128)(2,1)S(1)}, bf16[64,1024]{1,0:T(8,128)(2,1)S(1)}, u32[]{:S(2)}, u32[]{:S(2)}) collective-permute-start(bf16[64,1024]{1,0:T(8,128)(2,1)S(1)} %get-tuple-element.52), channel_id=1, source_target_pairs={{0,6},{1,7},{2,0},{3,1},{4,2},{5,3},{6,4},{7,5},{8,14},{9,15},{10,... | collective-permute-start | bytes 393224 | tf_op jit(solution)/shard_map/ppermute | solution.py:178
  68.0 5.3 %collective-permute-start.6 = (f32[32,1024]{1,0:T(8,128)S(1)}, f32[32,1024]{1,0:T(8,128)S(1)}, u32[]{:S(2)}, u32[]{:S(2)}) collective-permute-start(f32[32,1024]{1,0:T(8,128)S(1)} %get-tuple-element.42), channel_id=1, source_target_pairs={{0,1},{1,0},{2,3},{3,2},{4,5},{5,4},{6,7},{7,6},{8,9},{9,8},{10,11... | collective-permute-start | bytes 393224 | tf_op jit(solution)/shard_map/ppermute | solution.py:178
  73.2 5.0 %collective-permute-start.14 = (f32[32,1024]{1,0:T(8,128)S(1)}, f32[32,1024]{1,0:T(8,128)S(1)}, u32[]{:S(2)}, u32[]{:S(2)}) collective-permute-start(f32[32,1024]{1,0:T(8,128)S(1)} %get-tuple-element.54), channel_id=1, source_target_pairs={{0,1},{1,0},{2,3},{3,2},{4,5},{5,4},{6,7},{7,6},{8,9},{9,8},{10,11... | collective-permute-start | bytes 393224 | tf_op jit(solution)/shard_map/ppermute | solution.py:178

commit v3 on v0

v3 whole, which is shorter than its diff:
```python
import jax
import jax.numpy as jnp
from jax import lax
from jax.experimental import pallas as pl
from jax.experimental.pallas import tpu as pltpu
from jax.sharding import PartitionSpec as P

BF16, F32 = jnp.bfloat16, jnp.float32
TILE = 512
SUB = 64
VMEM = pl.BlockSpec(memory_space=pltpu.VMEM)
HBM = pl.BlockSpec(memory_space=pltpu.HBM)


def params(mib):
    return pltpu.CompilerParams(vmem_limit_bytes=mib * 1024 * 1024)


def position():
    q, r = lax.axis_index("sector"), lax.axis_index("grid")
    x, z, y = r // 8, lax.rem(r // 2, 4), lax.rem(r, 2)
    odd = lax.rem(q, 2) == 1
    return jnp.where(odd, z, x), jnp.where(odd, x, z), y, odd, q == 3


def tiles(rows, cols, step):
    high = rows // TILE

    @pl.loop(0, high * (cols // TILE))
    def _(t):
        at = pl.ds(pl.multiple_of(lax.rem(t, high) * TILE, TILE), TILE)
        step(t, at, pl.ds(pl.multiple_of((t // high) * TILE, TILE), TILE))


def transform(b, c, put, wait=None):
    def step(t, rows, cols):
        if wait is not None:
            wait(t)
        put(rows, cols, jnp.dot(b[rows, :], c[:, cols], preferred_element_type=F32).astype(BF16))

    tiles(b.shape[0], c.shape[1], step)


def spread(w, wide):
    for k in range(w.shape[0]):
        wide[k * 128 : (k + 1) * 128, :] = jnp.broadcast_to(w[k : k + 1, :], (128, 128)).T


def weighted(wide, rows, field):
    factor = jnp.concatenate([wide[rows, :]] * (field.shape[1] // 128), axis=1)
    return (factor * field.astype(F32)).astype(BF16)


def multiply(v, w, product):
    for i, half in enumerate(v):

        @pl.loop(0, w.shape[1] // TILE)
        def _(n, i=i, half=half):
            cols = pl.ds(pl.multiple_of(n * TILE, TILE), TILE)
            product[i * TILE : (i + 1) * TILE, cols] = lax.dot_general(
                half[...], w[:, cols], (((0,), (0,)), ((), ())), preferred_element_type=F32
            ).astype(BF16)


RING = (
    ((0, 0), (0, 1), (0, 2), (0, 3)),
    ((2, 0), (2, 1), (1, 2), (1, 3)),
    ((2, 2), (2, 3), (3, 0), (3, 1)),
    ((1, 0), (1, 1), (3, 2), (3, 3)),
)


def cut(products, outs):
    own, _, _, odd, _ = position()
    for out, blocks in zip(outs, RING, strict=True):
        for n, (k, second) in enumerate(blocks):
            first = lax.rem(own + k, 4)
            block = jnp.where(odd, second * 4 + first, first * 4 + second)
            rows = pl.ds(pl.multiple_of(block * SUB, SUB), SUB)
            at = 0
            for product in products:
                out[n * SUB : (n + 1) * SUB, at : at + product.shape[1]] = product[rows, :]
                at += product.shape[1]


def halves_of(v):
    return [v.at[:, pl.ds(n * TILE, TILE)] for n in range(2)]


def first_kernel(b_hbm, c_hbm, v_out, b, c_second, c, total, sems):
    deep = b.shape[1] // 2
    of_b, of_c = [], []
    for k in range(2):
        at = pl.ds(k * deep, deep)
        of_c.append(pltpu.make_async_copy(c_hbm.at[0, at, pl.ds(0, TILE)], c.at[at], sems.at[k]))
        for m in range(2):
            rows = pl.ds(m * TILE, TILE)
            of_b.append(pltpu.make_async_copy(b_hbm.at[rows, at], b.at[rows, at], sems.at[2 + 2 * k + m]))
    rest = pltpu.make_async_copy(c_hbm.at[0, :, pl.ds(TILE, TILE)], c_second, sems.at[6])
    for copy in (of_b[0], of_c[0], of_b[2], of_c[1], of_b[1], of_b[3], rest):
        copy.start()

    @pl.loop(0, 4)
    def _(t):
        for n, needed in enumerate(((of_b[0], of_c[0]), (of_b[2], of_c[1]), (of_b[1],), (of_b[3],))):

            @pl.when(t == n)
            def _():
                for copy in needed:
                    copy.wait()

        m, k = t // 2, lax.rem(t, 2)
        rows, at = pl.ds(pl.multiple_of(m * TILE, TILE), TILE), pl.ds(pl.multiple_of(k * deep, deep), deep)
        here = jnp.dot(b[rows, at], c[at, :], preferred_element_type=F32)

        @pl.when(k == 0)
        def _():
            total[...] = here

        @pl.when(k == 1)
        def _():
            v_out[rows, :] = (total[...] + here).astype(BF16)

    rest.wait()


def second_kernel(b, c, c_hbm, v_out, c1, sem):
    copy = pltpu.make_async_copy(c_hbm.at[1], c1, sem)
    copy.start()

    def put(rows, cols, values):
        v_out[rows, cols] = values

    transform(b, c, put)
    copy.wait()


def third_kernel(b, c1, v0a, v0b, weights, next_hbm, v_out, product, after_a, after_b, wide, w, sems):
    last = position()[4]
    copies = [
        pltpu.make_async_copy(next_hbm.at[:, pl.ds(n * TILE, TILE)], after, sems.at[n])
        for n, after in enumerate((after_a, after_b))
    ]

    @pl.when(last)
    def _():
        for copy in copies:
            copy.start()

    spread(weights, wide)

    def put(rows, cols, values):
        v_out[rows, cols] = values
        w[rows, cols] = weighted(wide, rows, values)

    transform(b, c1, put)
    multiply((v0a, v0b), w, product)

    @pl.when(last)
    def _():
        for copy in copies:
            copy.wait()


def weigh(field, wide, w):
    @pl.loop(0, field.shape[0] // 128)
    def _(m):
        rows = pl.ds(pl.multiple_of(m * 128, 128), 128)
        w[rows, :] = weighted(wide, rows, field[rows, :])


def following(b, after, arrived, wide, w):
    last = position()[4]

    @pl.when(last)
    def _():
        def put(rows, cols, values):
            w[rows, cols] = weighted(wide, rows, values)

        transform(b, after, put)

    @pl.when(jnp.logical_not(last))
    def _():
        weigh(arrived, wide, w)


def fourth_kernel(b, after, v1, arrived, wide, before, out0, out1, out2, out3, w, product):
    following(b, after, arrived, wide, w)
    multiply(halves_of(v1), w, product)
    cut((before, product), (out0, out1, out2, out3))


def fifth_kernel(b, after, v1, arrived, wide, out0, out1, out2, out3, w, product):
    following(b, after, arrived, wide, w)
    multiply(halves_of(v1), w, product)
    cut((product,), (out0, out1, out2, out3))


def relay(later, got_plus, got_minus, plus, minus):
    half = later.shape[0] // 2
    plus[...] = (later[:half, :].astype(F32) + got_plus[:half, :].astype(F32)).astype(BF16)
    minus[...] = (later[half:, :].astype(F32) + got_minus[:half, :].astype(F32)).astype(BF16)


def first_sum(*refs):
    (own, out1, out2, out3), total = refs[10:14], refs[14]
    at = 0
    for s in range(2):
        part, got_plus, got_minus, relayed_plus, relayed_minus = refs[5 * s : 5 * s + 5]
        half, cols = part.shape[0] // 2, slice(at, at + part.shape[1])
        at += part.shape[1]
        for rows, direct, relayed in (
            (slice(0, half), got_minus, relayed_plus),
            (slice(half, 2 * half), got_plus, relayed_minus),
        ):
            total[rows, cols] = part[rows, :].astype(F32) + direct[half:, :].astype(F32) + relayed[...].astype(F32)
    place = position()[1]
    for k, out in enumerate((own, out1, out2, out3)):
        rows = pl.ds(pl.multiple_of(lax.rem(place + k, 4) * SUB, SUB), SUB)
        out[...] = total[rows, :].astype(out.dtype)


def second_sum(own, a, b, c, kept, out):
    place, half = position()[2], SUB // 2
    for k, to in enumerate((kept, out)):
        rows = pl.ds(pl.multiple_of(lax.rem(place + k, 2) * half, half), half)
        total = own[rows, :] + a[rows, :].astype(F32) + b[rows, :].astype(F32) + c[rows, :].astype(F32)
        to[...] = total.astype(to.dtype)


def last_sum(kept, got, out):
    width = out.shape[2]
    for s in range(2):
        cols = slice(s * width, (s + 1) * width)
        out[s] = kept[:, cols] + got[:, cols].astype(F32)


def pairs_of(move):
    found = []
    for q in range(4):
        for r in range(32):
            t = move(q, r // 8, (r // 2) % 4, r % 2)
            if t is not None:
                found.append((q * 32 + r, t[0] * 32 + (t[1] % 4) * 8 + (t[2] % 4) * 2 + t[3] % 2))
    return found


def along(first, k):
    def move(q, x, z, y):
        return (q, x + k, z, y) if (q % 2 == 0) == first else (q, x, z + k, y)

    return move


def send(value, move):
    return lax.ppermute(value, ("sector", "grid"), pairs_of(move))


def per_device(coeffs, basis_values, weights, next_coeffs):
    grid_points, basis = basis_values.shape
    width = coeffs.shape[2]
    coeffs, basis_values, next_coeffs = (
        pltpu.with_memory_space_constraint(a, pltpu.HBM) for a in (coeffs, basis_values, next_coeffs)
    )
    rows_of = weights.reshape(grid_points // 128, 128)
    field = pltpu.VMEM((grid_points, width), BF16)
    half_field = pltpu.VMEM((grid_points, TILE), BF16)
    spectrum = pltpu.VMEM((basis, width), BF16)
    half_spectrum = pltpu.VMEM((basis, TILE), BF16)

    def cost(transforms, products):
        return pl.CostEstimate(
            flops=int(2 * grid_points * width * (transforms * basis + products * width)),
            bytes_accessed=int(2 * (transforms * basis * (grid_points + width) + 3 * width * width)),
            transcendentals=0,
        )

    def call(kernel, ins, outs, scratch_shapes=(), mib=12, spent=(0, 0), name=None):
        return pl.pallas_call(
            kernel,
            out_shape=outs,
            in_specs=[HBM if any(a is h for h in (coeffs, basis_values, next_coeffs)) else VMEM for a in ins],
            out_specs=[VMEM] * len(outs),
            scratch_shapes=list(scratch_shapes),
            compiler_params=params(mib),
            cost_estimate=cost(*spent),
            name=name,
        )(*ins)

    v0a, b, c_second = call(
        first_kernel,
        (basis_values, coeffs),
        [half_field, pltpu.VMEM((grid_points, basis), BF16), half_spectrum],
        [half_spectrum, pltpu.VMEM((TILE, TILE), F32), pltpu.SemaphoreType.DMA((7,))],
        spent=(0.5, 0),
        name="first_values_a",
    )
    before_last = lambda q, x, z, y: (q - 1, x, z, y) if q else None
    v0b, c1 = call(
        second_kernel,
        (b, c_second, coeffs),
        [half_field, spectrum],
        [pltpu.SemaphoreType.DMA],
        spent=(0.5, 0),
        name="first_values_b",
    )
    arrived_b = send(v0b, before_last)
    arrived_a = send(v0a, before_last)
    v1, product, after_a, after_b, wide = call(
        third_kernel,
        (b, c1, v0a, v0b, rows_of, next_coeffs),
        [field, pltpu.VMEM((width, width), BF16), half_spectrum, half_spectrum, pltpu.VMEM((grid_points, 128), F32)],
        [field, pltpu.SemaphoreType.DMA((2,))],
        mib=16,
        spent=(0, 0.01),
        name="second_values",
    )

    def parts(cols):
        return [pltpu.VMEM((width // 4, cols), BF16)] * 4

    parts0 = call(
        fourth_kernel,
        (b, after_a, v1, arrived_a, wide, product),
        parts(width + TILE),
        [half_field, pltpu.VMEM((width, TILE), BF16)],
        spent=(0, 0.01),
        name="second_intersection_a",
    )
    parts1 = call(
        fifth_kernel,
        (b, after_b, v1, arrived_b, wide),
        parts(width - TILE),
        [half_field, pltpu.VMEM((width, TILE), BF16)],
        spent=(0, 0.01),
        name="second_intersection_b",
    )

    def ring(parts):
        own, plus, minus, later = parts
        got = [send(plus, along(True, 1)), send(minus, along(True, -1))]
        outs = call(relay, (later, *got), [pltpu.VMEM((width // 8, own.shape[1]), BF16)] * 2, mib=8, name="relay")
        return [own, *got, send(outs[0], along(True, 1)), send(outs[1], along(True, -1))]

    own, *outs = call(
        first_sum,
        (*ring(parts0), *ring(parts1)),
        [pltpu.VMEM((SUB, 2 * width), F32)] + [pltpu.VMEM((SUB, 2 * width), BF16)] * 3,
        [pltpu.VMEM((width // 4, 2 * width), F32)],
        mib=8,
        name="first_sum",
    )
    got = [send(outs[k - 1], along(False, k)) for k in (2, 1, 3)]
    kept, out = call(
        second_sum,
        (own, *got),
        [pltpu.VMEM((SUB // 2, 2 * width), F32), pltpu.VMEM((SUB // 2, 2 * width), BF16)],
        mib=8,
        name="second_sum",
    )
    arrived = send(out, lambda q, x, z, y: (q, x, z, y + 1))
    (result,) = call(
        last_sum, (kept, arrived), [jax.ShapeDtypeStruct((2, SUB // 2, width), F32)], mib=8, name="last_sum"
    )
    return result


def solution(mesh):
    return jax.shard_map(
        per_device,
        mesh=mesh,
        in_specs=(P("sector", None, None), P("grid", None), P("grid"), P()),
        out_specs=P("sector", "grid", None),
        check_vma=False,
    )
```

time: 447 us -> 70.8 us (0.16)
  waiting for transfers between devices: 388 us -> 24.4 us
  matrix products: 33.2 us -> 0 us
  Pallas kernels: 0 us -> 25.3 us
  starting transfers between devices: 2.57 us -> 20.8 us
  between operations: 13.5 us -> 0.12 us
    psum x1 -> x0, waiting for transfers between devices: 381 us -> none  [per_device(): summed = lax.psum(partials, 'grid')]
    dot_general x4 -> x0, matrix products: 33.2 us -> none  [the longest x2 22.2 us: transform(): jnp.dot(basis_values, coefficient, preferred_element_type=jnp.float32)]
    pallas_call x0 -> x10, Pallas kernels: none -> 25.3 us  [call(): pl.pallas_call(kernel, out_shape=outs, in_specs=[HBM if any((a is h for h...]
    ppermute x1 -> x14, starting transfers between devices: 2.57 us -> 20.8 us  [send(): return lax.ppermute(value, ('sector', 'grid'), pairs_of(move))]
    ppermute x1 -> x14, waiting for transfers between devices: 6.41 us -> 24.4 us  [send(): return lax.ppermute(value, ('sector', 'grid'), pairs_of(move))]
  transfers between devices with their start and end apart: 2 -> 14, of which waited for: 2 -> 10; matrix products, arithmetic and copies ran while one was open for 4% -> 0% of each run, Pallas kernels for 0% -> 25%
where the time goes in v3:
time: 70.8 us; the launch traced here: 70.6 us
  Pallas kernels  25.3 us (36%)
  waiting for transfers between devices  24.4 us (34%)
  starting transfers between devices  20.8 us (29%)
    pallas_call x10, Pallas kernels, call(): pl.pallas_call(kernel, out_shape=outs, in_specs=[HBM if any((a is h for h...  25.3 us
    ppermute x14, waiting for transfers between devices, send(): return lax.ppermute(value, ('sector', 'grid'), pairs_of(move))  24.4 us
    ppermute x14, starting transfers between devices, send(): return lax.ppermute(value, ('sector', 'grid'), pairs_of(move))  20.8 us
  transfers between devices with their start and end apart: 14, of which 10 were waited for; matrix products, arithmetic and copies ran while one was open for 0% of the time, Pallas kernels for 25%

profile of v3, /device:TPU:30, one launch (start us, length us, event | category | flops | bytes accessed | tf_op | source)
XLA Modules:
  0.0 70.6 jit_solution(16725490708368116644)
XLA Ops:
  0.0 6.2 %first_values_a.1 = (bf16[1024,512]{1,0:T(8,128)(2,1)S(1)}, bf16[1024,3072]{1,0:T(8,128)(2,1)S(1)}, bf16[3072,512]{1,0:T(8,128)(2,1)S(1)}) custom-call(bf16[1024,3072]{1,0:T(8,128)(2,1)} %b_hbm.1, bf16[2,3072,1024]{2,1,0:T(8,128)(2,1)} %c_hbm.3), custom_call_target="tpu_custom_call" | custom-call | flops 3221225472 | bytes 12582912 | tf_op jit(solution)/shard_map/first_values_a/pallas_call | solution.py:279
  6.2 2.6 %collective-permute-start = (bf16[1024,512]{1,0:T(8,128)(2,1)S(1)}, bf16[1024,512]{1,0:T(8,128)(2,1)S(1)}, u32[]{:S(2)}, u32[]{:S(2)}) collective-permute-start(bf16[1024,512]{1,0:T(8,128)(2,1)S(1)} %get-tuple-element.36.v0a), channel_id=1, source_target_pairs={{32,0},{33,1},{34,2},{35,3},{36,4},{37,5},{38,6},{39,7},{40,8},{41... | collective-permute-start | bytes 3145736 | tf_op jit(solution)/shard_map/ppermute | solution.py:256
  8.8 0.0 copy-start
  8.8 3.6 %first_values_b.1 = (bf16[1024,512]{1,0:T(8,128)(2,1)S(1)}, bf16[3072,1024]{1,0:T(8,128)(2,1)S(1)}) custom-call(bf16[1024,3072]{1,0:T(8,128)(2,1)S(1)} %get-tuple-element.33.b, bf16[3072,512]{1,0:T(8,128)(2,1)S(1)} %get-tuple-element.34.c, bf16[2,3072,1024]{2,1,0:T(8,128)(2,1)} %c_hbm.3), custom_call_target="tpu_custom_call" | custom-call | flops 3221225472 | bytes 12582912 | tf_op jit(solution)/shard_map/first_values_b/pallas_call | solution.py:279
  12.4 2.6 %collective-permute-start.5 = (bf16[1024,512]{1,0:T(8,128)(2,1)S(1)}, bf16[1024,512]{1,0:T(8,128)(2,1)S(1)}, u32[]{:S(2)}, u32[]{:S(2)}) collective-permute-start(bf16[1024,512]{1,0:T(8,128)(2,1)S(1)} %get-tuple-element.37.v0b), channel_id=1, source_target_pairs={{32,0},{33,1},{34,2},{35,3},{36,4},{37,5},{38,6},{39,7},{40,8},{41... | collective-permute-start | bytes 3145736 | tf_op jit(solution)/shard_map/ppermute | solution.py:256
  15.0 0.0 copy-done
  15.0 10.5 %second_values.1 = (bf16[1024,1024]{1,0:T(8,128)(2,1)S(1)}, bf16[1024,1024]{1,0:T(8,128)(2,1)S(1)}, bf16[3072,512]{1,0:T(8,128)(2,1)S(1)}, bf16[3072,512]{1,0:T(8,128)(2,1)S(1)}, f32[1024,128]{1,0:T(8,128)S(1)}) custom-call(bf16[1024,3072]{1,0:T(8,128)(2,1)S(1)} %get-tuple-element.33.b, bf16[3072,1024]{1,0:T(8,128)(2,1)S(1)} %get-tuple-element.35.c1, ...), custom_call_target="tpu_custom_call" | custom-call | flops 21474836 | bytes 6291456 | tf_op jit(solution)/shard_map/second_values/pallas_call | solution.py:279
  25.5 0.0 collective-permute-done.arrived
  25.5 1.7 %second_intersection_a.1 = (bf16[256,1536]{1,0:T(8,128)(2,1)S(1)}, bf16[256,1536]{1,0:T(8,128)(2,1)S(1)}, bf16[256,1536]{1,0:T(8,128)(2,1)S(1)}, bf16[256,1536]{1,0:T(8,128)(2,1)S(1)}) custom-call(bf16[1024,3072]{1,0:T(8,128)(2,1)S(1)} %get-tuple-element.33.b, bf16[3072,512]{1,0:T(8,128)(2,1)S(1)} %get-tuple-element.38.after, ...), custom_call_target="tpu_custom_call" | custom-call | flops 21474836 | bytes 6291456 | tf_op jit(solution)/shard_map/second_intersection_a/pallas_call | solution.py:279
  27.2 0.5 collective-permute-start.1
  27.8 1.6 %collective-permute-start.2 = (bf16[256,1536]{1,0:T(8,128)(2,1)S(1)}, bf16[256,1536]{1,0:T(8,128)(2,1)S(1)}, u32[]{:S(2)}, u32[]{:S(2)}) collective-permute-start(bf16[256,1536]{1,0:T(8,128)(2,1)S(1)} %get-tuple-element.44), channel_id=1, source_target_pairs={{0,24},{1,25},{2,26},{3,27},{4,28},{5,29},{6,30},{7,31},{8,0},{9,1... | collective-permute-start | bytes 2359304 | tf_op jit(solution)/shard_map/ppermute | solution.py:256
  29.3 2.9 %collective-permute-done.5.arrived = bf16[1024,512]{1,0:T(8,128)(2,1)S(1)} collective-permute-done((bf16[1024,512]{1,0:T(8,128)(2,1)S(1)}, bf16[1024,512]{1,0:T(8,128)(2,1)S(1)}, u32[]{:S(2)}, u32[]{:S(2)}) %collective-permute-start.5) | collective-permute-done | bytes 1048608 | tf_op jit(solution)/shard_map/ppermute | solution.py:256
  32.3 1.6 %second_intersection_b.1 = (bf16[256,512]{1,0:T(8,128)(2,1)S(1)}, bf16[256,512]{1,0:T(8,128)(2,1)S(1)}, bf16[256,512]{1,0:T(8,128)(2,1)S(1)}, bf16[256,512]{1,0:T(8,128)(2,1)S(1)}) custom-call(bf16[1024,3072]{1,0:T(8,128)(2,1)S(1)} %get-tuple-element.33.b, bf16[3072,512]{1,0:T(8,128)(2,1)S(1)} %get-tuple-element.48.after, ...), custom_call_target="tpu_custom_call" | custom-call | flops 21474836 | bytes 6291456 | tf_op jit(solution)/shard_map/second_intersection_b/pallas_call | solution.py:279
  33.9 0.6 collective-permute-start.6
  34.4 1.5 %collective-permute-start.7 = (bf16[256,512]{1,0:T(8,128)(2,1)S(1)}, bf16[256,512]{1,0:T(8,128)(2,1)S(1)}, u32[]{:S(2)}, u32[]{:S(2)}) collective-permute-start(bf16[256,512]{1,0:T(8,128)(2,1)S(1)} %get-tuple-element.51), channel_id=1, source_target_pairs={{0,24},{1,25},{2,26},{3,27},{4,28},{5,29},{6,30},{7,31},{8,0},{9,1... | collective-permute-start | bytes 786440 | tf_op jit(solution)/shard_map/ppermute | solution.py:256
  36.0 3.3 %collective-permute-done.1.got_plus.refs_1_ = bf16[256,1536]{1,0:T(8,128)(2,1)S(1)} collective-permute-done((bf16[256,1536]{1,0:T(8,128)(2,1)S(1)}, bf16[256,1536]{1,0:T(8,128)(2,1)S(1)}, u32[]{:S(2)}, u32[]{:S(2)}) %collective-permute-start.1) | collective-permute-done | bytes 786464 | tf_op jit(solution)/shard_map/ppermute | solution.py:256
  39.3 1.7 %collective-permute-done.2.got_minus.refs_2_ = bf16[256,1536]{1,0:T(8,128)(2,1)S(1)} collective-permute-done((bf16[256,1536]{1,0:T(8,128)(2,1)S(1)}, bf16[256,1536]{1,0:T(8,128)(2,1)S(1)}, u32[]{:S(2)}, u32[]{:S(2)}) %collective-permute-start.2) | collective-permute-done | bytes 786464 | tf_op jit(solution)/shard_map/ppermute | solution.py:256
  41.0 0.2 relay.2
  41.2 0.4 collective-permute-start.3
  41.5 1.7 %collective-permute-start.4 = (bf16[128,1536]{1,0:T(8,128)(2,1)S(1)}, bf16[128,1536]{1,0:T(8,128)(2,1)S(1)}, u32[]{:S(2)}, u32[]{:S(2)}) collective-permute-start(bf16[128,1536]{1,0:T(8,128)(2,1)S(1)} %get-tuple-element.47), channel_id=1, source_target_pairs={{0,24},{1,25},{2,26},{3,27},{4,28},{5,29},{6,30},{7,31},{8,0},{9,1... | collective-permute-start | bytes 1179656 | tf_op jit(solution)/shard_map/ppermute | solution.py:256
  43.3 0.0 collective-permute-done.6.got_plus.refs_6_
  43.3 0.5 collective-permute-done.7.got_minus.refs_7_
  43.8 0.1 relay.3
  43.9 1.0 %collective-permute-start.8 = (bf16[128,512]{1,0:T(8,128)(2,1)S(1)}, bf16[128,512]{1,0:T(8,128)(2,1)S(1)}, u32[]{:S(2)}, u32[]{:S(2)}) collective-permute-start(bf16[128,512]{1,0:T(8,128)(2,1)S(1)} %get-tuple-element.53), channel_id=1, source_target_pairs={{0,8},{1,9},{2,10},{3,11},{4,12},{5,13},{6,14},{7,15},{8,16},{9,17... | collective-permute-start | bytes 393224 | tf_op jit(solution)/shard_map/ppermute | solution.py:256
  44.9 1.1 %collective-permute-start.9 = (bf16[128,512]{1,0:T(8,128)(2,1)S(1)}, bf16[128,512]{1,0:T(8,128)(2,1)S(1)}, u32[]{:S(2)}, u32[]{:S(2)}) collective-permute-start(bf16[128,512]{1,0:T(8,128)(2,1)S(1)} %get-tuple-element.54), channel_id=1, source_target_pairs={{0,24},{1,25},{2,26},{3,27},{4,28},{5,29},{6,30},{7,31},{8,0},{9,1... | collective-permute-start | bytes 393224 | tf_op jit(solution)/shard_map/ppermute | solution.py:256
  46.0 4.5 %collective-permute-done.8.refs_8_ = bf16[128,512]{1,0:T(8,128)(2,1)S(1)} collective-permute-done((bf16[128,512]{1,0:T(8,128)(2,1)S(1)}, bf16[128,512]{1,0:T(8,128)(2,1)S(1)}, u32[]{:S(2)}, u32[]{:S(2)}) %collective-permute-start.8) | collective-permute-done | bytes 131104 | tf_op jit(solution)/shard_map/ppermute | solution.py:256
  50.4 1.5 %collective-permute-done.9.refs_9_ = bf16[128,512]{1,0:T(8,128)(2,1)S(1)} collective-permute-done((bf16[128,512]{1,0:T(8,128)(2,1)S(1)}, bf16[128,512]{1,0:T(8,128)(2,1)S(1)}, u32[]{:S(2)}, u32[]{:S(2)}) %collective-permute-start.9) | collective-permute-done | bytes 131104 | tf_op jit(solution)/shard_map/ppermute | solution.py:256
  51.9 0.0 collective-permute-done.3.refs_3_
  51.9 0.0 collective-permute-done.4.refs_4_
  51.9 0.7 first_sum.1
  52.6 3.9 %collective-permute-start.10 = (bf16[64,2048]{1,0:T(8,128)(2,1)S(1)}, bf16[64,2048]{1,0:T(8,128)(2,1)S(1)}, u32[]{:S(2)}, u32[]{:S(2)}) collective-permute-start(bf16[64,2048]{1,0:T(8,128)(2,1)S(1)} %get-tuple-element.56), channel_id=1, source_target_pairs={{0,4},{1,5},{2,6},{3,7},{4,0},{5,1},{6,2},{7,3},{8,12},{9,13},{10,... | collective-permute-start | bytes 786440 | tf_op jit(solution)/shard_map/ppermute | solution.py:256
  56.6 1.0 %collective-permute-start.11 = (bf16[64,2048]{1,0:T(8,128)(2,1)S(1)}, bf16[64,2048]{1,0:T(8,128)(2,1)S(1)}, u32[]{:S(2)}, u32[]{:S(2)}) collective-permute-start(bf16[64,2048]{1,0:T(8,128)(2,1)S(1)} %get-tuple-element.57), channel_id=1, source_target_pairs={{0,2},{1,3},{2,4},{3,5},{4,6},{5,7},{6,0},{7,1},{8,10},{9,11},{10,... | collective-permute-start | bytes 786440 | tf_op jit(solution)/shard_map/ppermute | solution.py:256
  57.6 2.2 %collective-permute-start.12 = (bf16[64,2048]{1,0:T(8,128)(2,1)S(1)}, bf16[64,2048]{1,0:T(8,128)(2,1)S(1)}, u32[]{:S(2)}, u32[]{:S(2)}) collective-permute-start(bf16[64,2048]{1,0:T(8,128)(2,1)S(1)} %get-tuple-element.58), channel_id=1, source_target_pairs={{0,6},{1,7},{2,0},{3,1},{4,2},{5,3},{6,4},{7,5},{8,14},{9,15},{10,... | collective-permute-start | bytes 786440 | tf_op jit(solution)/shard_map/ppermute | solution.py:256
  59.8 1.1 %collective-permute-done.10.a = bf16[64,2048]{1,0:T(8,128)(2,1)S(1)} collective-permute-done((bf16[64,2048]{1,0:T(8,128)(2,1)S(1)}, bf16[64,2048]{1,0:T(8,128)(2,1)S(1)}, u32[]{:S(2)}, u32[]{:S(2)}) %collective-permute-start.10) | collective-permute-done | bytes 262176 | tf_op jit(solution)/shard_map/ppermute | solution.py:256
  60.9 3.2 %collective-permute-done.11.b = bf16[64,2048]{1,0:T(8,128)(2,1)S(1)} collective-permute-done((bf16[64,2048]{1,0:T(8,128)(2,1)S(1)}, bf16[64,2048]{1,0:T(8,128)(2,1)S(1)}, u32[]{:S(2)}, u32[]{:S(2)}) %collective-permute-start.11) | collective-permute-done | bytes 262176 | tf_op jit(solution)/shard_map/ppermute | solution.py:256
  64.2 0.6 collective-permute-done.12.c
  64.8 0.1 second_sum.1
  64.9 0.1 collective-permute-start.13
  65.0 5.0 %collective-permute-done.13.got = bf16[32,2048]{1,0:T(8,128)(2,1)S(1)} collective-permute-done((bf16[32,2048]{1,0:T(8,128)(2,1)S(1)}, bf16[32,2048]{1,0:T(8,128)(2,1)S(1)}, u32[]{:S(2)}, u32[]{:S(2)}) %collective-permute-start.13) | collective-permute-done | bytes 131104 | tf_op jit(solution)/shard_map/ppermute | solution.py:256
  69.9 0.7 %last_sum.1 = f32[2,32,1024]{2,1,0:T(8,128)} custom-call(f32[32,2048]{1,0:T(8,128)S(1)} %get-tuple-element.59.kept, bf16[32,2048]{1,0:T(8,128)(2,1)S(1)} %collective-permute-done.13.got), custom_call_target="tpu_custom_call" | custom-call | bytes 6291456 | tf_op jit(solution)/shard_map/last_sum/pallas_call | solution.py:279
Async XLA Ops:
  6.2 19.3 %collective-permute-start = (bf16[1024,512]{1,0:T(8,128)(2,1)S(1)}, bf16[1024,512]{1,0:T(8,128)(2,1)S(1)}, u32[]{:S(2)}, u32[]{:S(2)}) collective-permute-start(bf16[1024,512]{1,0:T(8,128)(2,1)S(1)} %get-tuple-element.36.v0a), channel_id=1, source_target_pairs={{32,0},{33,1},{34,2},{35,3},{36,4},{37,5},{38,6},{39,7},{40,8},{41... | collective-permute-start | bytes 3145736 | tf_op jit(solution)/shard_map/ppermute | solution.py:256
  8.8 6.2 %copy-start = (f32[1024]{0:T(1024)S(1)}, f32[1024]{0:T(1024)}, u32[]{:S(2)}) copy-start(f32[1024]{0:T(1024)} %param.6) | copy-start | bytes 12292
  12.4 19.9 %collective-permute-start.5 = (bf16[1024,512]{1,0:T(8,128)(2,1)S(1)}, bf16[1024,512]{1,0:T(8,128)(2,1)S(1)}, u32[]{:S(2)}, u32[]{:S(2)}) collective-permute-start(bf16[1024,512]{1,0:T(8,128)(2,1)S(1)} %get-tuple-element.37.v0b), channel_id=1, source_target_pairs={{32,0},{33,1},{34,2},{35,3},{36,4},{37,5},{38,6},{39,7},{40,8},{41... | collective-permute-start | bytes 3145736 | tf_op jit(solution)/shard_map/ppermute | solution.py:256
  27.2 12.1 %collective-permute-start.1 = (bf16[256,1536]{1,0:T(8,128)(2,1)S(1)}, bf16[256,1536]{1,0:T(8,128)(2,1)S(1)}, u32[]{:S(2)}, u32[]{:S(2)}) collective-permute-start(bf16[256,1536]{1,0:T(8,128)(2,1)S(1)} %get-tuple-element.43), channel_id=1, source_target_pairs={{0,8},{1,9},{2,10},{3,11},{4,12},{5,13},{6,14},{7,15},{8,16},{9,17... | collective-permute-start | bytes 2359304 | tf_op jit(solution)/shard_map/ppermute | solution.py:256
  27.8 13.2 %collective-permute-start.2 = (bf16[256,1536]{1,0:T(8,128)(2,1)S(1)}, bf16[256,1536]{1,0:T(8,128)(2,1)S(1)}, u32[]{:S(2)}, u32[]{:S(2)}) collective-permute-start(bf16[256,1536]{1,0:T(8,128)(2,1)S(1)} %get-tuple-element.44), channel_id=1, source_target_pairs={{0,24},{1,25},{2,26},{3,27},{4,28},{5,29},{6,30},{7,31},{8,0},{9,1... | collective-permute-start | bytes 2359304 | tf_op jit(solution)/shard_map/ppermute | solution.py:256
  33.9 9.4 %collective-permute-start.6 = (bf16[256,512]{1,0:T(8,128)(2,1)S(1)}, bf16[256,512]{1,0:T(8,128)(2,1)S(1)}, u32[]{:S(2)}, u32[]{:S(2)}) collective-permute-start(bf16[256,512]{1,0:T(8,128)(2,1)S(1)} %get-tuple-element.50), channel_id=1, source_target_pairs={{0,8},{1,9},{2,10},{3,11},{4,12},{5,13},{6,14},{7,15},{8,16},{9,17... | collective-permute-start | bytes 786440 | tf_op jit(solution)/shard_map/ppermute | solution.py:256
  34.4 9.4 %collective-permute-start.7 = (bf16[256,512]{1,0:T(8,128)(2,1)S(1)}, bf16[256,512]{1,0:T(8,128)(2,1)S(1)}, u32[]{:S(2)}, u32[]{:S(2)}) collective-permute-start(bf16[256,512]{1,0:T(8,128)(2,1)S(1)} %get-tuple-element.51), channel_id=1, source_target_pairs={{0,24},{1,25},{2,26},{3,27},{4,28},{5,29},{6,30},{7,31},{8,0},{9,1... | collective-permute-start | bytes 786440 | tf_op jit(solution)/shard_map/ppermute | solution.py:256
  41.2 10.8 %collective-permute-start.3 = (bf16[128,1536]{1,0:T(8,128)(2,1)S(1)}, bf16[128,1536]{1,0:T(8,128)(2,1)S(1)}, u32[]{:S(2)}, u32[]{:S(2)}) collective-permute-start(bf16[128,1536]{1,0:T(8,128)(2,1)S(1)} %get-tuple-element.46), channel_id=1, source_target_pairs={{0,8},{1,9},{2,10},{3,11},{4,12},{5,13},{6,14},{7,15},{8,16},{9,17... | collective-permute-start | bytes 1179656 | tf_op jit(solution)/shard_map/ppermute | solution.py:256
  41.5 10.4 %collective-permute-start.4 = (bf16[128,1536]{1,0:T(8,128)(2,1)S(1)}, bf16[128,1536]{1,0:T(8,128)(2,1)S(1)}, u32[]{:S(2)}, u32[]{:S(2)}) collective-permute-start(bf16[128,1536]{1,0:T(8,128)(2,1)S(1)} %get-tuple-element.47), channel_id=1, source_target_pairs={{0,24},{1,25},{2,26},{3,27},{4,28},{5,29},{6,30},{7,31},{8,0},{9,1... | collective-permute-start | bytes 1179656 | tf_op jit(solution)/shard_map/ppermute | solution.py:256
  43.9 6.6 %collective-permute-start.8 = (bf16[128,512]{1,0:T(8,128)(2,1)S(1)}, bf16[128,512]{1,0:T(8,128)(2,1)S(1)}, u32[]{:S(2)}, u32[]{:S(2)}) collective-permute-start(bf16[128,512]{1,0:T(8,128)(2,1)S(1)} %get-tuple-element.53), channel_id=1, source_target_pairs={{0,8},{1,9},{2,10},{3,11},{4,12},{5,13},{6,14},{7,15},{8,16},{9,17... | collective-permute-start | bytes 393224 | tf_op jit(solution)/shard_map/ppermute | solution.py:256
  44.9 7.0 %collective-permute-start.9 = (bf16[128,512]{1,0:T(8,128)(2,1)S(1)}, bf16[128,512]{1,0:T(8,128)(2,1)S(1)}, u32[]{:S(2)}, u32[]{:S(2)}) collective-permute-start(bf16[128,512]{1,0:T(8,128)(2,1)S(1)} %get-tuple-element.54), channel_id=1, source_target_pairs={{0,24},{1,25},{2,26},{3,27},{4,28},{5,29},{6,30},{7,31},{8,0},{9,1... | collective-permute-start | bytes 393224 | tf_op jit(solution)/shard_map/ppermute | solution.py:256
  52.6 8.3 %collective-permute-start.10 = (bf16[64,2048]{1,0:T(8,128)(2,1)S(1)}, bf16[64,2048]{1,0:T(8,128)(2,1)S(1)}, u32[]{:S(2)}, u32[]{:S(2)}) collective-permute-start(bf16[64,2048]{1,0:T(8,128)(2,1)S(1)} %get-tuple-element.56), channel_id=1, source_target_pairs={{0,4},{1,5},{2,6},{3,7},{4,0},{5,1},{6,2},{7,3},{8,12},{9,13},{10,... | collective-permute-start | bytes 786440 | tf_op jit(solution)/shard_map/ppermute | solution.py:256
  56.6 7.6 %collective-permute-start.11 = (bf16[64,2048]{1,0:T(8,128)(2,1)S(1)}, bf16[64,2048]{1,0:T(8,128)(2,1)S(1)}, u32[]{:S(2)}, u32[]{:S(2)}) collective-permute-start(bf16[64,2048]{1,0:T(8,128)(2,1)S(1)} %get-tuple-element.57), channel_id=1, source_target_pairs={{0,2},{1,3},{2,4},{3,5},{4,6},{5,7},{6,0},{7,1},{8,10},{9,11},{10,... | collective-permute-start | bytes 786440 | tf_op jit(solution)/shard_map/ppermute | solution.py:256
  57.6 7.2 %collective-permute-start.12 = (bf16[64,2048]{1,0:T(8,128)(2,1)S(1)}, bf16[64,2048]{1,0:T(8,128)(2,1)S(1)}, u32[]{:S(2)}, u32[]{:S(2)}) collective-permute-start(bf16[64,2048]{1,0:T(8,128)(2,1)S(1)} %get-tuple-element.58), channel_id=1, source_target_pairs={{0,6},{1,7},{2,0},{3,1},{4,2},{5,3},{6,4},{7,5},{8,14},{9,15},{10,... | collective-permute-start | bytes 786440 | tf_op jit(solution)/shard_map/ppermute | solution.py:256
  64.9 5.0 %collective-permute-start.13 = (bf16[32,2048]{1,0:T(8,128)(2,1)S(1)}, bf16[32,2048]{1,0:T(8,128)(2,1)S(1)}, u32[]{:S(2)}, u32[]{:S(2)}) collective-permute-start(bf16[32,2048]{1,0:T(8,128)(2,1)S(1)} %get-tuple-element.60), channel_id=1, source_target_pairs={{0,1},{1,0},{2,3},{3,2},{4,5},{5,4},{6,7},{7,6},{8,9},{9,8},{10,11... | collective-permute-start | bytes 393224 | tf_op jit(solution)/shard_map/ppermute | solution.py:256

commit v4 on v3

v4 whole, which is shorter than its diff:
```python
import jax
import jax.numpy as jnp
from jax import lax
from jax.experimental import pallas as pl
from jax.experimental.pallas import tpu as pltpu
from jax.sharding import PartitionSpec as P

BF16, F32 = jnp.bfloat16, jnp.float32
DEEP = 512
TILE = 256
EARLY = 256
SUB = 64
VMEM = pl.BlockSpec(memory_space=pltpu.VMEM)
HBM = pl.BlockSpec(memory_space=pltpu.HBM)


def params(mib):
    return pltpu.CompilerParams(vmem_limit_bytes=mib * 1024 * 1024)


def position():
    q, r = lax.axis_index("sector"), lax.axis_index("grid")
    x, z, y = r // 8, lax.rem(r // 2, 4), lax.rem(r, 2)
    odd = lax.rem(q, 2) == 1
    return jnp.where(odd, z, x), jnp.where(odd, x, z), y, odd, q == 3, q == 0


def tiles(cols, step):
    @pl.loop(0, cols // TILE)
    def _(t):
        step(pl.ds(pl.multiple_of(t * TILE, TILE), TILE))


def transform(b, c, put, copies=None):
    @pl.loop(0, c.shape[1] // TILE)
    def _(t):
        for n, copy in enumerate(copies or ()):

            @pl.when(t == n + 1)
            def _(copy=copy):
                copy.wait()

        cols = pl.ds(pl.multiple_of(t * TILE, TILE), TILE)
        put(cols, jnp.dot(b[...], c[:, cols], preferred_element_type=F32).astype(BF16))


def spread(w, wide):
    for k in range(w.shape[0]):
        wide[k * 128 : (k + 1) * 128, :] = jnp.broadcast_to(w[k : k + 1, :], (128, 128)).T


def weighted(wide, field):
    factor = jnp.concatenate([wide[...]] * (field.shape[1] // 128), axis=1)
    return (factor * field.astype(F32)).astype(BF16)


def multiply(v, w, product):
    def step(cols):
        at = 0
        for part in v:
            product[at : at + part.shape[1], cols] = lax.dot_general(
                part[...], w[:, cols], (((0,), (0,)), ((), ())), preferred_element_type=F32
            ).astype(BF16)
            at += part.shape[1]

    tiles(w.shape[1], step)


UNIT = 32
FORWARD = 5
RING = (
    tuple((0, n) for n in range(8)),
    tuple((2, n) for n in range(FORWARD)) + tuple((1, n) for n in range(FORWARD, 8)),
    tuple((2, n) for n in range(FORWARD, 8)) + tuple((3, n) for n in range(FORWARD)),
    tuple((1, n) for n in range(FORWARD)) + tuple((3, n) for n in range(FORWARD, 8)),
)


def cut(products, outs):
    own, _, _, odd, _, _ = position()
    for out, units in zip(outs, RING, strict=True):
        for n, (k, unit) in enumerate(units):
            first, second = lax.rem(own + k, 4), unit // 2
            block = jnp.where(odd, second * 4 + first, first * 4 + second) * 2 + unit % 2
            rows = pl.ds(pl.multiple_of(block * UNIT, UNIT), UNIT)
            at = 0
            for product in products:
                out[n * UNIT : (n + 1) * UNIT, at : at + product.shape[1]] = product[rows, :]
                at += product.shape[1]


def first_kernel(b_hbm, c_hbm, next_hbm, v_out, b, c_second, c, total, sems):
    first = position()[5]
    deep, early = b.shape[1] // 2, pl.ds(0, EARLY)
    of_b, of_c, of_next = [], [], []
    for k in range(2):
        at = pl.ds(k * deep, deep)
        of_c.append(pltpu.make_async_copy(c_hbm.at[0, at, early], c.at[at], sems.at[k]))
        of_next.append(pltpu.make_async_copy(next_hbm.at[at, early], c.at[at], sems.at[k]))
        for m in range(2):
            rows = pl.ds(m * DEEP, DEEP)
            of_b.append(pltpu.make_async_copy(b_hbm.at[rows, at], b.at[rows, at], sems.at[2 + 2 * k + m]))
    rest = pltpu.make_async_copy(c_hbm.at[0, :, pl.ds(EARLY, TILE)], c_second.at[:, pl.ds(0, TILE)], sems.at[6])
    for k in range(2):
        of_b[2 * k].start()

        @pl.when(first)
        def _():
            of_next[k].start()

        @pl.when(jnp.logical_not(first))
        def _():
            of_c[k].start()

    for copy in (of_b[1], of_b[3], rest):
        copy.start()

    @pl.loop(0, 4)
    def _(t):
        for n, needed in enumerate(((of_b[0], of_c[0]), (of_b[2], of_c[1]), (of_b[1],), (of_b[3],))):

            @pl.when(t == n)
            def _():
                for copy in needed:
                    copy.wait()

        m, k = t // 2, lax.rem(t, 2)
        rows, at = pl.ds(pl.multiple_of(m * DEEP, DEEP), DEEP), pl.ds(pl.multiple_of(k * deep, deep), deep)
        here = jnp.dot(b[rows, at], c[at, :], preferred_element_type=F32)

        @pl.when(k == 0)
        def _():
            total[...] = here

        @pl.when(k == 1)
        def _():
            v_out[rows, :] = (total[...] + here).astype(BF16)

    rest.wait()


def second_kernel(b, _, c_hbm, v_out, c_first, c1, c, sems):
    first = position()[5]
    early = pltpu.make_async_copy(c_hbm.at[0, :, pl.ds(0, EARLY)], c_first, sems.at[0])
    copy = pltpu.make_async_copy(c_hbm.at[1], c1, sems.at[1])
    copies = []
    for n in range(1, c.shape[1] // TILE):
        here, there = pl.ds(n * TILE, TILE), pl.ds(EARLY + n * TILE, TILE)
        copies.append(pltpu.make_async_copy(c_hbm.at[0, :, there], c.at[:, here], sems.at[1 + n]))
    for tile in copies:
        tile.start()
    copy.start()

    @pl.when(first)
    def _():
        early.start()

    def put(cols, values):
        v_out[:, cols] = values

    transform(b, c, put, copies)
    copy.wait()

    @pl.when(first)
    def _():
        early.wait()


def third_kernel(b, c_first, c1, v0a, v0b, weights, next_hbm, v_out, product, after, wide, va, w, sem):
    _, _, _, _, last, first = position()
    copy = pltpu.make_async_copy(next_hbm.at[:, pl.ds(EARLY, after.shape[1])], after, sem)

    @pl.when(last)
    def _():
        copy.start()

    @pl.when(first)
    def _():
        def put(cols, values):
            va[:, cols] = values

        transform(b, c_first, put)

    @pl.when(jnp.logical_not(first))
    def _():
        va[...] = v0a[...]

    spread(weights, wide)

    def put(cols, values):
        v_out[:, cols] = values
        w[:, cols] = weighted(wide, values)

    transform(b, c1, put)
    multiply((va, v0b), w, product)

    @pl.when(last)
    def _():
        copy.wait()


def weigh(field, wide, w):
    def step(cols):
        w[:, cols] = weighted(wide, field[:, cols])

    tiles(field.shape[1], step)


def fourth_kernel(v1, arrived, wide, before, out0, out1, out2, out3, w, product):
    weigh(arrived, wide, w)
    multiply((v1,), w, product)
    cut((before, product), (out0, out1, out2, out3))


def fifth_kernel(b, after, v1, arrived, wide, out0, out1, out2, out3, w, product):
    last = position()[4]

    @pl.when(last)
    def _():
        def put(cols, values):
            w[:, cols] = weighted(wide, values)

        transform(b, after, put)

    @pl.when(jnp.logical_not(last))
    def _():
        weigh(arrived, wide, w)

    multiply((v1,), w, product)
    cut((product,), (out0, out1, out2, out3))


def relay(later, got_plus, got_minus, plus, minus):
    up, down = plus.shape[0], minus.shape[0]
    plus[...] = (later[:up, :].astype(F32) + got_plus[:up, :].astype(F32)).astype(BF16)
    minus[...] = (later[up:, :].astype(F32) + got_minus[:down, :].astype(F32)).astype(BF16)


def first_sum(*refs):
    (own, out1, out2, out3), total = refs[10:14], refs[14]
    at = 0
    for s in range(2):
        part, got_plus, got_minus, relayed_plus, relayed_minus = refs[5 * s : 5 * s + 5]
        up, down, cols = relayed_plus.shape[0], relayed_minus.shape[0], slice(at, at + part.shape[1])
        at += part.shape[1]
        for rows, direct, relayed in (
            (slice(0, up), got_minus[down:, :], relayed_plus),
            (slice(up, up + down), got_plus[up:, :], relayed_minus),
        ):
            total[rows, cols] = part[rows, :].astype(F32) + direct.astype(F32) + relayed[...].astype(F32)
    place = position()[1]
    for k, out in enumerate((own, out1, out2, out3)):
        rows = pl.ds(pl.multiple_of(lax.rem(place + k, 4) * SUB, SUB), SUB)
        out[...] = total[rows, :].astype(out.dtype)


def second_sum(own, a, b, c, kept, out):
    place, half = position()[2], SUB // 2
    for k, to in enumerate((kept, out)):
        rows = pl.ds(pl.multiple_of(lax.rem(place + k, 2) * half, half), half)
        total = own[rows, :] + a[rows, :].astype(F32) + b[rows, :].astype(F32) + c[rows, :].astype(F32)
        to[...] = total.astype(to.dtype)


def last_sum(kept, got, out):
    width = out.shape[2]
    for s in range(2):
        cols = slice(s * width, (s + 1) * width)
        out[s] = kept[:, cols] + got[:, cols].astype(F32)


def pairs_of(move):
    found = []
    for q in range(4):
        for r in range(32):
            t = move(q, r // 8, (r // 2) % 4, r % 2)
            if t is not None:
                found.append((q * 32 + r, t[0] * 32 + (t[1] % 4) * 8 + (t[2] % 4) * 2 + t[3] % 2))
    return found


def along(first, k):
    def move(q, x, z, y):
        return (q, x + k, z, y) if (q % 2 == 0) == first else (q, x, z + k, y)

    return move


def send(value, move):
    return lax.ppermute(value, ("sector", "grid"), pairs_of(move))


def per_device(coeffs, basis_values, weights, next_coeffs):
    grid_points, basis = basis_values.shape
    width = coeffs.shape[2]
    coeffs, basis_values, next_coeffs = (
        pltpu.with_memory_space_constraint(a, pltpu.HBM) for a in (coeffs, basis_values, next_coeffs)
    )
    rows_of = weights.reshape(grid_points // 128, 128)
    late = width - EARLY
    field = pltpu.VMEM((grid_points, width), BF16)
    early_field, late_field = (pltpu.VMEM((grid_points, n), BF16) for n in (EARLY, late))
    spectrum = pltpu.VMEM((basis, width), BF16)
    early_spectrum, late_spectrum = (pltpu.VMEM((basis, n), BF16) for n in (EARLY, late))
    factors = pltpu.VMEM((grid_points, 128), F32)

    def cost(transforms, products):
        return pl.CostEstimate(
            flops=int(2 * grid_points * width * (transforms * basis + products * width)),
            bytes_accessed=int(2 * (transforms * basis * (grid_points + width) + 3 * width * width)),
            transcendentals=0,
        )

    def call(kernel, ins, outs, scratch_shapes=(), mib=12, spent=(0, 0), name=None, aliases=None):
        return pl.pallas_call(
            kernel,
            out_shape=outs,
            in_specs=[HBM if any(a is h for h in (coeffs, basis_values, next_coeffs)) else VMEM for a in ins],
            out_specs=[VMEM] * len(outs),
            scratch_shapes=list(scratch_shapes),
            compiler_params=params(mib),
            cost_estimate=cost(*spent),
            input_output_aliases=aliases or {},
            name=name,
        )(*ins)

    v0a, b, c_second = call(
        first_kernel,
        (basis_values, coeffs, next_coeffs),
        [early_field, pltpu.VMEM((grid_points, basis), BF16), late_spectrum],
        [early_spectrum, pltpu.VMEM((DEEP, EARLY), F32), pltpu.SemaphoreType.DMA((7,))],
        spent=(0.5, 0),
        name="first_values_a",
    )
    v0b, c_first, c1, _ = call(
        second_kernel,
        (b, c_second, coeffs),
        [late_field, early_spectrum, spectrum, late_spectrum],
        [pltpu.SemaphoreType.DMA((1 + late // TILE,))],
        aliases={1: 3},
        spent=(0.5, 0),
        name="first_values_b",
    )
    arrived_b = send(v0b, lambda q, x, z, y: (q - 1, x, z, y) if q else None)
    arrived_a = send(v0a, lambda q, x, z, y: ((q - 1) % 4, x, z, y))
    v1, product, after, wide = call(
        third_kernel,
        (b, c_first, c1, v0a, v0b, rows_of, next_coeffs),
        [field, pltpu.VMEM((width, width), BF16), late_spectrum, factors],
        [early_field, field, pltpu.SemaphoreType.DMA],
        mib=16,
        spent=(0, 0.01),
        name="second_values",
    )

    def parts(cols):
        return [pltpu.VMEM((width // 4, cols), BF16)] * 4

    parts0 = call(
        fourth_kernel,
        (v1, arrived_a, wide, product),
        parts(width + EARLY),
        [early_field, pltpu.VMEM((width, EARLY), BF16)],
        spent=(2, 2),
        name="second_intersection_a",
    )
    parts1 = call(
        fifth_kernel,
        (b, after, v1, arrived_b, wide),
        parts(late),
        [late_field, pltpu.VMEM((width, late), BF16)],
        spent=(0, 0.01),
        name="second_intersection_b",
    )

    def ring(parts):
        own, plus, minus, later = parts
        got = [send(plus, along(True, 1)), send(minus, along(True, -1))]
        outs = call(
            relay,
            (later, *got),
            [pltpu.VMEM((n * UNIT, own.shape[1]), BF16) for n in (FORWARD, 8 - FORWARD)],
            mib=8,
            name="relay",
        )
        return [own, *got, send(outs[0], along(True, 1)), send(outs[1], along(True, -1))]

    own, *outs = call(
        first_sum,
        (*ring(parts0), *ring(parts1)),
        [pltpu.VMEM((SUB, 2 * width), F32)] + [pltpu.VMEM((SUB, 2 * width), BF16)] * 3,
        [pltpu.VMEM((width // 4, 2 * width), F32)],
        mib=8,
        name="first_sum",
    )
    got = [send(outs[k - 1], along(False, k)) for k in (2, 1, 3)]
    kept, out = call(
        second_sum,
        (own, *got),
        [pltpu.VMEM((SUB // 2, 2 * width), F32), pltpu.VMEM((SUB // 2, 2 * width), BF16)],
        mib=8,
        name="second_sum",
    )
    arrived = send(out, lambda q, x, z, y: (q, x, z, y + 1))
    (result,) = call(
        last_sum, (kept, arrived), [jax.ShapeDtypeStruct((2, SUB // 2, width), F32)], mib=8, name="last_sum"
    )
    return result


def solution(mesh):
    return jax.shard_map(
        per_device,
        mesh=mesh,
        in_specs=(P("sector", None, None), P("grid", None), P("grid"), P()),
        out_specs=P("sector", "grid", None),
        check_vma=False,
    )
```

time: 70.8 us -> 70.1 us (level); the launches traced: 70.6 us -> 68.9 us
  starting transfers between devices: 20.8 us -> 19 us
    ppermute x14, starting transfers between devices: 20.8 us -> 19 us  [send(): return lax.ppermute(value, ('sector', 'grid'), pairs_of(move))]
  transfers between devices with their start and end apart: 14 -> 14, of which waited for: 10 -> 11; matrix products, arithmetic and copies ran while one was open for 0% -> 0% of each run, Pallas kernels for 25% -> 29%
where the time goes in v4:
time: 70.1 us; the launch traced here: 68.9 us
  Pallas kernels  25.9 us (37%)
  waiting for transfers between devices  23.9 us (34%)
  starting transfers between devices  19 us (27%)
    pallas_call x10, Pallas kernels, call(): pl.pallas_call(kernel, out_shape=outs, in_specs=[HBM if any((a is h for h...  25.9 us
    ppermute x14, waiting for transfers between devices, send(): return lax.ppermute(value, ('sector', 'grid'), pairs_of(move))  23.9 us
    ppermute x14, starting transfers between devices, send(): return lax.ppermute(value, ('sector', 'grid'), pairs_of(move))  19 us
  transfers between devices with their start and end apart: 14, of which 11 were waited for; matrix products, arithmetic and copies ran while one was open for 0% of the time, Pallas kernels for 29%

profile of v4, /device:TPU:30, one launch (start us, length us, event | category | flops | bytes accessed | tf_op | source)
XLA Modules:
  0.0 68.9 jit_solution(4611439679399329921)
XLA Ops:
  0.0 4.3 %first_values_a.1 = (bf16[1024,256]{1,0:T(8,128)(2,1)S(1)}, bf16[1024,3072]{1,0:T(8,128)(2,1)S(1)}, bf16[3072,768]{1,0:T(8,128)(2,1)S(1)}) custom-call(bf16[1024,3072]{1,0:T(8,128)(2,1)} %b_hbm.1, bf16[2,3072,1024]{2,1,0:T(8,128)(2,1)} %c_hbm.3, bf16[3072,1024]{1,0:T(8,128)(2,1)} %next_hbm.3), custom_call_target="tpu_custom_call" | custom-call | flops 3221225472 | bytes 12582912 | tf_op jit(solution)/shard_map/first_values_a/pallas_call | solution.py:315
  4.3 0.7 %collective-permute-start = (bf16[1024,256]{1,0:T(8,128)(2,1)S(1)}, bf16[1024,256]{1,0:T(8,128)(2,1)S(1)}, u32[]{:S(2)}, u32[]{:S(2)}) collective-permute-start(bf16[1024,256]{1,0:T(8,128)(2,1)S(1)} %get-tuple-element.37.v0a), channel_id=1, source_target_pairs={{0,96},{1,97},{2,98},{3,99},{4,100},{5,101},{6,102},{7,103},{8,104... | collective-permute-start | bytes 1572872 | tf_op jit(solution)/shard_map/ppermute | solution.py:290
  5.0 0.0 copy-start
  5.0 5.4 %first_values_b.1 = (bf16[1024,768]{1,0:T(8,128)(2,1)S(1)}, bf16[3072,256]{1,0:T(8,128)(2,1)S(1)}, bf16[3072,1024]{1,0:T(8,128)(2,1)S(1)}, bf16[3072,768]{1,0:T(8,128)(2,1)S(1)}) custom-call(bf16[1024,3072]{1,0:T(8,128)(2,1)S(1)} %get-tuple-element.33.b, bf16[3072,768]{1,0:T(8,128)(2,1)S(1)} %get-tuple-element.34._, ...), custom_call_target="tpu_custom_call", output_to_operand_aliasing={{3}: (1, {})} | custom-call | flops 3221225472 | bytes 12582912 | tf_op jit(solution)/shard_map/first_values_b/pallas_call | solution.py:315
  10.4 2.6 %collective-permute-start.5 = (bf16[1024,768]{1,0:T(8,128)(2,1)S(1)}, bf16[1024,768]{1,0:T(8,128)(2,1)S(1)}, u32[]{:S(2)}, u32[]{:S(2)}) collective-permute-start(bf16[1024,768]{1,0:T(8,128)(2,1)S(1)} %get-tuple-element.38.v0b), channel_id=1, source_target_pairs={{32,0},{33,1},{34,2},{35,3},{36,4},{37,5},{38,6},{39,7},{40,8},{41... | collective-permute-start | bytes 4718600 | tf_op jit(solution)/shard_map/ppermute | solution.py:290
  13.0 0.0 copy-done
  13.0 10.6 %second_values.1 = (bf16[1024,1024]{1,0:T(8,128)(2,1)S(1)}, bf16[1024,1024]{1,0:T(8,128)(2,1)S(1)}, bf16[3072,768]{1,0:T(8,128)(2,1)S(1)}, f32[1024,128]{1,0:T(8,128)S(1)}) custom-call(bf16[1024,3072]{1,0:T(8,128)(2,1)S(1)} %get-tuple-element.33.b, bf16[3072,256]{1,0:T(8,128)(2,1)S(1)} %get-tuple-element.35.c_first, ...), custom_call_target="tpu_custom_call" | custom-call | flops 21474836 | bytes 6291456 | tf_op jit(solution)/shard_map/second_values/pallas_call | solution.py:315
  23.7 0.0 collective-permute-done.arrived
  23.7 1.0 %second_intersection_a.1 = (bf16[256,1280]{1,0:T(8,128)(2,1)S(1)}, bf16[256,1280]{1,0:T(8,128)(2,1)S(1)}, bf16[256,1280]{1,0:T(8,128)(2,1)S(1)}, bf16[256,1280]{1,0:T(8,128)(2,1)S(1)}) custom-call(bf16[1024,1024]{1,0:T(8,128)(2,1)S(1)} %get-tuple-element.39.v1, bf16[1024,256]{1,0:T(8,128)(2,1)S(1)} %collective-permute-done.arrived, ...), custom_call_target="tpu_custom_call" | custom-call | flops 17179869184 | bytes 31457280 | tf_op jit(solution)/shard_map/second_intersection_a/pallas_call | solution.py:315
  24.7 0.5 collective-permute-start.1
  25.2 1.5 %collective-permute-start.2 = (bf16[256,1280]{1,0:T(8,128)(2,1)S(1)}, bf16[256,1280]{1,0:T(8,128)(2,1)S(1)}, u32[]{:S(2)}, u32[]{:S(2)}) collective-permute-start(bf16[256,1280]{1,0:T(8,128)(2,1)S(1)} %get-tuple-element.44), channel_id=1, source_target_pairs={{0,24},{1,25},{2,26},{3,27},{4,28},{5,29},{6,30},{7,31},{8,0},{9,1... | collective-permute-start | bytes 1966088 | tf_op jit(solution)/shard_map/ppermute | solution.py:290
  26.8 4.2 %collective-permute-done.5.arrived = bf16[1024,768]{1,0:T(8,128)(2,1)S(1)} collective-permute-done((bf16[1024,768]{1,0:T(8,128)(2,1)S(1)}, bf16[1024,768]{1,0:T(8,128)(2,1)S(1)}, u32[]{:S(2)}, u32[]{:S(2)}) %collective-permute-start.5) | collective-permute-done | bytes 1572896 | tf_op jit(solution)/shard_map/ppermute | solution.py:290
  30.9 2.9 %second_intersection_b.1 = (bf16[256,768]{1,0:T(8,128)(2,1)S(1)}, bf16[256,768]{1,0:T(8,128)(2,1)S(1)}, bf16[256,768]{1,0:T(8,128)(2,1)S(1)}, bf16[256,768]{1,0:T(8,128)(2,1)S(1)}) custom-call(bf16[1024,3072]{1,0:T(8,128)(2,1)S(1)} %get-tuple-element.33.b, bf16[3072,768]{1,0:T(8,128)(2,1)S(1)} %get-tuple-element.48.after, ...), custom_call_target="tpu_custom_call" | custom-call | flops 21474836 | bytes 6291456 | tf_op jit(solution)/shard_map/second_intersection_b/pallas_call | solution.py:315
  33.8 0.5 collective-permute-start.6
  34.4 1.5 %collective-permute-start.7 = (bf16[256,768]{1,0:T(8,128)(2,1)S(1)}, bf16[256,768]{1,0:T(8,128)(2,1)S(1)}, u32[]{:S(2)}, u32[]{:S(2)}) collective-permute-start(bf16[256,768]{1,0:T(8,128)(2,1)S(1)} %get-tuple-element.51), channel_id=1, source_target_pairs={{0,24},{1,25},{2,26},{3,27},{4,28},{5,29},{6,30},{7,31},{8,0},{9,1... | collective-permute-start | bytes 1179656 | tf_op jit(solution)/shard_map/ppermute | solution.py:290
  35.9 0.0 collective-permute-done.1.got_plus.refs_1_
  35.9 1.1 %collective-permute-done.2.got_minus.refs_2_ = bf16[256,1280]{1,0:T(8,128)(2,1)S(1)} collective-permute-done((bf16[256,1280]{1,0:T(8,128)(2,1)S(1)}, bf16[256,1280]{1,0:T(8,128)(2,1)S(1)}, u32[]{:S(2)}, u32[]{:S(2)}) %collective-permute-start.2) | collective-permute-done | bytes 655392 | tf_op jit(solution)/shard_map/ppermute | solution.py:290
  37.0 0.2 relay.2
  37.2 0.7 %collective-permute-start.3 = (bf16[160,1280]{1,0:T(8,128)(2,1)S(1)}, bf16[160,1280]{1,0:T(8,128)(2,1)S(1)}, u32[]{:S(2)}, u32[]{:S(2)}) collective-permute-start(bf16[160,1280]{1,0:T(8,128)(2,1)S(1)} %get-tuple-element.46), channel_id=1, source_target_pairs={{0,8},{1,9},{2,10},{3,11},{4,12},{5,13},{6,14},{7,15},{8,16},{9,17... | collective-permute-start | bytes 1228808 | tf_op jit(solution)/shard_map/ppermute | solution.py:290
  37.9 1.4 %collective-permute-start.4 = (bf16[96,1280]{1,0:T(8,128)(2,1)S(1)}, bf16[96,1280]{1,0:T(8,128)(2,1)S(1)}, u32[]{:S(2)}, u32[]{:S(2)}) collective-permute-start(bf16[96,1280]{1,0:T(8,128)(2,1)S(1)} %get-tuple-element.47), channel_id=1, source_target_pairs={{0,24},{1,25},{2,26},{3,27},{4,28},{5,29},{6,30},{7,31},{8,0},{9,1... | collective-permute-start | bytes 737288 | tf_op jit(solution)/shard_map/ppermute | solution.py:290
  39.2 2.4 %collective-permute-done.6.got_plus.refs_6_ = bf16[256,768]{1,0:T(8,128)(2,1)S(1)} collective-permute-done((bf16[256,768]{1,0:T(8,128)(2,1)S(1)}, bf16[256,768]{1,0:T(8,128)(2,1)S(1)}, u32[]{:S(2)}, u32[]{:S(2)}) %collective-permute-start.6) | collective-permute-done | bytes 393248 | tf_op jit(solution)/shard_map/ppermute | solution.py:290
  41.7 1.7 %collective-permute-done.7.got_minus.refs_7_ = bf16[256,768]{1,0:T(8,128)(2,1)S(1)} collective-permute-done((bf16[256,768]{1,0:T(8,128)(2,1)S(1)}, bf16[256,768]{1,0:T(8,128)(2,1)S(1)}, u32[]{:S(2)}, u32[]{:S(2)}) %collective-permute-start.7) | collective-permute-done | bytes 393248 | tf_op jit(solution)/shard_map/ppermute | solution.py:290
  43.4 0.1 relay.3
  43.5 0.3 collective-permute-start.8
  43.8 1.7 %collective-permute-start.9 = (bf16[96,768]{1,0:T(8,128)(2,1)S(1)}, bf16[96,768]{1,0:T(8,128)(2,1)S(1)}, u32[]{:S(2)}, u32[]{:S(2)}) collective-permute-start(bf16[96,768]{1,0:T(8,128)(2,1)S(1)} %get-tuple-element.54), channel_id=1, source_target_pairs={{0,24},{1,25},{2,26},{3,27},{4,28},{5,29},{6,30},{7,31},{8,0},{9,1... | collective-permute-start | bytes 442376 | tf_op jit(solution)/shard_map/ppermute | solution.py:290
  45.6 0.4 collective-permute-done.4.refs_4_
  46.0 0.1 collective-permute-done.3.refs_3_
  46.1 4.1 %collective-permute-done.9.refs_9_ = bf16[96,768]{1,0:T(8,128)(2,1)S(1)} collective-permute-done((bf16[96,768]{1,0:T(8,128)(2,1)S(1)}, bf16[96,768]{1,0:T(8,128)(2,1)S(1)}, u32[]{:S(2)}, u32[]{:S(2)}) %collective-permute-start.9) | collective-permute-done | bytes 147488 | tf_op jit(solution)/shard_map/ppermute | solution.py:290
  50.2 0.0 collective-permute-done.8.refs_8_
  50.2 0.7 first_sum.1
  50.9 4.0 %collective-permute-start.10 = (bf16[64,2048]{1,0:T(8,128)(2,1)S(1)}, bf16[64,2048]{1,0:T(8,128)(2,1)S(1)}, u32[]{:S(2)}, u32[]{:S(2)}) collective-permute-start(bf16[64,2048]{1,0:T(8,128)(2,1)S(1)} %get-tuple-element.56), channel_id=1, source_target_pairs={{0,4},{1,5},{2,6},{3,7},{4,0},{5,1},{6,2},{7,3},{8,12},{9,13},{10,... | collective-permute-start | bytes 786440 | tf_op jit(solution)/shard_map/ppermute | solution.py:290
  54.8 1.0 %collective-permute-start.11 = (bf16[64,2048]{1,0:T(8,128)(2,1)S(1)}, bf16[64,2048]{1,0:T(8,128)(2,1)S(1)}, u32[]{:S(2)}, u32[]{:S(2)}) collective-permute-start(bf16[64,2048]{1,0:T(8,128)(2,1)S(1)} %get-tuple-element.57), channel_id=1, source_target_pairs={{0,2},{1,3},{2,4},{3,5},{4,6},{5,7},{6,0},{7,1},{8,10},{9,11},{10,... | collective-permute-start | bytes 786440 | tf_op jit(solution)/shard_map/ppermute | solution.py:290
  55.8 2.2 %collective-permute-start.12 = (bf16[64,2048]{1,0:T(8,128)(2,1)S(1)}, bf16[64,2048]{1,0:T(8,128)(2,1)S(1)}, u32[]{:S(2)}, u32[]{:S(2)}) collective-permute-start(bf16[64,2048]{1,0:T(8,128)(2,1)S(1)} %get-tuple-element.58), channel_id=1, source_target_pairs={{0,6},{1,7},{2,0},{3,1},{4,2},{5,3},{6,4},{7,5},{8,14},{9,15},{10,... | collective-permute-start | bytes 786440 | tf_op jit(solution)/shard_map/ppermute | solution.py:290
  58.1 1.1 %collective-permute-done.10.a = bf16[64,2048]{1,0:T(8,128)(2,1)S(1)} collective-permute-done((bf16[64,2048]{1,0:T(8,128)(2,1)S(1)}, bf16[64,2048]{1,0:T(8,128)(2,1)S(1)}, u32[]{:S(2)}, u32[]{:S(2)}) %collective-permute-start.10) | collective-permute-done | bytes 262176 | tf_op jit(solution)/shard_map/ppermute | solution.py:290
  59.2 3.2 %collective-permute-done.11.b = bf16[64,2048]{1,0:T(8,128)(2,1)S(1)} collective-permute-done((bf16[64,2048]{1,0:T(8,128)(2,1)S(1)}, bf16[64,2048]{1,0:T(8,128)(2,1)S(1)}, u32[]{:S(2)}, u32[]{:S(2)}) %collective-permute-start.11) | collective-permute-done | bytes 262176 | tf_op jit(solution)/shard_map/ppermute | solution.py:290
  62.4 0.6 collective-permute-done.12.c
  63.0 0.1 second_sum.1
  63.1 0.1 collective-permute-start.13
  63.2 5.0 %collective-permute-done.13.got = bf16[32,2048]{1,0:T(8,128)(2,1)S(1)} collective-permute-done((bf16[32,2048]{1,0:T(8,128)(2,1)S(1)}, bf16[32,2048]{1,0:T(8,128)(2,1)S(1)}, u32[]{:S(2)}, u32[]{:S(2)}) %collective-permute-start.13) | collective-permute-done | bytes 131104 | tf_op jit(solution)/shard_map/ppermute | solution.py:290
  68.2 0.7 %last_sum.1 = f32[2,32,1024]{2,1,0:T(8,128)} custom-call(f32[32,2048]{1,0:T(8,128)S(1)} %get-tuple-element.59.kept, bf16[32,2048]{1,0:T(8,128)(2,1)S(1)} %collective-permute-done.13.got), custom_call_target="tpu_custom_call" | custom-call | bytes 6291456 | tf_op jit(solution)/shard_map/last_sum/pallas_call | solution.py:315
Async XLA Ops:
  4.3 19.4 %collective-permute-start = (bf16[1024,256]{1,0:T(8,128)(2,1)S(1)}, bf16[1024,256]{1,0:T(8,128)(2,1)S(1)}, u32[]{:S(2)}, u32[]{:S(2)}) collective-permute-start(bf16[1024,256]{1,0:T(8,128)(2,1)S(1)} %get-tuple-element.37.v0a), channel_id=1, source_target_pairs={{0,96},{1,97},{2,98},{3,99},{4,100},{5,101},{6,102},{7,103},{8,104... | collective-permute-start | bytes 1572872 | tf_op jit(solution)/shard_map/ppermute | solution.py:290
  5.0 8.0 %copy-start = (f32[1024]{0:T(1024)S(1)}, f32[1024]{0:T(1024)}, u32[]{:S(2)}) copy-start(f32[1024]{0:T(1024)} %param.6) | copy-start | bytes 12292
  10.4 20.5 %collective-permute-start.5 = (bf16[1024,768]{1,0:T(8,128)(2,1)S(1)}, bf16[1024,768]{1,0:T(8,128)(2,1)S(1)}, u32[]{:S(2)}, u32[]{:S(2)}) collective-permute-start(bf16[1024,768]{1,0:T(8,128)(2,1)S(1)} %get-tuple-element.38.v0b), channel_id=1, source_target_pairs={{32,0},{33,1},{34,2},{35,3},{36,4},{37,5},{38,6},{39,7},{40,8},{41... | collective-permute-start | bytes 4718600 | tf_op jit(solution)/shard_map/ppermute | solution.py:290
  24.7 11.3 %collective-permute-start.1 = (bf16[256,1280]{1,0:T(8,128)(2,1)S(1)}, bf16[256,1280]{1,0:T(8,128)(2,1)S(1)}, u32[]{:S(2)}, u32[]{:S(2)}) collective-permute-start(bf16[256,1280]{1,0:T(8,128)(2,1)S(1)} %get-tuple-element.43), channel_id=1, source_target_pairs={{0,8},{1,9},{2,10},{3,11},{4,12},{5,13},{6,14},{7,15},{8,16},{9,17... | collective-permute-start | bytes 1966088 | tf_op jit(solution)/shard_map/ppermute | solution.py:290
  25.2 11.8 %collective-permute-start.2 = (bf16[256,1280]{1,0:T(8,128)(2,1)S(1)}, bf16[256,1280]{1,0:T(8,128)(2,1)S(1)}, u32[]{:S(2)}, u32[]{:S(2)}) collective-permute-start(bf16[256,1280]{1,0:T(8,128)(2,1)S(1)} %get-tuple-element.44), channel_id=1, source_target_pairs={{0,24},{1,25},{2,26},{3,27},{4,28},{5,29},{6,30},{7,31},{8,0},{9,1... | collective-permute-start | bytes 1966088 | tf_op jit(solution)/shard_map/ppermute | solution.py:290
  33.8 7.8 %collective-permute-start.6 = (bf16[256,768]{1,0:T(8,128)(2,1)S(1)}, bf16[256,768]{1,0:T(8,128)(2,1)S(1)}, u32[]{:S(2)}, u32[]{:S(2)}) collective-permute-start(bf16[256,768]{1,0:T(8,128)(2,1)S(1)} %get-tuple-element.50), channel_id=1, source_target_pairs={{0,8},{1,9},{2,10},{3,11},{4,12},{5,13},{6,14},{7,15},{8,16},{9,17... | collective-permute-start | bytes 1179656 | tf_op jit(solution)/shard_map/ppermute | solution.py:290
  34.4 9.0 %collective-permute-start.7 = (bf16[256,768]{1,0:T(8,128)(2,1)S(1)}, bf16[256,768]{1,0:T(8,128)(2,1)S(1)}, u32[]{:S(2)}, u32[]{:S(2)}) collective-permute-start(bf16[256,768]{1,0:T(8,128)(2,1)S(1)} %get-tuple-element.51), channel_id=1, source_target_pairs={{0,24},{1,25},{2,26},{3,27},{4,28},{5,29},{6,30},{7,31},{8,0},{9,1... | collective-permute-start | bytes 1179656 | tf_op jit(solution)/shard_map/ppermute | solution.py:290
  37.2 8.9 %collective-permute-start.3 = (bf16[160,1280]{1,0:T(8,128)(2,1)S(1)}, bf16[160,1280]{1,0:T(8,128)(2,1)S(1)}, u32[]{:S(2)}, u32[]{:S(2)}) collective-permute-start(bf16[160,1280]{1,0:T(8,128)(2,1)S(1)} %get-tuple-element.46), channel_id=1, source_target_pairs={{0,8},{1,9},{2,10},{3,11},{4,12},{5,13},{6,14},{7,15},{8,16},{9,17... | collective-permute-start | bytes 1228808 | tf_op jit(solution)/shard_map/ppermute | solution.py:290
  37.9 8.2 %collective-permute-start.4 = (bf16[96,1280]{1,0:T(8,128)(2,1)S(1)}, bf16[96,1280]{1,0:T(8,128)(2,1)S(1)}, u32[]{:S(2)}, u32[]{:S(2)}) collective-permute-start(bf16[96,1280]{1,0:T(8,128)(2,1)S(1)} %get-tuple-element.47), channel_id=1, source_target_pairs={{0,24},{1,25},{2,26},{3,27},{4,28},{5,29},{6,30},{7,31},{8,0},{9,1... | collective-permute-start | bytes 737288 | tf_op jit(solution)/shard_map/ppermute | solution.py:290
  43.5 6.7 %collective-permute-start.8 = (bf16[160,768]{1,0:T(8,128)(2,1)S(1)}, bf16[160,768]{1,0:T(8,128)(2,1)S(1)}, u32[]{:S(2)}, u32[]{:S(2)}) collective-permute-start(bf16[160,768]{1,0:T(8,128)(2,1)S(1)} %get-tuple-element.53), channel_id=1, source_target_pairs={{0,8},{1,9},{2,10},{3,11},{4,12},{5,13},{6,14},{7,15},{8,16},{9,17... | collective-permute-start | bytes 737288 | tf_op jit(solution)/shard_map/ppermute | solution.py:290
  43.8 6.4 %collective-permute-start.9 = (bf16[96,768]{1,0:T(8,128)(2,1)S(1)}, bf16[96,768]{1,0:T(8,128)(2,1)S(1)}, u32[]{:S(2)}, u32[]{:S(2)}) collective-permute-start(bf16[96,768]{1,0:T(8,128)(2,1)S(1)} %get-tuple-element.54), channel_id=1, source_target_pairs={{0,24},{1,25},{2,26},{3,27},{4,28},{5,29},{6,30},{7,31},{8,0},{9,1... | collective-permute-start | bytes 442376 | tf_op jit(solution)/shard_map/ppermute | solution.py:290
  50.9 8.3 %collective-permute-start.10 = (bf16[64,2048]{1,0:T(8,128)(2,1)S(1)}, bf16[64,2048]{1,0:T(8,128)(2,1)S(1)}, u32[]{:S(2)}, u32[]{:S(2)}) collective-permute-start(bf16[64,2048]{1,0:T(8,128)(2,1)S(1)} %get-tuple-element.56), channel_id=1, source_target_pairs={{0,4},{1,5},{2,6},{3,7},{4,0},{5,1},{6,2},{7,3},{8,12},{9,13},{10,... | collective-permute-start | bytes 786440 | tf_op jit(solution)/shard_map/ppermute | solution.py:290
  54.8 7.6 %collective-permute-start.11 = (bf16[64,2048]{1,0:T(8,128)(2,1)S(1)}, bf16[64,2048]{1,0:T(8,128)(2,1)S(1)}, u32[]{:S(2)}, u32[]{:S(2)}) collective-permute-start(bf16[64,2048]{1,0:T(8,128)(2,1)S(1)} %get-tuple-element.57), channel_id=1, source_target_pairs={{0,2},{1,3},{2,4},{3,5},{4,6},{5,7},{6,0},{7,1},{8,10},{9,11},{10,... | collective-permute-start | bytes 786440 | tf_op jit(solution)/shard_map/ppermute | solution.py:290
  55.8 7.2 %collective-permute-start.12 = (bf16[64,2048]{1,0:T(8,128)(2,1)S(1)}, bf16[64,2048]{1,0:T(8,128)(2,1)S(1)}, u32[]{:S(2)}, u32[]{:S(2)}) collective-permute-start(bf16[64,2048]{1,0:T(8,128)(2,1)S(1)} %get-tuple-element.58), channel_id=1, source_target_pairs={{0,6},{1,7},{2,0},{3,1},{4,2},{5,3},{6,4},{7,5},{8,14},{9,15},{10,... | collective-permute-start | bytes 786440 | tf_op jit(solution)/shard_map/ppermute | solution.py:290
  63.1 5.0 %collective-permute-start.13 = (bf16[32,2048]{1,0:T(8,128)(2,1)S(1)}, bf16[32,2048]{1,0:T(8,128)(2,1)S(1)}, u32[]{:S(2)}, u32[]{:S(2)}) collective-permute-start(bf16[32,2048]{1,0:T(8,128)(2,1)S(1)} %get-tuple-element.60), channel_id=1, source_target_pairs={{0,1},{1,0},{2,3},{3,2},{4,5},{5,4},{6,7},{7,6},{8,9},{9,8},{10,11... | collective-permute-start | bytes 393224 | tf_op jit(solution)/shard_map/ppermute | solution.py:290

commit v5 on v4

--- a/solution.py
+++ b/solution.py
@@ -89,7 +89,7 @@
                 at += product.shape[1]
 
 
-def first_kernel(b_hbm, c_hbm, next_hbm, v_out, b, c_second, c, total, sems):
+def first_kernel(b_hbm, c_hbm, next_hbm, weights_hbm, v_out, b, c_second, wide, c, total, weights, sems):
     first = position()[5]
     deep, early = b.shape[1] // 2, pl.ds(0, EARLY)
     of_b, of_c, of_next = [], [], []
@@ -101,6 +101,8 @@
             rows = pl.ds(m * DEEP, DEEP)
             of_b.append(pltpu.make_async_copy(b_hbm.at[rows, at], b.at[rows, at], sems.at[2 + 2 * k + m]))
     rest = pltpu.make_async_copy(c_hbm.at[0, :, pl.ds(EARLY, TILE)], c_second.at[:, pl.ds(0, TILE)], sems.at[6])
+    of_weights = pltpu.make_async_copy(weights_hbm, weights, sems.at[7])
+    of_weights.start()
     for k in range(2):
         of_b[2 * k].start()
 
@@ -114,6 +116,8 @@
 
     for copy in (of_b[1], of_b[3], rest):
         copy.start()
+    of_weights.wait()
+    spread(weights, wide)
 
     @pl.loop(0, 4)
     def _(t):
@@ -166,7 +170,7 @@
         early.wait()
 
 
-def third_kernel(b, c_first, c1, v0a, v0b, weights, next_hbm, v_out, product, after, wide, va, w, sem):
+def third_kernel(b, c_first, c1, v0a, v0b, wide, next_hbm, v_out, product, after, va, w, sem):
     _, _, _, _, last, first = position()
     copy = pltpu.make_async_copy(next_hbm.at[:, pl.ds(EARLY, after.shape[1])], after, sem)
 
@@ -184,8 +188,6 @@
     @pl.when(jnp.logical_not(first))
     def _():
         va[...] = v0a[...]
-
-    spread(weights, wide)
 
     def put(cols, values):
         v_out[:, cols] = values
@@ -236,22 +238,25 @@
     minus[...] = (later[up:, :].astype(F32) + got_minus[:down, :].astype(F32)).astype(BF16)
 
 
-def first_sum(*refs):
-    (own, out1, out2, out3), total = refs[10:14], refs[14]
-    at = 0
-    for s in range(2):
-        part, got_plus, got_minus, relayed_plus, relayed_minus = refs[5 * s : 5 * s + 5]
-        up, down, cols = relayed_plus.shape[0], relayed_minus.shape[0], slice(at, at + part.shape[1])
-        at += part.shape[1]
-        for rows, direct, relayed in (
-            (slice(0, up), got_minus[down:, :], relayed_plus),
-            (slice(up, up + down), got_plus[up:, :], relayed_minus),
-        ):
-            total[rows, cols] = part[rows, :].astype(F32) + direct.astype(F32) + relayed[...].astype(F32)
+def first_sum(part, got_plus, got_minus, relayed_plus, relayed_minus, outs, at, total):
+    up, down = relayed_plus.shape[0], relayed_minus.shape[0]
+    for rows, direct, relayed in (
+        (slice(0, up), got_minus[down:, :], relayed_plus),
+        (slice(up, up + down), got_plus[up:, :], relayed_minus),
+    ):
+        total[rows, :] = part[rows, :].astype(F32) + direct.astype(F32) + relayed[...].astype(F32)
     place = position()[1]
-    for k, out in enumerate((own, out1, out2, out3)):
+    for k, out in enumerate(outs):
         rows = pl.ds(pl.multiple_of(lax.rem(place + k, 4) * SUB, SUB), SUB)
-        out[...] = total[rows, :].astype(out.dtype)
+        out[:, at : at + total.shape[1]] = total[rows, :].astype(out.dtype)
+
+
+def first_sum_a(*refs):
+    first_sum(*refs[:5], refs[5:9], 0, refs[9])
+
+
+def first_sum_b(*refs):
+    first_sum(*refs[:5], refs[9:13], refs[9].shape[1] - refs[13].shape[1], refs[13])
 
 
 def second_sum(own, a, b, c, kept, out):
@@ -296,7 +301,7 @@
     coeffs, basis_values, next_coeffs = (
         pltpu.with_memory_space_constraint(a, pltpu.HBM) for a in (coeffs, basis_values, next_coeffs)
     )
-    rows_of = weights.reshape(grid_points // 128, 128)
+    rows_of = pltpu.with_memory_space_constraint(weights.reshape(grid_points // 128, 128), pltpu.HBM)
     late = width - EARLY
     field = pltpu.VMEM((grid_points, width), BF16)
     early_field, late_field = (pltpu.VMEM((grid_points, n), BF16) for n in (EARLY, late))
@@ -315,7 +320,7 @@
         return pl.pallas_call(
             kernel,
             out_shape=outs,
-            in_specs=[HBM if any(a is h for h in (coeffs, basis_values, next_coeffs)) else VMEM for a in ins],
+            in_specs=[HBM if any(a is h for h in (coeffs, basis_values, next_coeffs, rows_of)) else VMEM for a in ins],
             out_specs=[VMEM] * len(outs),
             scratch_shapes=list(scratch_shapes),
             compiler_params=params(mib),
@@ -324,11 +329,16 @@
             name=name,
         )(*ins)
 
-    v0a, b, c_second = call(
+    v0a, b, c_second, wide = call(
         first_kernel,
-        (basis_values, coeffs, next_coeffs),
-        [early_field, pltpu.VMEM((grid_points, basis), BF16), late_spectrum],
-        [early_spectrum, pltpu.VMEM((DEEP, EARLY), F32), pltpu.SemaphoreType.DMA((7,))],
+        (basis_values, coeffs, next_coeffs, rows_of),
+        [early_field, pltpu.VMEM((grid_points, basis), BF16), late_spectrum, factors],
+        [
+            early_spectrum,
+            pltpu.VMEM((DEEP, EARLY), F32),
+            pltpu.VMEM((grid_points // 128, 128), F32),
+            pltpu.SemaphoreType.DMA((8,)),
+        ],
         spent=(0.5, 0),
         name="first_values_a",
     )
@@ -343,10 +353,10 @@
     )
     arrived_b = send(v0b, lambda q, x, z, y: (q - 1, x, z, y) if q else None)
     arrived_a = send(v0a, lambda q, x, z, y: ((q - 1) % 4, x, z, y))
-    v1, product, after, wide = call(
+    v1, product, after = call(
         third_kernel,
-        (b, c_first, c1, v0a, v0b, rows_of, next_coeffs),
-        [field, pltpu.VMEM((width, width), BF16), late_spectrum, factors],
+        (b, c_first, c1, v0a, v0b, wide, next_coeffs),
+        [field, pltpu.VMEM((width, width), BF16), late_spectrum],
         [early_field, field, pltpu.SemaphoreType.DMA],
         mib=16,
         spent=(0, 0.01),
@@ -385,13 +395,18 @@
         )
         return [own, *got, send(outs[0], along(True, 1)), send(outs[1], along(True, -1))]
 
+    blocks = [pltpu.VMEM((SUB, 2 * width), F32)] + [pltpu.VMEM((SUB, 2 * width), BF16)] * 3
+    rings = ring(parts0), ring(parts1)
+    totals = [[pltpu.VMEM((width // 4, arrays[0].shape[1]), F32)] for arrays in rings]
+    begun = call(first_sum_a, rings[0], blocks, totals[0], mib=8, name="first_sum_a")
     own, *outs = call(
-        first_sum,
-        (*ring(parts0), *ring(parts1)),
-        [pltpu.VMEM((SUB, 2 * width), F32)] + [pltpu.VMEM((SUB, 2 * width), BF16)] * 3,
-        [pltpu.VMEM((width // 4, 2 * width), F32)],
+        first_sum_b,
+        (*rings[1], *begun),
+        blocks,
+        totals[1],
         mib=8,
-        name="first_sum",
+        name="first_sum_b",
+        aliases={5 + n: n for n in range(4)},
     )
     got = [send(outs[k - 1], along(False, k)) for k in (2, 1, 3)]
     kept, out = call(

time: 70.1 us -> 69.5 us (level)
    pallas_call x10 -> x11, Pallas kernels: 25.9 us -> 25.6 us  [call(): pl.pallas_call(kernel, out_shape=outs, in_specs=[HBM if any((a is h for h...]
  transfers between devices with their start and end apart: 14 -> 14, of which waited for: 11 -> 11; matrix products, arithmetic and copies ran while one was open for 0% -> 0% of each run, Pallas kernels for 29% -> 30%
where the time goes in v5:
time: 69.5 us; the launch traced here: 68.4 us
  Pallas kernels  25.6 us (37%)
  waiting for transfers between devices  23.7 us (34%)
  starting transfers between devices  19 us (27%)
    pallas_call x11, Pallas kernels, call(): pl.pallas_call(kernel, out_shape=outs, in_specs=[HBM if any((a is h for h...  25.6 us
    ppermute x14, waiting for transfers between devices, send(): return lax.ppermute(value, ('sector', 'grid'), pairs_of(move))  23.7 us
    ppermute x14, starting transfers between devices, send(): return lax.ppermute(value, ('sector', 'grid'), pairs_of(move))  19 us
  transfers between devices with their start and end apart: 14, of which 11 were waited for; matrix products, arithmetic and copies ran while one was open for 0% of the time, Pallas kernels for 30%

profile of v5, /device:TPU:30, one launch (start us, length us, event | category | flops | bytes accessed | tf_op | source)
XLA Modules:
  0.0 68.4 jit_solution(15953712918687112627)
XLA Ops:
  0.0 4.3 %first_values_a.1 = (bf16[1024,256]{1,0:T(8,128)(2,1)S(1)}, bf16[1024,3072]{1,0:T(8,128)(2,1)S(1)}, bf16[3072,768]{1,0:T(8,128)(2,1)S(1)}, f32[1024,128]{1,0:T(8,128)S(1)}) custom-call(bf16[1024,3072]{1,0:T(8,128)(2,1)} %b_hbm.1, bf16[2,3072,1024]{2,1,0:T(8,128)(2,1)} %c_hbm.3, bf16[3072,1024]{1,0:T(8,128)(2,1)} %next_hbm.3, f32[8,128]{1,0:T(8,128)} %bitcast.1), custom_call_target="tpu_custom_call" | custom-call | flops 3221225472 | bytes 12582912 | tf_op jit(solution)/shard_map/first_values_a/pallas_call | solution.py:320
  4.3 0.7 %collective-permute-start.5 = (bf16[1024,256]{1,0:T(8,128)(2,1)S(1)}, bf16[1024,256]{1,0:T(8,128)(2,1)S(1)}, u32[]{:S(2)}, u32[]{:S(2)}) collective-permute-start(bf16[1024,256]{1,0:T(8,128)(2,1)S(1)} %get-tuple-element.41.v0a), channel_id=1, source_target_pairs={{0,96},{1,97},{2,98},{3,99},{4,100},{5,101},{6,102},{7,103},{8,104... | collective-permute-start | bytes 1572872 | tf_op jit(solution)/shard_map/ppermute | solution.py:295
  5.0 5.4 %first_values_b.1 = (bf16[1024,768]{1,0:T(8,128)(2,1)S(1)}, bf16[3072,256]{1,0:T(8,128)(2,1)S(1)}, bf16[3072,1024]{1,0:T(8,128)(2,1)S(1)}, bf16[3072,768]{1,0:T(8,128)(2,1)S(1)}) custom-call(bf16[1024,3072]{1,0:T(8,128)(2,1)S(1)} %get-tuple-element.37.b, bf16[3072,768]{1,0:T(8,128)(2,1)S(1)} %get-tuple-element.38._, ...), custom_call_target="tpu_custom_call", output_to_operand_aliasing={{3}: (1, {})} | custom-call | flops 3221225472 | bytes 12582912 | tf_op jit(solution)/shard_map/first_values_b/pallas_call | solution.py:320
  10.5 2.6 %collective-permute-start = (bf16[1024,768]{1,0:T(8,128)(2,1)S(1)}, bf16[1024,768]{1,0:T(8,128)(2,1)S(1)}, u32[]{:S(2)}, u32[]{:S(2)}) collective-permute-start(bf16[1024,768]{1,0:T(8,128)(2,1)S(1)} %get-tuple-element.42.v0b), channel_id=1, source_target_pairs={{32,0},{33,1},{34,2},{35,3},{36,4},{37,5},{38,6},{39,7},{40,8},{41... | collective-permute-start | bytes 4718600 | tf_op jit(solution)/shard_map/ppermute | solution.py:295
  13.1 10.4 %second_values.1 = (bf16[1024,1024]{1,0:T(8,128)(2,1)S(1)}, bf16[1024,1024]{1,0:T(8,128)(2,1)S(1)}, bf16[3072,768]{1,0:T(8,128)(2,1)S(1)}) custom-call(bf16[1024,3072]{1,0:T(8,128)(2,1)S(1)} %get-tuple-element.37.b, bf16[3072,256]{1,0:T(8,128)(2,1)S(1)} %get-tuple-element.39.c_first, bf16[3072,1024]{1,0:T(8,128)(2,1)S(1)} %get-tuple-element.40.c1, ...), custom_call_target="tpu_custom_call" | custom-call | flops 21474836 | bytes 6291456 | tf_op jit(solution)/shard_map/second_values/pallas_call | solution.py:320
  23.4 0.0 collective-permute-done.5.arrived
  23.4 0.9 %second_intersection_a.1 = (bf16[256,1280]{1,0:T(8,128)(2,1)S(1)}, bf16[256,1280]{1,0:T(8,128)(2,1)S(1)}, bf16[256,1280]{1,0:T(8,128)(2,1)S(1)}, bf16[256,1280]{1,0:T(8,128)(2,1)S(1)}) custom-call(bf16[1024,1024]{1,0:T(8,128)(2,1)S(1)} %get-tuple-element.45.v1, bf16[1024,256]{1,0:T(8,128)(2,1)S(1)} %collective-permute-done.5.arrived, ...), custom_call_target="tpu_custom_call" | custom-call | flops 17179869184 | bytes 31457280 | tf_op jit(solution)/shard_map/second_intersection_a/pallas_call | solution.py:320
  24.4 0.5 collective-permute-start.6
  24.9 1.5 %collective-permute-start.7 = (bf16[256,1280]{1,0:T(8,128)(2,1)S(1)}, bf16[256,1280]{1,0:T(8,128)(2,1)S(1)}, u32[]{:S(2)}, u32[]{:S(2)}) collective-permute-start(bf16[256,1280]{1,0:T(8,128)(2,1)S(1)} %get-tuple-element.55), channel_id=1, source_target_pairs={{0,24},{1,25},{2,26},{3,27},{4,28},{5,29},{6,30},{7,31},{8,0},{9,1... | collective-permute-start | bytes 1966088 | tf_op jit(solution)/shard_map/ppermute | solution.py:295
  26.5 4.5 %collective-permute-done.arrived = bf16[1024,768]{1,0:T(8,128)(2,1)S(1)} collective-permute-done((bf16[1024,768]{1,0:T(8,128)(2,1)S(1)}, bf16[1024,768]{1,0:T(8,128)(2,1)S(1)}, u32[]{:S(2)}, u32[]{:S(2)}) %collective-permute-start) | collective-permute-done | bytes 1572896 | tf_op jit(solution)/shard_map/ppermute | solution.py:295
  31.0 2.8 %second_intersection_b.1 = (bf16[256,768]{1,0:T(8,128)(2,1)S(1)}, bf16[256,768]{1,0:T(8,128)(2,1)S(1)}, bf16[256,768]{1,0:T(8,128)(2,1)S(1)}, bf16[256,768]{1,0:T(8,128)(2,1)S(1)}) custom-call(bf16[1024,3072]{1,0:T(8,128)(2,1)S(1)} %get-tuple-element.37.b, bf16[3072,768]{1,0:T(8,128)(2,1)S(1)} %get-tuple-element.44.after, ...), custom_call_target="tpu_custom_call" | custom-call | flops 21474836 | bytes 6291456 | tf_op jit(solution)/shard_map/second_intersection_b/pallas_call | solution.py:320
  33.8 0.5 collective-permute-start.1
  34.4 1.5 %collective-permute-start.2 = (bf16[256,768]{1,0:T(8,128)(2,1)S(1)}, bf16[256,768]{1,0:T(8,128)(2,1)S(1)}, u32[]{:S(2)}, u32[]{:S(2)}) collective-permute-start(bf16[256,768]{1,0:T(8,128)(2,1)S(1)} %get-tuple-element.48), channel_id=1, source_target_pairs={{0,24},{1,25},{2,26},{3,27},{4,28},{5,29},{6,30},{7,31},{8,0},{9,1... | collective-permute-start | bytes 1179656 | tf_op jit(solution)/shard_map/ppermute | solution.py:295
  35.9 0.0 collective-permute-done.6.got_plus.refs_1_
  35.9 0.8 %collective-permute-done.7.got_minus.refs_2_ = bf16[256,1280]{1,0:T(8,128)(2,1)S(1)} collective-permute-done((bf16[256,1280]{1,0:T(8,128)(2,1)S(1)}, bf16[256,1280]{1,0:T(8,128)(2,1)S(1)}, u32[]{:S(2)}, u32[]{:S(2)}) %collective-permute-start.7) | collective-permute-done | bytes 655392 | tf_op jit(solution)/shard_map/ppermute | solution.py:295
  36.7 0.2 relay.3
  36.9 0.9 %collective-permute-start.8 = (bf16[160,1280]{1,0:T(8,128)(2,1)S(1)}, bf16[160,1280]{1,0:T(8,128)(2,1)S(1)}, u32[]{:S(2)}, u32[]{:S(2)}) collective-permute-start(bf16[160,1280]{1,0:T(8,128)(2,1)S(1)} %get-tuple-element.57), channel_id=1, source_target_pairs={{0,8},{1,9},{2,10},{3,11},{4,12},{5,13},{6,14},{7,15},{8,16},{9,17... | collective-permute-start | bytes 1228808 | tf_op jit(solution)/shard_map/ppermute | solution.py:295
  37.8 1.2 %collective-permute-start.9 = (bf16[96,1280]{1,0:T(8,128)(2,1)S(1)}, bf16[96,1280]{1,0:T(8,128)(2,1)S(1)}, u32[]{:S(2)}, u32[]{:S(2)}) collective-permute-start(bf16[96,1280]{1,0:T(8,128)(2,1)S(1)} %get-tuple-element.58), channel_id=1, source_target_pairs={{0,24},{1,25},{2,26},{3,27},{4,28},{5,29},{6,30},{7,31},{8,0},{9,1... | collective-permute-start | bytes 737288 | tf_op jit(solution)/shard_map/ppermute | solution.py:295
  39.0 2.7 %collective-permute-done.1.got_plus.refs_1_ = bf16[256,768]{1,0:T(8,128)(2,1)S(1)} collective-permute-done((bf16[256,768]{1,0:T(8,128)(2,1)S(1)}, bf16[256,768]{1,0:T(8,128)(2,1)S(1)}, u32[]{:S(2)}, u32[]{:S(2)}) %collective-permute-start.1) | collective-permute-done | bytes 393248 | tf_op jit(solution)/shard_map/ppermute | solution.py:295
  41.7 1.7 %collective-permute-done.2.got_minus.refs_2_ = bf16[256,768]{1,0:T(8,128)(2,1)S(1)} collective-permute-done((bf16[256,768]{1,0:T(8,128)(2,1)S(1)}, bf16[256,768]{1,0:T(8,128)(2,1)S(1)}, u32[]{:S(2)}, u32[]{:S(2)}) %collective-permute-start.2) | collective-permute-done | bytes 393248 | tf_op jit(solution)/shard_map/ppermute | solution.py:295
  43.3 0.1 relay.2
  43.4 0.4 collective-permute-start.3
  43.8 1.7 %collective-permute-start.4 = (bf16[96,768]{1,0:T(8,128)(2,1)S(1)}, bf16[96,768]{1,0:T(8,128)(2,1)S(1)}, u32[]{:S(2)}, u32[]{:S(2)}) collective-permute-start(bf16[96,768]{1,0:T(8,128)(2,1)S(1)} %get-tuple-element.51), channel_id=1, source_target_pairs={{0,24},{1,25},{2,26},{3,27},{4,28},{5,29},{6,30},{7,31},{8,0},{9,1... | collective-permute-start | bytes 442376 | tf_op jit(solution)/shard_map/ppermute | solution.py:295
  45.5 0.4 collective-permute-done.9.refs_4_
  46.0 0.1 collective-permute-done.8.refs_3_
  46.0 0.4 first_sum_a.1
  46.5 3.7 %collective-permute-done.4.refs_4_ = bf16[96,768]{1,0:T(8,128)(2,1)S(1)} collective-permute-done((bf16[96,768]{1,0:T(8,128)(2,1)S(1)}, bf16[96,768]{1,0:T(8,128)(2,1)S(1)}, u32[]{:S(2)}, u32[]{:S(2)}) %collective-permute-start.4) | collective-permute-done | bytes 147488 | tf_op jit(solution)/shard_map/ppermute | solution.py:295
  50.1 0.0 collective-permute-done.3.refs_3_
  50.1 0.2 first_sum_b.1
  50.4 4.0 %collective-permute-start.10 = (bf16[64,2048]{1,0:T(8,128)(2,1)S(1)}, bf16[64,2048]{1,0:T(8,128)(2,1)S(1)}, u32[]{:S(2)}, u32[]{:S(2)}) collective-permute-start(bf16[64,2048]{1,0:T(8,128)(2,1)S(1)} %get-tuple-element.64), channel_id=1, source_target_pairs={{0,4},{1,5},{2,6},{3,7},{4,0},{5,1},{6,2},{7,3},{8,12},{9,13},{10,... | collective-permute-start | bytes 786440 | tf_op jit(solution)/shard_map/ppermute | solution.py:295
  54.4 1.0 %collective-permute-start.11 = (bf16[64,2048]{1,0:T(8,128)(2,1)S(1)}, bf16[64,2048]{1,0:T(8,128)(2,1)S(1)}, u32[]{:S(2)}, u32[]{:S(2)}) collective-permute-start(bf16[64,2048]{1,0:T(8,128)(2,1)S(1)} %get-tuple-element.65), channel_id=1, source_target_pairs={{0,2},{1,3},{2,4},{3,5},{4,6},{5,7},{6,0},{7,1},{8,10},{9,11},{10,... | collective-permute-start | bytes 786440 | tf_op jit(solution)/shard_map/ppermute | solution.py:295
  55.4 2.2 %collective-permute-start.12 = (bf16[64,2048]{1,0:T(8,128)(2,1)S(1)}, bf16[64,2048]{1,0:T(8,128)(2,1)S(1)}, u32[]{:S(2)}, u32[]{:S(2)}) collective-permute-start(bf16[64,2048]{1,0:T(8,128)(2,1)S(1)} %get-tuple-element.66), channel_id=1, source_target_pairs={{0,6},{1,7},{2,0},{3,1},{4,2},{5,3},{6,4},{7,5},{8,14},{9,15},{10,... | collective-permute-start | bytes 786440 | tf_op jit(solution)/shard_map/ppermute | solution.py:295
  57.6 1.1 %collective-permute-done.10.a = bf16[64,2048]{1,0:T(8,128)(2,1)S(1)} collective-permute-done((bf16[64,2048]{1,0:T(8,128)(2,1)S(1)}, bf16[64,2048]{1,0:T(8,128)(2,1)S(1)}, u32[]{:S(2)}, u32[]{:S(2)}) %collective-permute-start.10) | collective-permute-done | bytes 262176 | tf_op jit(solution)/shard_map/ppermute | solution.py:295
  58.7 3.2 %collective-permute-done.11.b = bf16[64,2048]{1,0:T(8,128)(2,1)S(1)} collective-permute-done((bf16[64,2048]{1,0:T(8,128)(2,1)S(1)}, bf16[64,2048]{1,0:T(8,128)(2,1)S(1)}, u32[]{:S(2)}, u32[]{:S(2)}) %collective-permute-start.11) | collective-permute-done | bytes 262176 | tf_op jit(solution)/shard_map/ppermute | solution.py:295
  61.9 0.6 collective-permute-done.12.c
  62.5 0.1 second_sum.1
  62.6 0.1 collective-permute-start.13
  62.7 5.0 %collective-permute-done.13.got = bf16[32,2048]{1,0:T(8,128)(2,1)S(1)} collective-permute-done((bf16[32,2048]{1,0:T(8,128)(2,1)S(1)}, bf16[32,2048]{1,0:T(8,128)(2,1)S(1)}, u32[]{:S(2)}, u32[]{:S(2)}) %collective-permute-start.13) | collective-permute-done | bytes 131104 | tf_op jit(solution)/shard_map/ppermute | solution.py:295
  67.7 0.7 %last_sum.1 = f32[2,32,1024]{2,1,0:T(8,128)} custom-call(f32[32,2048]{1,0:T(8,128)S(1)} %get-tuple-element.67.kept, bf16[32,2048]{1,0:T(8,128)(2,1)S(1)} %collective-permute-done.13.got), custom_call_target="tpu_custom_call" | custom-call | bytes 6291456 | tf_op jit(solution)/shard_map/last_sum/pallas_call | solution.py:320
Async XLA Ops:
  4.3 19.2 %collective-permute-start.5 = (bf16[1024,256]{1,0:T(8,128)(2,1)S(1)}, bf16[1024,256]{1,0:T(8,128)(2,1)S(1)}, u32[]{:S(2)}, u32[]{:S(2)}) collective-permute-start(bf16[1024,256]{1,0:T(8,128)(2,1)S(1)} %get-tuple-element.41.v0a), channel_id=1, source_target_pairs={{0,96},{1,97},{2,98},{3,99},{4,100},{5,101},{6,102},{7,103},{8,104... | collective-permute-start | bytes 1572872 | tf_op jit(solution)/shard_map/ppermute | solution.py:295
  10.5 20.5 %collective-permute-start = (bf16[1024,768]{1,0:T(8,128)(2,1)S(1)}, bf16[1024,768]{1,0:T(8,128)(2,1)S(1)}, u32[]{:S(2)}, u32[]{:S(2)}) collective-permute-start(bf16[1024,768]{1,0:T(8,128)(2,1)S(1)} %get-tuple-element.42.v0b), channel_id=1, source_target_pairs={{32,0},{33,1},{34,2},{35,3},{36,4},{37,5},{38,6},{39,7},{40,8},{41... | collective-permute-start | bytes 4718600 | tf_op jit(solution)/shard_map/ppermute | solution.py:295
  24.4 11.5 %collective-permute-start.6 = (bf16[256,1280]{1,0:T(8,128)(2,1)S(1)}, bf16[256,1280]{1,0:T(8,128)(2,1)S(1)}, u32[]{:S(2)}, u32[]{:S(2)}) collective-permute-start(bf16[256,1280]{1,0:T(8,128)(2,1)S(1)} %get-tuple-element.54), channel_id=1, source_target_pairs={{0,8},{1,9},{2,10},{3,11},{4,12},{5,13},{6,14},{7,15},{8,16},{9,17... | collective-permute-start | bytes 1966088 | tf_op jit(solution)/shard_map/ppermute | solution.py:295
  24.9 11.8 %collective-permute-start.7 = (bf16[256,1280]{1,0:T(8,128)(2,1)S(1)}, bf16[256,1280]{1,0:T(8,128)(2,1)S(1)}, u32[]{:S(2)}, u32[]{:S(2)}) collective-permute-start(bf16[256,1280]{1,0:T(8,128)(2,1)S(1)} %get-tuple-element.55), channel_id=1, source_target_pairs={{0,24},{1,25},{2,26},{3,27},{4,28},{5,29},{6,30},{7,31},{8,0},{9,1... | collective-permute-start | bytes 1966088 | tf_op jit(solution)/shard_map/ppermute | solution.py:295
  33.8 7.8 %collective-permute-start.1 = (bf16[256,768]{1,0:T(8,128)(2,1)S(1)}, bf16[256,768]{1,0:T(8,128)(2,1)S(1)}, u32[]{:S(2)}, u32[]{:S(2)}) collective-permute-start(bf16[256,768]{1,0:T(8,128)(2,1)S(1)} %get-tuple-element.47), channel_id=1, source_target_pairs={{0,8},{1,9},{2,10},{3,11},{4,12},{5,13},{6,14},{7,15},{8,16},{9,17... | collective-permute-start | bytes 1179656 | tf_op jit(solution)/shard_map/ppermute | solution.py:295
  34.4 9.0 %collective-permute-start.2 = (bf16[256,768]{1,0:T(8,128)(2,1)S(1)}, bf16[256,768]{1,0:T(8,128)(2,1)S(1)}, u32[]{:S(2)}, u32[]{:S(2)}) collective-permute-start(bf16[256,768]{1,0:T(8,128)(2,1)S(1)} %get-tuple-element.48), channel_id=1, source_target_pairs={{0,24},{1,25},{2,26},{3,27},{4,28},{5,29},{6,30},{7,31},{8,0},{9,1... | collective-permute-start | bytes 1179656 | tf_op jit(solution)/shard_map/ppermute | solution.py:295
  36.9 9.1 %collective-permute-start.8 = (bf16[160,1280]{1,0:T(8,128)(2,1)S(1)}, bf16[160,1280]{1,0:T(8,128)(2,1)S(1)}, u32[]{:S(2)}, u32[]{:S(2)}) collective-permute-start(bf16[160,1280]{1,0:T(8,128)(2,1)S(1)} %get-tuple-element.57), channel_id=1, source_target_pairs={{0,8},{1,9},{2,10},{3,11},{4,12},{5,13},{6,14},{7,15},{8,16},{9,17... | collective-permute-start | bytes 1228808 | tf_op jit(solution)/shard_map/ppermute | solution.py:295
  37.8 8.2 %collective-permute-start.9 = (bf16[96,1280]{1,0:T(8,128)(2,1)S(1)}, bf16[96,1280]{1,0:T(8,128)(2,1)S(1)}, u32[]{:S(2)}, u32[]{:S(2)}) collective-permute-start(bf16[96,1280]{1,0:T(8,128)(2,1)S(1)} %get-tuple-element.58), channel_id=1, source_target_pairs={{0,24},{1,25},{2,26},{3,27},{4,28},{5,29},{6,30},{7,31},{8,0},{9,1... | collective-permute-start | bytes 737288 | tf_op jit(solution)/shard_map/ppermute | solution.py:295
  43.4 6.7 %collective-permute-start.3 = (bf16[160,768]{1,0:T(8,128)(2,1)S(1)}, bf16[160,768]{1,0:T(8,128)(2,1)S(1)}, u32[]{:S(2)}, u32[]{:S(2)}) collective-permute-start(bf16[160,768]{1,0:T(8,128)(2,1)S(1)} %get-tuple-element.50), channel_id=1, source_target_pairs={{0,8},{1,9},{2,10},{3,11},{4,12},{5,13},{6,14},{7,15},{8,16},{9,17... | collective-permute-start | bytes 737288 | tf_op jit(solution)/shard_map/ppermute | solution.py:295
  43.8 6.4 %collective-permute-start.4 = (bf16[96,768]{1,0:T(8,128)(2,1)S(1)}, bf16[96,768]{1,0:T(8,128)(2,1)S(1)}, u32[]{:S(2)}, u32[]{:S(2)}) collective-permute-start(bf16[96,768]{1,0:T(8,128)(2,1)S(1)} %get-tuple-element.51), channel_id=1, source_target_pairs={{0,24},{1,25},{2,26},{3,27},{4,28},{5,29},{6,30},{7,31},{8,0},{9,1... | collective-permute-start | bytes 442376 | tf_op jit(solution)/shard_map/ppermute | solution.py:295
  50.4 8.3 %collective-permute-start.10 = (bf16[64,2048]{1,0:T(8,128)(2,1)S(1)}, bf16[64,2048]{1,0:T(8,128)(2,1)S(1)}, u32[]{:S(2)}, u32[]{:S(2)}) collective-permute-start(bf16[64,2048]{1,0:T(8,128)(2,1)S(1)} %get-tuple-element.64), channel_id=1, source_target_pairs={{0,4},{1,5},{2,6},{3,7},{4,0},{5,1},{6,2},{7,3},{8,12},{9,13},{10,... | collective-permute-start | bytes 786440 | tf_op jit(solution)/shard_map/ppermute | solution.py:295
  54.4 7.6 %collective-permute-start.11 = (bf16[64,2048]{1,0:T(8,128)(2,1)S(1)}, bf16[64,2048]{1,0:T(8,128)(2,1)S(1)}, u32[]{:S(2)}, u32[]{:S(2)}) collective-permute-start(bf16[64,2048]{1,0:T(8,128)(2,1)S(1)} %get-tuple-element.65), channel_id=1, source_target_pairs={{0,2},{1,3},{2,4},{3,5},{4,6},{5,7},{6,0},{7,1},{8,10},{9,11},{10,... | collective-permute-start | bytes 786440 | tf_op jit(solution)/shard_map/ppermute | solution.py:295
  55.4 7.2 %collective-permute-start.12 = (bf16[64,2048]{1,0:T(8,128)(2,1)S(1)}, bf16[64,2048]{1,0:T(8,128)(2,1)S(1)}, u32[]{:S(2)}, u32[]{:S(2)}) collective-permute-start(bf16[64,2048]{1,0:T(8,128)(2,1)S(1)} %get-tuple-element.66), channel_id=1, source_target_pairs={{0,6},{1,7},{2,0},{3,1},{4,2},{5,3},{6,4},{7,5},{8,14},{9,15},{10,... | collective-permute-start | bytes 786440 | tf_op jit(solution)/shard_map/ppermute | solution.py:295
  62.6 5.0 %collective-permute-start.13 = (bf16[32,2048]{1,0:T(8,128)(2,1)S(1)}, bf16[32,2048]{1,0:T(8,128)(2,1)S(1)}, u32[]{:S(2)}, u32[]{:S(2)}) collective-permute-start(bf16[32,2048]{1,0:T(8,128)(2,1)S(1)} %get-tuple-element.68), channel_id=1, source_target_pairs={{0,1},{1,0},{2,3},{3,2},{4,5},{5,4},{6,7},{7,6},{8,9},{9,8},{10,11... | collective-permute-start | bytes 393224 | tf_op jit(solution)/shard_map/ppermute | solution.py:295

commit v6 on v5

--- a/solution.py
+++ b/solution.py
@@ -25,14 +25,14 @@
     return jnp.where(odd, z, x), jnp.where(odd, x, z), y, odd, q == 3, q == 0
 
 
-def tiles(cols, step):
-    @pl.loop(0, cols // TILE)
+def tiles(cols, step, tile=TILE):
+    @pl.loop(0, cols // tile)
     def _(t):
-        step(pl.ds(pl.multiple_of(t * TILE, TILE), TILE))
-
-
-def transform(b, c, put, copies=None):
-    @pl.loop(0, c.shape[1] // TILE)
+        step(pl.ds(pl.multiple_of(t * tile, tile), tile))
+
+
+def transform(b, c, put, copies=None, tile=TILE):
+    @pl.loop(0, c.shape[1] // tile)
     def _(t):
         for n, copy in enumerate(copies or ()):
 
@@ -40,7 +40,7 @@
             def _(copy=copy):
                 copy.wait()
 
-        cols = pl.ds(pl.multiple_of(t * TILE, TILE), TILE)
+        cols = pl.ds(pl.multiple_of(t * tile, tile), tile)
         put(cols, jnp.dot(b[...], c[:, cols], preferred_element_type=F32).astype(BF16))
 
 
@@ -54,7 +54,7 @@
     return (factor * field.astype(F32)).astype(BF16)
 
 
-def multiply(v, w, product):
+def multiply(v, w, product, tile=TILE):
     def step(cols):
         at = 0
         for part in v:
@@ -63,7 +63,7 @@
             ).astype(BF16)
             at += part.shape[1]
 
-    tiles(w.shape[1], step)
+    tiles(w.shape[1], step, tile)
 
 
 UNIT = 32
@@ -193,8 +193,8 @@
         v_out[:, cols] = values
         w[:, cols] = weighted(wide, values)
 
-    transform(b, c1, put)
-    multiply((va, v0b), w, product)
+    transform(b, c1, put, tile=2 * TILE)
+    multiply((va, v0b), w, product, 2 * TILE)
 
     @pl.when(last)
     def _():

time: 69.5 us -> 69.3 us (level)
  Pallas kernels: 25.6 us -> 24.7 us
  waiting for transfers between devices: 23.7 us -> 24.6 us
    ppermute x14, waiting for transfers between devices: 23.7 us -> 24.6 us  [send(): return lax.ppermute(value, ('sector', 'grid'), pairs_of(move))]
    pallas_call x11, Pallas kernels: 25.6 us -> 24.7 us  [call(): pl.pallas_call(kernel, out_shape=outs, in_specs=[HBM if any((a is h for h...]
  transfers between devices with their start and end apart: 14 -> 14, of which waited for: 11 -> 10; matrix products, arithmetic and copies ran while one was open for 0% -> 0% of each run, Pallas kernels for 30% -> 28%
where the time goes in v6:
time: 69.3 us; the launch traced here: 68.4 us
  Pallas kernels  24.7 us (36%)
  waiting for transfers between devices  24.6 us (35%)
  starting transfers between devices  19 us (27%)
    pallas_call x11, Pallas kernels, call(): pl.pallas_call(kernel, out_shape=outs, in_specs=[HBM if any((a is h for h...  24.7 us
    ppermute x14, waiting for transfers between devices, send(): return lax.ppermute(value, ('sector', 'grid'), pairs_of(move))  24.6 us
    ppermute x14, starting transfers between devices, send(): return lax.ppermute(value, ('sector', 'grid'), pairs_of(move))  19 us
  transfers between devices with their start and end apart: 14, of which 10 were waited for; matrix products, arithmetic and copies ran while one was open for 0% of the time, Pallas kernels for 28%

profile of v6, /device:TPU:30, one launch (start us, length us, event | category | flops | bytes accessed | tf_op | source)
XLA Modules:
  0.0 68.4 jit_solution(844645682633511242)
XLA Ops:
  0.0 4.3 %first_values_a.1 = (bf16[1024,256]{1,0:T(8,128)(2,1)S(1)}, bf16[1024,3072]{1,0:T(8,128)(2,1)S(1)}, bf16[3072,768]{1,0:T(8,128)(2,1)S(1)}, f32[1024,128]{1,0:T(8,128)S(1)}) custom-call(bf16[1024,3072]{1,0:T(8,128)(2,1)} %b_hbm.1, bf16[2,3072,1024]{2,1,0:T(8,128)(2,1)} %c_hbm.3, bf16[3072,1024]{1,0:T(8,128)(2,1)} %next_hbm.3, f32[8,128]{1,0:T(8,128)} %bitcast.1), custom_call_target="tpu_custom_call" | custom-call | flops 3221225472 | bytes 12582912 | tf_op jit(solution)/shard_map/first_values_a/pallas_call | solution.py:320
  4.3 0.7 %collective-permute-start.5 = (bf16[1024,256]{1,0:T(8,128)(2,1)S(1)}, bf16[1024,256]{1,0:T(8,128)(2,1)S(1)}, u32[]{:S(2)}, u32[]{:S(2)}) collective-permute-start(bf16[1024,256]{1,0:T(8,128)(2,1)S(1)} %get-tuple-element.41.v0a), channel_id=1, source_target_pairs={{0,96},{1,97},{2,98},{3,99},{4,100},{5,101},{6,102},{7,103},{8,104... | collective-permute-start | bytes 1572872 | tf_op jit(solution)/shard_map/ppermute | solution.py:295
  5.0 5.4 %first_values_b.1 = (bf16[1024,768]{1,0:T(8,128)(2,1)S(1)}, bf16[3072,256]{1,0:T(8,128)(2,1)S(1)}, bf16[3072,1024]{1,0:T(8,128)(2,1)S(1)}, bf16[3072,768]{1,0:T(8,128)(2,1)S(1)}) custom-call(bf16[1024,3072]{1,0:T(8,128)(2,1)S(1)} %get-tuple-element.37.b, bf16[3072,768]{1,0:T(8,128)(2,1)S(1)} %get-tuple-element.38._, ...), custom_call_target="tpu_custom_call", output_to_operand_aliasing={{3}: (1, {})} | custom-call | flops 3221225472 | bytes 12582912 | tf_op jit(solution)/shard_map/first_values_b/pallas_call | solution.py:320
  10.5 2.6 %collective-permute-start = (bf16[1024,768]{1,0:T(8,128)(2,1)S(1)}, bf16[1024,768]{1,0:T(8,128)(2,1)S(1)}, u32[]{:S(2)}, u32[]{:S(2)}) collective-permute-start(bf16[1024,768]{1,0:T(8,128)(2,1)S(1)} %get-tuple-element.42.v0b), channel_id=1, source_target_pairs={{32,0},{33,1},{34,2},{35,3},{36,4},{37,5},{38,6},{39,7},{40,8},{41... | collective-permute-start | bytes 4718600 | tf_op jit(solution)/shard_map/ppermute | solution.py:295
  13.1 9.5 %second_values.1 = (bf16[1024,1024]{1,0:T(8,128)(2,1)S(1)}, bf16[1024,1024]{1,0:T(8,128)(2,1)S(1)}, bf16[3072,768]{1,0:T(8,128)(2,1)S(1)}) custom-call(bf16[1024,3072]{1,0:T(8,128)(2,1)S(1)} %get-tuple-element.37.b, bf16[3072,256]{1,0:T(8,128)(2,1)S(1)} %get-tuple-element.39.c_first, bf16[3072,1024]{1,0:T(8,128)(2,1)S(1)} %get-tuple-element.40.c1, ...), custom_call_target="tpu_custom_call" | custom-call | flops 21474836 | bytes 6291456 | tf_op jit(solution)/shard_map/second_values/pallas_call | solution.py:320
  22.5 0.0 collective-permute-done.5.arrived
  22.5 0.9 %second_intersection_a.1 = (bf16[256,1280]{1,0:T(8,128)(2,1)S(1)}, bf16[256,1280]{1,0:T(8,128)(2,1)S(1)}, bf16[256,1280]{1,0:T(8,128)(2,1)S(1)}, bf16[256,1280]{1,0:T(8,128)(2,1)S(1)}) custom-call(bf16[1024,1024]{1,0:T(8,128)(2,1)S(1)} %get-tuple-element.45.v1, bf16[1024,256]{1,0:T(8,128)(2,1)S(1)} %collective-permute-done.5.arrived, ...), custom_call_target="tpu_custom_call" | custom-call | flops 17179869184 | bytes 31457280 | tf_op jit(solution)/shard_map/second_intersection_a/pallas_call | solution.py:320
  23.5 0.6 collective-permute-start.6
  24.1 1.5 %collective-permute-start.7 = (bf16[256,1280]{1,0:T(8,128)(2,1)S(1)}, bf16[256,1280]{1,0:T(8,128)(2,1)S(1)}, u32[]{:S(2)}, u32[]{:S(2)}) collective-permute-start(bf16[256,1280]{1,0:T(8,128)(2,1)S(1)} %get-tuple-element.55), channel_id=1, source_target_pairs={{0,24},{1,25},{2,26},{3,27},{4,28},{5,29},{6,30},{7,31},{8,0},{9,1... | collective-permute-start | bytes 1966088 | tf_op jit(solution)/shard_map/ppermute | solution.py:295
  25.6 5.4 %collective-permute-done.arrived = bf16[1024,768]{1,0:T(8,128)(2,1)S(1)} collective-permute-done((bf16[1024,768]{1,0:T(8,128)(2,1)S(1)}, bf16[1024,768]{1,0:T(8,128)(2,1)S(1)}, u32[]{:S(2)}, u32[]{:S(2)}) %collective-permute-start) | collective-permute-done | bytes 1572896 | tf_op jit(solution)/shard_map/ppermute | solution.py:295
  31.0 2.8 %second_intersection_b.1 = (bf16[256,768]{1,0:T(8,128)(2,1)S(1)}, bf16[256,768]{1,0:T(8,128)(2,1)S(1)}, bf16[256,768]{1,0:T(8,128)(2,1)S(1)}, bf16[256,768]{1,0:T(8,128)(2,1)S(1)}) custom-call(bf16[1024,3072]{1,0:T(8,128)(2,1)S(1)} %get-tuple-element.37.b, bf16[3072,768]{1,0:T(8,128)(2,1)S(1)} %get-tuple-element.44.after, ...), custom_call_target="tpu_custom_call" | custom-call | flops 21474836 | bytes 6291456 | tf_op jit(solution)/shard_map/second_intersection_b/pallas_call | solution.py:320
  33.8 0.5 collective-permute-start.1
  34.4 1.6 %collective-permute-start.2 = (bf16[256,768]{1,0:T(8,128)(2,1)S(1)}, bf16[256,768]{1,0:T(8,128)(2,1)S(1)}, u32[]{:S(2)}, u32[]{:S(2)}) collective-permute-start(bf16[256,768]{1,0:T(8,128)(2,1)S(1)} %get-tuple-element.48), channel_id=1, source_target_pairs={{0,24},{1,25},{2,26},{3,27},{4,28},{5,29},{6,30},{7,31},{8,0},{9,1... | collective-permute-start | bytes 1179656 | tf_op jit(solution)/shard_map/ppermute | solution.py:295
  35.9 0.0 collective-permute-done.6.got_plus.refs_1_
  35.9 0.0 collective-permute-done.7.got_minus.refs_2_
  35.9 0.2 relay.3
  36.1 1.8 %collective-permute-start.8 = (bf16[160,1280]{1,0:T(8,128)(2,1)S(1)}, bf16[160,1280]{1,0:T(8,128)(2,1)S(1)}, u32[]{:S(2)}, u32[]{:S(2)}) collective-permute-start(bf16[160,1280]{1,0:T(8,128)(2,1)S(1)} %get-tuple-element.57), channel_id=1, source_target_pairs={{0,8},{1,9},{2,10},{3,11},{4,12},{5,13},{6,14},{7,15},{8,16},{9,17... | collective-permute-start | bytes 1228808 | tf_op jit(solution)/shard_map/ppermute | solution.py:295
  37.8 0.3 collective-permute-start.9
  38.2 3.5 %collective-permute-done.1.got_plus.refs_1_ = bf16[256,768]{1,0:T(8,128)(2,1)S(1)} collective-permute-done((bf16[256,768]{1,0:T(8,128)(2,1)S(1)}, bf16[256,768]{1,0:T(8,128)(2,1)S(1)}, u32[]{:S(2)}, u32[]{:S(2)}) %collective-permute-start.1) | collective-permute-done | bytes 393248 | tf_op jit(solution)/shard_map/ppermute | solution.py:295
  41.7 1.7 %collective-permute-done.2.got_minus.refs_2_ = bf16[256,768]{1,0:T(8,128)(2,1)S(1)} collective-permute-done((bf16[256,768]{1,0:T(8,128)(2,1)S(1)}, bf16[256,768]{1,0:T(8,128)(2,1)S(1)}, u32[]{:S(2)}, u32[]{:S(2)}) %collective-permute-start.2) | collective-permute-done | bytes 393248 | tf_op jit(solution)/shard_map/ppermute | solution.py:295
  43.3 0.1 relay.2
  43.4 0.4 collective-permute-start.3
  43.8 1.7 %collective-permute-start.4 = (bf16[96,768]{1,0:T(8,128)(2,1)S(1)}, bf16[96,768]{1,0:T(8,128)(2,1)S(1)}, u32[]{:S(2)}, u32[]{:S(2)}) collective-permute-start(bf16[96,768]{1,0:T(8,128)(2,1)S(1)} %get-tuple-element.51), channel_id=1, source_target_pairs={{0,24},{1,25},{2,26},{3,27},{4,28},{5,29},{6,30},{7,31},{8,0},{9,1... | collective-permute-start | bytes 442376 | tf_op jit(solution)/shard_map/ppermute | solution.py:295
  45.5 0.4 collective-permute-done.9.refs_4_
  46.0 0.1 collective-permute-done.8.refs_3_
  46.0 0.4 first_sum_a.1
  46.5 3.7 %collective-permute-done.4.refs_4_ = bf16[96,768]{1,0:T(8,128)(2,1)S(1)} collective-permute-done((bf16[96,768]{1,0:T(8,128)(2,1)S(1)}, bf16[96,768]{1,0:T(8,128)(2,1)S(1)}, u32[]{:S(2)}, u32[]{:S(2)}) %collective-permute-start.4) | collective-permute-done | bytes 147488 | tf_op jit(solution)/shard_map/ppermute | solution.py:295
  50.1 0.0 collective-permute-done.3.refs_3_
  50.1 0.2 first_sum_b.1
  50.4 4.0 %collective-permute-start.10 = (bf16[64,2048]{1,0:T(8,128)(2,1)S(1)}, bf16[64,2048]{1,0:T(8,128)(2,1)S(1)}, u32[]{:S(2)}, u32[]{:S(2)}) collective-permute-start(bf16[64,2048]{1,0:T(8,128)(2,1)S(1)} %get-tuple-element.64), channel_id=1, source_target_pairs={{0,4},{1,5},{2,6},{3,7},{4,0},{5,1},{6,2},{7,3},{8,12},{9,13},{10,... | collective-permute-start | bytes 786440 | tf_op jit(solution)/shard_map/ppermute | solution.py:295
  54.3 1.0 %collective-permute-start.11 = (bf16[64,2048]{1,0:T(8,128)(2,1)S(1)}, bf16[64,2048]{1,0:T(8,128)(2,1)S(1)}, u32[]{:S(2)}, u32[]{:S(2)}) collective-permute-start(bf16[64,2048]{1,0:T(8,128)(2,1)S(1)} %get-tuple-element.65), channel_id=1, source_target_pairs={{0,2},{1,3},{2,4},{3,5},{4,6},{5,7},{6,0},{7,1},{8,10},{9,11},{10,... | collective-permute-start | bytes 786440 | tf_op jit(solution)/shard_map/ppermute | solution.py:295
  55.4 2.2 %collective-permute-start.12 = (bf16[64,2048]{1,0:T(8,128)(2,1)S(1)}, bf16[64,2048]{1,0:T(8,128)(2,1)S(1)}, u32[]{:S(2)}, u32[]{:S(2)}) collective-permute-start(bf16[64,2048]{1,0:T(8,128)(2,1)S(1)} %get-tuple-element.66), channel_id=1, source_target_pairs={{0,6},{1,7},{2,0},{3,1},{4,2},{5,3},{6,4},{7,5},{8,14},{9,15},{10,... | collective-permute-start | bytes 786440 | tf_op jit(solution)/shard_map/ppermute | solution.py:295
  57.6 1.1 %collective-permute-done.10.a = bf16[64,2048]{1,0:T(8,128)(2,1)S(1)} collective-permute-done((bf16[64,2048]{1,0:T(8,128)(2,1)S(1)}, bf16[64,2048]{1,0:T(8,128)(2,1)S(1)}, u32[]{:S(2)}, u32[]{:S(2)}) %collective-permute-start.10) | collective-permute-done | bytes 262176 | tf_op jit(solution)/shard_map/ppermute | solution.py:295
  58.7 3.2 %collective-permute-done.11.b = bf16[64,2048]{1,0:T(8,128)(2,1)S(1)} collective-permute-done((bf16[64,2048]{1,0:T(8,128)(2,1)S(1)}, bf16[64,2048]{1,0:T(8,128)(2,1)S(1)}, u32[]{:S(2)}, u32[]{:S(2)}) %collective-permute-start.11) | collective-permute-done | bytes 262176 | tf_op jit(solution)/shard_map/ppermute | solution.py:295
  61.9 0.6 collective-permute-done.12.c
  62.5 0.1 second_sum.1
  62.6 0.1 collective-permute-start.13
  62.7 5.0 %collective-permute-done.13.got = bf16[32,2048]{1,0:T(8,128)(2,1)S(1)} collective-permute-done((bf16[32,2048]{1,0:T(8,128)(2,1)S(1)}, bf16[32,2048]{1,0:T(8,128)(2,1)S(1)}, u32[]{:S(2)}, u32[]{:S(2)}) %collective-permute-start.13) | collective-permute-done | bytes 131104 | tf_op jit(solution)/shard_map/ppermute | solution.py:295
  67.7 0.7 %last_sum.1 = f32[2,32,1024]{2,1,0:T(8,128)} custom-call(f32[32,2048]{1,0:T(8,128)S(1)} %get-tuple-element.67.kept, bf16[32,2048]{1,0:T(8,128)(2,1)S(1)} %collective-permute-done.13.got), custom_call_target="tpu_custom_call" | custom-call | bytes 6291456 | tf_op jit(solution)/shard_map/last_sum/pallas_call | solution.py:320
Async XLA Ops:
  4.3 18.2 %collective-permute-start.5 = (bf16[1024,256]{1,0:T(8,128)(2,1)S(1)}, bf16[1024,256]{1,0:T(8,128)(2,1)S(1)}, u32[]{:S(2)}, u32[]{:S(2)}) collective-permute-start(bf16[1024,256]{1,0:T(8,128)(2,1)S(1)} %get-tuple-element.41.v0a), channel_id=1, source_target_pairs={{0,96},{1,97},{2,98},{3,99},{4,100},{5,101},{6,102},{7,103},{8,104... | collective-permute-start | bytes 1572872 | tf_op jit(solution)/shard_map/ppermute | solution.py:295
  10.5 20.5 %collective-permute-start = (bf16[1024,768]{1,0:T(8,128)(2,1)S(1)}, bf16[1024,768]{1,0:T(8,128)(2,1)S(1)}, u32[]{:S(2)}, u32[]{:S(2)}) collective-permute-start(bf16[1024,768]{1,0:T(8,128)(2,1)S(1)} %get-tuple-element.42.v0b), channel_id=1, source_target_pairs={{32,0},{33,1},{34,2},{35,3},{36,4},{37,5},{38,6},{39,7},{40,8},{41... | collective-permute-start | bytes 4718600 | tf_op jit(solution)/shard_map/ppermute | solution.py:295
  23.5 12.4 %collective-permute-start.6 = (bf16[256,1280]{1,0:T(8,128)(2,1)S(1)}, bf16[256,1280]{1,0:T(8,128)(2,1)S(1)}, u32[]{:S(2)}, u32[]{:S(2)}) collective-permute-start(bf16[256,1280]{1,0:T(8,128)(2,1)S(1)} %get-tuple-element.54), channel_id=1, source_target_pairs={{0,8},{1,9},{2,10},{3,11},{4,12},{5,13},{6,14},{7,15},{8,16},{9,17... | collective-permute-start | bytes 1966088 | tf_op jit(solution)/shard_map/ppermute | solution.py:295
  24.1 11.8 %collective-permute-start.7 = (bf16[256,1280]{1,0:T(8,128)(2,1)S(1)}, bf16[256,1280]{1,0:T(8,128)(2,1)S(1)}, u32[]{:S(2)}, u32[]{:S(2)}) collective-permute-start(bf16[256,1280]{1,0:T(8,128)(2,1)S(1)} %get-tuple-element.55), channel_id=1, source_target_pairs={{0,24},{1,25},{2,26},{3,27},{4,28},{5,29},{6,30},{7,31},{8,0},{9,1... | collective-permute-start | bytes 1966088 | tf_op jit(solution)/shard_map/ppermute | solution.py:295
  33.8 7.8 %collective-permute-start.1 = (bf16[256,768]{1,0:T(8,128)(2,1)S(1)}, bf16[256,768]{1,0:T(8,128)(2,1)S(1)}, u32[]{:S(2)}, u32[]{:S(2)}) collective-permute-start(bf16[256,768]{1,0:T(8,128)(2,1)S(1)} %get-tuple-element.47), channel_id=1, source_target_pairs={{0,8},{1,9},{2,10},{3,11},{4,12},{5,13},{6,14},{7,15},{8,16},{9,17... | collective-permute-start | bytes 1179656 | tf_op jit(solution)/shard_map/ppermute | solution.py:295
  34.4 9.0 %collective-permute-start.2 = (bf16[256,768]{1,0:T(8,128)(2,1)S(1)}, bf16[256,768]{1,0:T(8,128)(2,1)S(1)}, u32[]{:S(2)}, u32[]{:S(2)}) collective-permute-start(bf16[256,768]{1,0:T(8,128)(2,1)S(1)} %get-tuple-element.48), channel_id=1, source_target_pairs={{0,24},{1,25},{2,26},{3,27},{4,28},{5,29},{6,30},{7,31},{8,0},{9,1... | collective-permute-start | bytes 1179656 | tf_op jit(solution)/shard_map/ppermute | solution.py:295
  36.1 10.0 %collective-permute-start.8 = (bf16[160,1280]{1,0:T(8,128)(2,1)S(1)}, bf16[160,1280]{1,0:T(8,128)(2,1)S(1)}, u32[]{:S(2)}, u32[]{:S(2)}) collective-permute-start(bf16[160,1280]{1,0:T(8,128)(2,1)S(1)} %get-tuple-element.57), channel_id=1, source_target_pairs={{0,8},{1,9},{2,10},{3,11},{4,12},{5,13},{6,14},{7,15},{8,16},{9,17... | collective-permute-start | bytes 1228808 | tf_op jit(solution)/shard_map/ppermute | solution.py:295
  37.8 8.2 %collective-permute-start.9 = (bf16[96,1280]{1,0:T(8,128)(2,1)S(1)}, bf16[96,1280]{1,0:T(8,128)(2,1)S(1)}, u32[]{:S(2)}, u32[]{:S(2)}) collective-permute-start(bf16[96,1280]{1,0:T(8,128)(2,1)S(1)} %get-tuple-element.58), channel_id=1, source_target_pairs={{0,24},{1,25},{2,26},{3,27},{4,28},{5,29},{6,30},{7,31},{8,0},{9,1... | collective-permute-start | bytes 737288 | tf_op jit(solution)/shard_map/ppermute | solution.py:295
  43.4 6.7 %collective-permute-start.3 = (bf16[160,768]{1,0:T(8,128)(2,1)S(1)}, bf16[160,768]{1,0:T(8,128)(2,1)S(1)}, u32[]{:S(2)}, u32[]{:S(2)}) collective-permute-start(bf16[160,768]{1,0:T(8,128)(2,1)S(1)} %get-tuple-element.50), channel_id=1, source_target_pairs={{0,8},{1,9},{2,10},{3,11},{4,12},{5,13},{6,14},{7,15},{8,16},{9,17... | collective-permute-start | bytes 737288 | tf_op jit(solution)/shard_map/ppermute | solution.py:295
  43.8 6.4 %collective-permute-start.4 = (bf16[96,768]{1,0:T(8,128)(2,1)S(1)}, bf16[96,768]{1,0:T(8,128)(2,1)S(1)}, u32[]{:S(2)}, u32[]{:S(2)}) collective-permute-start(bf16[96,768]{1,0:T(8,128)(2,1)S(1)} %get-tuple-element.51), channel_id=1, source_target_pairs={{0,24},{1,25},{2,26},{3,27},{4,28},{5,29},{6,30},{7,31},{8,0},{9,1... | collective-permute-start | bytes 442376 | tf_op jit(solution)/shard_map/ppermute | solution.py:295
  50.4 8.3 %collective-permute-start.10 = (bf16[64,2048]{1,0:T(8,128)(2,1)S(1)}, bf16[64,2048]{1,0:T(8,128)(2,1)S(1)}, u32[]{:S(2)}, u32[]{:S(2)}) collective-permute-start(bf16[64,2048]{1,0:T(8,128)(2,1)S(1)} %get-tuple-element.64), channel_id=1, source_target_pairs={{0,4},{1,5},{2,6},{3,7},{4,0},{5,1},{6,2},{7,3},{8,12},{9,13},{10,... | collective-permute-start | bytes 786440 | tf_op jit(solution)/shard_map/ppermute | solution.py:295
  54.3 7.6 %collective-permute-start.11 = (bf16[64,2048]{1,0:T(8,128)(2,1)S(1)}, bf16[64,2048]{1,0:T(8,128)(2,1)S(1)}, u32[]{:S(2)}, u32[]{:S(2)}) collective-permute-start(bf16[64,2048]{1,0:T(8,128)(2,1)S(1)} %get-tuple-element.65), channel_id=1, source_target_pairs={{0,2},{1,3},{2,4},{3,5},{4,6},{5,7},{6,0},{7,1},{8,10},{9,11},{10,... | collective-permute-start | bytes 786440 | tf_op jit(solution)/shard_map/ppermute | solution.py:295
  55.4 7.2 %collective-permute-start.12 = (bf16[64,2048]{1,0:T(8,128)(2,1)S(1)}, bf16[64,2048]{1,0:T(8,128)(2,1)S(1)}, u32[]{:S(2)}, u32[]{:S(2)}) collective-permute-start(bf16[64,2048]{1,0:T(8,128)(2,1)S(1)} %get-tuple-element.66), channel_id=1, source_target_pairs={{0,6},{1,7},{2,0},{3,1},{4,2},{5,3},{6,4},{7,5},{8,14},{9,15},{10,... | collective-permute-start | bytes 786440 | tf_op jit(solution)/shard_map/ppermute | solution.py:295
  62.6 5.0 %collective-permute-start.13 = (bf16[32,2048]{1,0:T(8,128)(2,1)S(1)}, bf16[32,2048]{1,0:T(8,128)(2,1)S(1)}, u32[]{:S(2)}, u32[]{:S(2)}) collective-permute-start(bf16[32,2048]{1,0:T(8,128)(2,1)S(1)} %get-tuple-element.68), channel_id=1, source_target_pairs={{0,1},{1,0},{2,3},{3,2},{4,5},{5,4},{6,7},{7,6},{8,9},{9,8},{10,11... | collective-permute-start | bytes 393224 | tf_op jit(solution)/shard_map/ppermute | solution.py:295

commit v7 on v6

--- a/solution.py
+++ b/solution.py
@@ -222,13 +222,13 @@
         def put(cols, values):
             w[:, cols] = weighted(wide, values)
 
-        transform(b, after, put)
+        transform(b, after, put, tile=after.shape[1] // 2)
 
     @pl.when(jnp.logical_not(last))
     def _():
         weigh(arrived, wide, w)
 
-    multiply((v1,), w, product)
+    multiply((v1,), w, product, w.shape[1] // 2)
     cut((product,), (out0, out1, out2, out3))
 
 

time: 69.3 us -> 69.5 us (level)
  no operation moved by 1% of the time
where the time goes in v7:
time: 69.5 us; the launch traced here: 68.6 us
  Pallas kernels  24.9 us (36%)
  waiting for transfers between devices  24.6 us (35%)
  starting transfers between devices  19 us (27%)
    pallas_call x11, Pallas kernels, call(): pl.pallas_call(kernel, out_shape=outs, in_specs=[HBM if any((a is h for h...  24.9 us
    ppermute x14, waiting for transfers between devices, send(): return lax.ppermute(value, ('sector', 'grid'), pairs_of(move))  24.6 us
    ppermute x14, starting transfers between devices, send(): return lax.ppermute(value, ('sector', 'grid'), pairs_of(move))  19 us
  transfers between devices with their start and end apart: 14, of which 10 were waited for; matrix products, arithmetic and copies ran while one was open for 0% of the time, Pallas kernels for 28%

profile of v7, /device:TPU:30, one launch (start us, length us, event | category | flops | bytes accessed | tf_op | source)
XLA Modules:
  0.0 68.6 jit_solution(6901684585306224288)
XLA Ops:
  0.0 4.3 %first_values_a.1 = (bf16[1024,256]{1,0:T(8,128)(2,1)S(1)}, bf16[1024,3072]{1,0:T(8,128)(2,1)S(1)}, bf16[3072,768]{1,0:T(8,128)(2,1)S(1)}, f32[1024,128]{1,0:T(8,128)S(1)}) custom-call(bf16[1024,3072]{1,0:T(8,128)(2,1)} %b_hbm.1, bf16[2,3072,1024]{2,1,0:T(8,128)(2,1)} %c_hbm.3, bf16[3072,1024]{1,0:T(8,128)(2,1)} %next_hbm.3, f32[8,128]{1,0:T(8,128)} %bitcast.1), custom_call_target="tpu_custom_call" | custom-call | flops 3221225472 | bytes 12582912 | tf_op jit(solution)/shard_map/first_values_a/pallas_call | solution.py:320
  4.3 0.7 %collective-permute-start.5 = (bf16[1024,256]{1,0:T(8,128)(2,1)S(1)}, bf16[1024,256]{1,0:T(8,128)(2,1)S(1)}, u32[]{:S(2)}, u32[]{:S(2)}) collective-permute-start(bf16[1024,256]{1,0:T(8,128)(2,1)S(1)} %get-tuple-element.41.v0a), channel_id=1, source_target_pairs={{0,96},{1,97},{2,98},{3,99},{4,100},{5,101},{6,102},{7,103},{8,104... | collective-permute-start | bytes 1572872 | tf_op jit(solution)/shard_map/ppermute | solution.py:295
  5.0 5.4 %first_values_b.1 = (bf16[1024,768]{1,0:T(8,128)(2,1)S(1)}, bf16[3072,256]{1,0:T(8,128)(2,1)S(1)}, bf16[3072,1024]{1,0:T(8,128)(2,1)S(1)}, bf16[3072,768]{1,0:T(8,128)(2,1)S(1)}) custom-call(bf16[1024,3072]{1,0:T(8,128)(2,1)S(1)} %get-tuple-element.37.b, bf16[3072,768]{1,0:T(8,128)(2,1)S(1)} %get-tuple-element.38._, ...), custom_call_target="tpu_custom_call", output_to_operand_aliasing={{3}: (1, {})} | custom-call | flops 3221225472 | bytes 12582912 | tf_op jit(solution)/shard_map/first_values_b/pallas_call | solution.py:320
  10.5 2.6 %collective-permute-start = (bf16[1024,768]{1,0:T(8,128)(2,1)S(1)}, bf16[1024,768]{1,0:T(8,128)(2,1)S(1)}, u32[]{:S(2)}, u32[]{:S(2)}) collective-permute-start(bf16[1024,768]{1,0:T(8,128)(2,1)S(1)} %get-tuple-element.42.v0b), channel_id=1, source_target_pairs={{32,0},{33,1},{34,2},{35,3},{36,4},{37,5},{38,6},{39,7},{40,8},{41... | collective-permute-start | bytes 4718600 | tf_op jit(solution)/shard_map/ppermute | solution.py:295
  13.1 9.5 %second_values.1 = (bf16[1024,1024]{1,0:T(8,128)(2,1)S(1)}, bf16[1024,1024]{1,0:T(8,128)(2,1)S(1)}, bf16[3072,768]{1,0:T(8,128)(2,1)S(1)}) custom-call(bf16[1024,3072]{1,0:T(8,128)(2,1)S(1)} %get-tuple-element.37.b, bf16[3072,256]{1,0:T(8,128)(2,1)S(1)} %get-tuple-element.39.c_first, bf16[3072,1024]{1,0:T(8,128)(2,1)S(1)} %get-tuple-element.40.c1, ...), custom_call_target="tpu_custom_call" | custom-call | flops 21474836 | bytes 6291456 | tf_op jit(solution)/shard_map/second_values/pallas_call | solution.py:320
  22.5 0.0 collective-permute-done.5.arrived
  22.5 0.9 %second_intersection_a.1 = (bf16[256,1280]{1,0:T(8,128)(2,1)S(1)}, bf16[256,1280]{1,0:T(8,128)(2,1)S(1)}, bf16[256,1280]{1,0:T(8,128)(2,1)S(1)}, bf16[256,1280]{1,0:T(8,128)(2,1)S(1)}) custom-call(bf16[1024,1024]{1,0:T(8,128)(2,1)S(1)} %get-tuple-element.45.v1, bf16[1024,256]{1,0:T(8,128)(2,1)S(1)} %collective-permute-done.5.arrived, ...), custom_call_target="tpu_custom_call" | custom-call | flops 17179869184 | bytes 31457280 | tf_op jit(solution)/shard_map/second_intersection_a/pallas_call | solution.py:320
  23.5 0.6 collective-permute-start.6
  24.1 1.5 %collective-permute-start.7 = (bf16[256,1280]{1,0:T(8,128)(2,1)S(1)}, bf16[256,1280]{1,0:T(8,128)(2,1)S(1)}, u32[]{:S(2)}, u32[]{:S(2)}) collective-permute-start(bf16[256,1280]{1,0:T(8,128)(2,1)S(1)} %get-tuple-element.55), channel_id=1, source_target_pairs={{0,24},{1,25},{2,26},{3,27},{4,28},{5,29},{6,30},{7,31},{8,0},{9,1... | collective-permute-start | bytes 1966088 | tf_op jit(solution)/shard_map/ppermute | solution.py:295
  25.6 5.4 %collective-permute-done.arrived = bf16[1024,768]{1,0:T(8,128)(2,1)S(1)} collective-permute-done((bf16[1024,768]{1,0:T(8,128)(2,1)S(1)}, bf16[1024,768]{1,0:T(8,128)(2,1)S(1)}, u32[]{:S(2)}, u32[]{:S(2)}) %collective-permute-start) | collective-permute-done | bytes 1572896 | tf_op jit(solution)/shard_map/ppermute | solution.py:295
  31.0 3.0 %second_intersection_b.1 = (bf16[256,768]{1,0:T(8,128)(2,1)S(1)}, bf16[256,768]{1,0:T(8,128)(2,1)S(1)}, bf16[256,768]{1,0:T(8,128)(2,1)S(1)}, bf16[256,768]{1,0:T(8,128)(2,1)S(1)}) custom-call(bf16[1024,3072]{1,0:T(8,128)(2,1)S(1)} %get-tuple-element.37.b, bf16[3072,768]{1,0:T(8,128)(2,1)S(1)} %get-tuple-element.44.after, ...), custom_call_target="tpu_custom_call" | custom-call | flops 21474836 | bytes 6291456 | tf_op jit(solution)/shard_map/second_intersection_b/pallas_call | solution.py:320
  34.0 0.5 collective-permute-start.1
  34.5 1.5 %collective-permute-start.2 = (bf16[256,768]{1,0:T(8,128)(2,1)S(1)}, bf16[256,768]{1,0:T(8,128)(2,1)S(1)}, u32[]{:S(2)}, u32[]{:S(2)}) collective-permute-start(bf16[256,768]{1,0:T(8,128)(2,1)S(1)} %get-tuple-element.48), channel_id=1, source_target_pairs={{0,24},{1,25},{2,26},{3,27},{4,28},{5,29},{6,30},{7,31},{8,0},{9,1... | collective-permute-start | bytes 1179656 | tf_op jit(solution)/shard_map/ppermute | solution.py:295
  36.1 0.0 collective-permute-done.6.got_plus.refs_1_
  36.1 0.0 collective-permute-done.7.got_minus.refs_2_
  36.1 0.2 relay.3
  36.2 1.8 %collective-permute-start.8 = (bf16[160,1280]{1,0:T(8,128)(2,1)S(1)}, bf16[160,1280]{1,0:T(8,128)(2,1)S(1)}, u32[]{:S(2)}, u32[]{:S(2)}) collective-permute-start(bf16[160,1280]{1,0:T(8,128)(2,1)S(1)} %get-tuple-element.57), channel_id=1, source_target_pairs={{0,8},{1,9},{2,10},{3,11},{4,12},{5,13},{6,14},{7,15},{8,16},{9,17... | collective-permute-start | bytes 1228808 | tf_op jit(solution)/shard_map/ppermute | solution.py:295
  38.0 0.3 collective-permute-start.9
  38.3 3.5 %collective-permute-done.1.got_plus.refs_1_ = bf16[256,768]{1,0:T(8,128)(2,1)S(1)} collective-permute-done((bf16[256,768]{1,0:T(8,128)(2,1)S(1)}, bf16[256,768]{1,0:T(8,128)(2,1)S(1)}, u32[]{:S(2)}, u32[]{:S(2)}) %collective-permute-start.1) | collective-permute-done | bytes 393248 | tf_op jit(solution)/shard_map/ppermute | solution.py:295
  41.8 1.7 %collective-permute-done.2.got_minus.refs_2_ = bf16[256,768]{1,0:T(8,128)(2,1)S(1)} collective-permute-done((bf16[256,768]{1,0:T(8,128)(2,1)S(1)}, bf16[256,768]{1,0:T(8,128)(2,1)S(1)}, u32[]{:S(2)}, u32[]{:S(2)}) %collective-permute-start.2) | collective-permute-done | bytes 393248 | tf_op jit(solution)/shard_map/ppermute | solution.py:295
  43.5 0.1 relay.2
  43.6 0.3 collective-permute-start.3
  44.0 1.7 %collective-permute-start.4 = (bf16[96,768]{1,0:T(8,128)(2,1)S(1)}, bf16[96,768]{1,0:T(8,128)(2,1)S(1)}, u32[]{:S(2)}, u32[]{:S(2)}) collective-permute-start(bf16[96,768]{1,0:T(8,128)(2,1)S(1)} %get-tuple-element.51), channel_id=1, source_target_pairs={{0,24},{1,25},{2,26},{3,27},{4,28},{5,29},{6,30},{7,31},{8,0},{9,1... | collective-permute-start | bytes 442376 | tf_op jit(solution)/shard_map/ppermute | solution.py:295
  45.7 0.4 collective-permute-done.9.refs_4_
  46.2 0.1 collective-permute-done.8.refs_3_
  46.2 0.4 first_sum_a.1
  46.7 3.7 %collective-permute-done.4.refs_4_ = bf16[96,768]{1,0:T(8,128)(2,1)S(1)} collective-permute-done((bf16[96,768]{1,0:T(8,128)(2,1)S(1)}, bf16[96,768]{1,0:T(8,128)(2,1)S(1)}, u32[]{:S(2)}, u32[]{:S(2)}) %collective-permute-start.4) | collective-permute-done | bytes 147488 | tf_op jit(solution)/shard_map/ppermute | solution.py:295
  50.3 0.0 collective-permute-done.3.refs_3_
  50.3 0.2 first_sum_b.1
  50.6 4.0 %collective-permute-start.10 = (bf16[64,2048]{1,0:T(8,128)(2,1)S(1)}, bf16[64,2048]{1,0:T(8,128)(2,1)S(1)}, u32[]{:S(2)}, u32[]{:S(2)}) collective-permute-start(bf16[64,2048]{1,0:T(8,128)(2,1)S(1)} %get-tuple-element.64), channel_id=1, source_target_pairs={{0,4},{1,5},{2,6},{3,7},{4,0},{5,1},{6,2},{7,3},{8,12},{9,13},{10,... | collective-permute-start | bytes 786440 | tf_op jit(solution)/shard_map/ppermute | solution.py:295
  54.5 1.0 %collective-permute-start.11 = (bf16[64,2048]{1,0:T(8,128)(2,1)S(1)}, bf16[64,2048]{1,0:T(8,128)(2,1)S(1)}, u32[]{:S(2)}, u32[]{:S(2)}) collective-permute-start(bf16[64,2048]{1,0:T(8,128)(2,1)S(1)} %get-tuple-element.65), channel_id=1, source_target_pairs={{0,2},{1,3},{2,4},{3,5},{4,6},{5,7},{6,0},{7,1},{8,10},{9,11},{10,... | collective-permute-start | bytes 786440 | tf_op jit(solution)/shard_map/ppermute | solution.py:295
  55.5 2.2 %collective-permute-start.12 = (bf16[64,2048]{1,0:T(8,128)(2,1)S(1)}, bf16[64,2048]{1,0:T(8,128)(2,1)S(1)}, u32[]{:S(2)}, u32[]{:S(2)}) collective-permute-start(bf16[64,2048]{1,0:T(8,128)(2,1)S(1)} %get-tuple-element.66), channel_id=1, source_target_pairs={{0,6},{1,7},{2,0},{3,1},{4,2},{5,3},{6,4},{7,5},{8,14},{9,15},{10,... | collective-permute-start | bytes 786440 | tf_op jit(solution)/shard_map/ppermute | solution.py:295
  57.8 1.1 %collective-permute-done.10.a = bf16[64,2048]{1,0:T(8,128)(2,1)S(1)} collective-permute-done((bf16[64,2048]{1,0:T(8,128)(2,1)S(1)}, bf16[64,2048]{1,0:T(8,128)(2,1)S(1)}, u32[]{:S(2)}, u32[]{:S(2)}) %collective-permute-start.10) | collective-permute-done | bytes 262176 | tf_op jit(solution)/shard_map/ppermute | solution.py:295
  58.9 3.2 %collective-permute-done.11.b = bf16[64,2048]{1,0:T(8,128)(2,1)S(1)} collective-permute-done((bf16[64,2048]{1,0:T(8,128)(2,1)S(1)}, bf16[64,2048]{1,0:T(8,128)(2,1)S(1)}, u32[]{:S(2)}, u32[]{:S(2)}) %collective-permute-start.11) | collective-permute-done | bytes 262176 | tf_op jit(solution)/shard_map/ppermute | solution.py:295
  62.1 0.6 collective-permute-done.12.c
  62.7 0.1 second_sum.1
  62.8 0.1 collective-permute-start.13
  62.9 5.0 %collective-permute-done.13.got = bf16[32,2048]{1,0:T(8,128)(2,1)S(1)} collective-permute-done((bf16[32,2048]{1,0:T(8,128)(2,1)S(1)}, bf16[32,2048]{1,0:T(8,128)(2,1)S(1)}, u32[]{:S(2)}, u32[]{:S(2)}) %collective-permute-start.13) | collective-permute-done | bytes 131104 | tf_op jit(solution)/shard_map/ppermute | solution.py:295
  67.9 0.7 %last_sum.1 = f32[2,32,1024]{2,1,0:T(8,128)} custom-call(f32[32,2048]{1,0:T(8,128)S(1)} %get-tuple-element.67.kept, bf16[32,2048]{1,0:T(8,128)(2,1)S(1)} %collective-permute-done.13.got), custom_call_target="tpu_custom_call" | custom-call | bytes 6291456 | tf_op jit(solution)/shard_map/last_sum/pallas_call | solution.py:320
Async XLA Ops:
  4.3 18.2 %collective-permute-start.5 = (bf16[1024,256]{1,0:T(8,128)(2,1)S(1)}, bf16[1024,256]{1,0:T(8,128)(2,1)S(1)}, u32[]{:S(2)}, u32[]{:S(2)}) collective-permute-start(bf16[1024,256]{1,0:T(8,128)(2,1)S(1)} %get-tuple-element.41.v0a), channel_id=1, source_target_pairs={{0,96},{1,97},{2,98},{3,99},{4,100},{5,101},{6,102},{7,103},{8,104... | collective-permute-start | bytes 1572872 | tf_op jit(solution)/shard_map/ppermute | solution.py:295
  10.5 20.5 %collective-permute-start = (bf16[1024,768]{1,0:T(8,128)(2,1)S(1)}, bf16[1024,768]{1,0:T(8,128)(2,1)S(1)}, u32[]{:S(2)}, u32[]{:S(2)}) collective-permute-start(bf16[1024,768]{1,0:T(8,128)(2,1)S(1)} %get-tuple-element.42.v0b), channel_id=1, source_target_pairs={{32,0},{33,1},{34,2},{35,3},{36,4},{37,5},{38,6},{39,7},{40,8},{41... | collective-permute-start | bytes 4718600 | tf_op jit(solution)/shard_map/ppermute | solution.py:295
  23.5 12.6 %collective-permute-start.6 = (bf16[256,1280]{1,0:T(8,128)(2,1)S(1)}, bf16[256,1280]{1,0:T(8,128)(2,1)S(1)}, u32[]{:S(2)}, u32[]{:S(2)}) collective-permute-start(bf16[256,1280]{1,0:T(8,128)(2,1)S(1)} %get-tuple-element.54), channel_id=1, source_target_pairs={{0,8},{1,9},{2,10},{3,11},{4,12},{5,13},{6,14},{7,15},{8,16},{9,17... | collective-permute-start | bytes 1966088 | tf_op jit(solution)/shard_map/ppermute | solution.py:295
  24.1 12.0 %collective-permute-start.7 = (bf16[256,1280]{1,0:T(8,128)(2,1)S(1)}, bf16[256,1280]{1,0:T(8,128)(2,1)S(1)}, u32[]{:S(2)}, u32[]{:S(2)}) collective-permute-start(bf16[256,1280]{1,0:T(8,128)(2,1)S(1)} %get-tuple-element.55), channel_id=1, source_target_pairs={{0,24},{1,25},{2,26},{3,27},{4,28},{5,29},{6,30},{7,31},{8,0},{9,1... | collective-permute-start | bytes 1966088 | tf_op jit(solution)/shard_map/ppermute | solution.py:295
  34.0 7.8 %collective-permute-start.1 = (bf16[256,768]{1,0:T(8,128)(2,1)S(1)}, bf16[256,768]{1,0:T(8,128)(2,1)S(1)}, u32[]{:S(2)}, u32[]{:S(2)}) collective-permute-start(bf16[256,768]{1,0:T(8,128)(2,1)S(1)} %get-tuple-element.47), channel_id=1, source_target_pairs={{0,8},{1,9},{2,10},{3,11},{4,12},{5,13},{6,14},{7,15},{8,16},{9,17... | collective-permute-start | bytes 1179656 | tf_op jit(solution)/shard_map/ppermute | solution.py:295
  34.5 9.0 %collective-permute-start.2 = (bf16[256,768]{1,0:T(8,128)(2,1)S(1)}, bf16[256,768]{1,0:T(8,128)(2,1)S(1)}, u32[]{:S(2)}, u32[]{:S(2)}) collective-permute-start(bf16[256,768]{1,0:T(8,128)(2,1)S(1)} %get-tuple-element.48), channel_id=1, source_target_pairs={{0,24},{1,25},{2,26},{3,27},{4,28},{5,29},{6,30},{7,31},{8,0},{9,1... | collective-permute-start | bytes 1179656 | tf_op jit(solution)/shard_map/ppermute | solution.py:295
  36.2 10.0 %collective-permute-start.8 = (bf16[160,1280]{1,0:T(8,128)(2,1)S(1)}, bf16[160,1280]{1,0:T(8,128)(2,1)S(1)}, u32[]{:S(2)}, u32[]{:S(2)}) collective-permute-start(bf16[160,1280]{1,0:T(8,128)(2,1)S(1)} %get-tuple-element.57), channel_id=1, source_target_pairs={{0,8},{1,9},{2,10},{3,11},{4,12},{5,13},{6,14},{7,15},{8,16},{9,17... | collective-permute-start | bytes 1228808 | tf_op jit(solution)/shard_map/ppermute | solution.py:295
  38.0 8.2 %collective-permute-start.9 = (bf16[96,1280]{1,0:T(8,128)(2,1)S(1)}, bf16[96,1280]{1,0:T(8,128)(2,1)S(1)}, u32[]{:S(2)}, u32[]{:S(2)}) collective-permute-start(bf16[96,1280]{1,0:T(8,128)(2,1)S(1)} %get-tuple-element.58), channel_id=1, source_target_pairs={{0,24},{1,25},{2,26},{3,27},{4,28},{5,29},{6,30},{7,31},{8,0},{9,1... | collective-permute-start | bytes 737288 | tf_op jit(solution)/shard_map/ppermute | solution.py:295
  43.6 6.7 %collective-permute-start.3 = (bf16[160,768]{1,0:T(8,128)(2,1)S(1)}, bf16[160,768]{1,0:T(8,128)(2,1)S(1)}, u32[]{:S(2)}, u32[]{:S(2)}) collective-permute-start(bf16[160,768]{1,0:T(8,128)(2,1)S(1)} %get-tuple-element.50), channel_id=1, source_target_pairs={{0,8},{1,9},{2,10},{3,11},{4,12},{5,13},{6,14},{7,15},{8,16},{9,17... | collective-permute-start | bytes 737288 | tf_op jit(solution)/shard_map/ppermute | solution.py:295
  44.0 6.4 %collective-permute-start.4 = (bf16[96,768]{1,0:T(8,128)(2,1)S(1)}, bf16[96,768]{1,0:T(8,128)(2,1)S(1)}, u32[]{:S(2)}, u32[]{:S(2)}) collective-permute-start(bf16[96,768]{1,0:T(8,128)(2,1)S(1)} %get-tuple-element.51), channel_id=1, source_target_pairs={{0,24},{1,25},{2,26},{3,27},{4,28},{5,29},{6,30},{7,31},{8,0},{9,1... | collective-permute-start | bytes 442376 | tf_op jit(solution)/shard_map/ppermute | solution.py:295
  50.6 8.3 %collective-permute-start.10 = (bf16[64,2048]{1,0:T(8,128)(2,1)S(1)}, bf16[64,2048]{1,0:T(8,128)(2,1)S(1)}, u32[]{:S(2)}, u32[]{:S(2)}) collective-permute-start(bf16[64,2048]{1,0:T(8,128)(2,1)S(1)} %get-tuple-element.64), channel_id=1, source_target_pairs={{0,4},{1,5},{2,6},{3,7},{4,0},{5,1},{6,2},{7,3},{8,12},{9,13},{10,... | collective-permute-start | bytes 786440 | tf_op jit(solution)/shard_map/ppermute | solution.py:295
  54.5 7.6 %collective-permute-start.11 = (bf16[64,2048]{1,0:T(8,128)(2,1)S(1)}, bf16[64,2048]{1,0:T(8,128)(2,1)S(1)}, u32[]{:S(2)}, u32[]{:S(2)}) collective-permute-start(bf16[64,2048]{1,0:T(8,128)(2,1)S(1)} %get-tuple-element.65), channel_id=1, source_target_pairs={{0,2},{1,3},{2,4},{3,5},{4,6},{5,7},{6,0},{7,1},{8,10},{9,11},{10,... | collective-permute-start | bytes 786440 | tf_op jit(solution)/shard_map/ppermute | solution.py:295
  55.5 7.2 %collective-permute-start.12 = (bf16[64,2048]{1,0:T(8,128)(2,1)S(1)}, bf16[64,2048]{1,0:T(8,128)(2,1)S(1)}, u32[]{:S(2)}, u32[]{:S(2)}) collective-permute-start(bf16[64,2048]{1,0:T(8,128)(2,1)S(1)} %get-tuple-element.66), channel_id=1, source_target_pairs={{0,6},{1,7},{2,0},{3,1},{4,2},{5,3},{6,4},{7,5},{8,14},{9,15},{10,... | collective-permute-start | bytes 786440 | tf_op jit(solution)/shard_map/ppermute | solution.py:295
  62.8 5.0 %collective-permute-start.13 = (bf16[32,2048]{1,0:T(8,128)(2,1)S(1)}, bf16[32,2048]{1,0:T(8,128)(2,1)S(1)}, u32[]{:S(2)}, u32[]{:S(2)}) collective-permute-start(bf16[32,2048]{1,0:T(8,128)(2,1)S(1)} %get-tuple-element.68), channel_id=1, source_target_pairs={{0,1},{1,0},{2,3},{3,2},{4,5},{5,4},{6,7},{7,6},{8,9},{9,8},{10,11... | collective-permute-start | bytes 393224 | tf_op jit(solution)/shard_map/ppermute | solution.py:295
